TPU v7x, 128 devices: a whole 4x4x4 slice. The times are simulated.
128 devices in a mesh: group: 8 (over y_hi, x), row: 16 (over z, y_lo, core).
Axes of the slice: x: 4, y: 4 (y_hi: 2, y_lo: 2; y = y_hi * 2 + y_lo), z: 4, core: 2. Of those that a mesh axis runs over, the one named last changes fastest.
Arguments:
- embeds: bfloat16 [65536, 768], P(('group', 'row')), may hold values from -120 to 120
- member: int32 [65536], P(('group', 'row')), may hold values from 0 to 7, as said below
Outputs:
- nearest: float32 [65536], P(('group', 'row'))
Inputs may be any that keep to these rules, and one draw needn't show every extreme that they name: `member`: rows come in aligned blocks of 512; no cluster takes more than 128 rows of one block. For each remainder of the block index modulo the row axis's size, one cluster takes exactly 128 rows of every block with that remainder.
All inputs are finite; a program needn't handle non-finite values.
Results may differ from a plain program's by a relative error of at most 0.00056.
Values may be sent and summed in bfloat16 or wider, within the bound.
No kernel may reach another device: no remote copies, remote signals or barrier semaphores. Data moves between devices by JAX's collectives and lax.ppermute only.
A program may use at most 128 MiB of HBM per device.

v0:
```python
import functools

import jax
import jax.numpy as jnp
import numpy as np
from jax import lax
from jax.experimental import pallas as pl
from jax.experimental.pallas import tpu as pltpu
from jax.sharding import PartitionSpec as P

D = 768
RB = 512
GROUPS = 8
META = 16
SENT = RB + META
UNROLL = 4
HALF = 256
BAND = 384
ABSENT = -4.0
LOW = -1e30
AXES = ("group", "row")

UNIT = ((1, 0, 0), (0, 1, 0), (0, 0, 1), (3, 0, 0), (0, 3, 0), (0, 0, 3))
PARENT = (None,) + (0, 0, 0, 2, 1, 3, 6, 4, 4, 5, 5, 7)
DIRS = (
    (None,) + (5, 0, 2, 1, 3, 4, 0, 5, 1, 5, 2, 0),
    (None,) + (4, 3, 1, 2, 0, 5, 3, 4, 2, 4, 1, 3),
)
SLOTS = len(PARENT)
OTHER = 20
MEETINGS = (
    ((0, (0, 20)), (1, (0, 20, 21)), (2, (0, 1, 20, 21)), (3, (1, 2, 20, 21))),
    (
        (4, (0, 1, 2, 3, 21, 22)),
        (5, (2, 3, 4, 20, 21, 23, 24, 25)),
        (6, (0, 1, 4, 5, 20, 22, 23, 25, 26)),
    ),
    (
        (7, (0, 3, 4, 5, 21, 22, 23, 24, 26, 27)),
        (8, (3, 5, 6, 7, 20, 21, 24, 25, 27)),
        (9, (0, 1, 2, 5, 6, 8, 22, 26, 27)),
    ),
    ((10, (2, 9, 20, 21, 23)), (11, (2, 8, 9, 20, 26)), (12, (23, 27))),
)


def members(meeting):
    rows = tuple(k for k, partners in meeting)
    rest = sorted({k for row, partners in meeting for k in partners} - set(rows))
    return rows, rows + tuple(rest)


NAMES = tuple(sorted({k for meeting in MEETINGS for k in members(meeting)[1]}))


def offsets():
    table = []
    for core in range(2):
        held = [(0, 0, 0)]
        for i in range(1, SLOTS):
            step, base = UNIT[DIRS[core][i]], held[PARENT[i]]
            held.append(tuple((a + b) % 4 for a, b in zip(step, base)))
        table.append(held)
    return table


def place(x, y, z, core):
    group = (y // 2) * 4 + x
    row = (z * 2 + y % 2) * 2 + core
    return group * 16 + row


def fetch(block, steps):
    pairs = []
    for x in range(4):
        for y in range(4):
            for z in range(4):
                for core in range(2):
                    dx, dy, dz = steps[core]
                    source = place((x + dx) % 4, (y + dy) % 4, (z + dz) % 4, core)
                    pairs.append((source, place(x, y, z, core)))
    return lax.ppermute(block, AXES, sorted(pairs))


def flip(block):
    return lax.ppermute(block, AXES, [(i, i ^ 1) for i in range(128)])


def home(name, group, row):
    x, y, z = lax.rem(group, 4), lax.div(group, 4) * 2 + lax.rem(lax.div(row, 2), 2), lax.div(row, 4)
    core = lax.rem(row, 2)
    table = offsets()
    swap = 1 if name >= OTHER else 0
    at = []
    for axis, here in enumerate((x, y, z)):
        first = table[swap][name % OTHER][axis]
        second = table[1 - swap][name % OTHER][axis]
        at.append(lax.rem(here + jnp.where(core == 0, first, second), 4))
    core = 1 - core if swap else core
    group = lax.div(at[1], 2) * 4 + at[0]
    return group * 16 + (at[2] * 2 + lax.rem(at[1], 2)) * 2 + core


def prepare_kernel(embeds_ref, member_ref, block_ref, target_ref):
    member = member_ref[...].astype(jnp.float32)
    column = jnp.transpose(jnp.broadcast_to(member, (128, RB)))[:, 0:1]
    above = lax.broadcasted_iota(jnp.int32, (RB, RB), 0)
    across = lax.broadcasted_iota(jnp.int32, (RB, RB), 1)
    before = (column < member) | ((column == member) & (above < across))
    target = jnp.sum(before.astype(jnp.float32), axis=0, keepdims=True).astype(jnp.int32)
    target_ref[...] = target
    values = embeds_ref[...].astype(jnp.float32)
    total = jnp.sum(values * values, axis=1, keepdims=True)
    normed = (values * lax.rsqrt(total + 1e-06)).astype(jnp.bfloat16)
    placer = (above == target).astype(jnp.bfloat16)
    block_ref[0:RB, :] = jnp.dot(placer, normed, preferred_element_type=jnp.float32).astype(
        jnp.bfloat16
    )
    ordered = jnp.sum(jnp.where(above == target, member, 0.0), axis=1, keepdims=True)
    ordered = jnp.transpose(jnp.broadcast_to(ordered, (RB, 128)))[0:META]
    block_ref[RB:SENT, :] = jnp.zeros((META, D), jnp.bfloat16)
    block_ref[RB:SENT, 0:RB] = ordered.astype(jnp.bfloat16)


def prepare(embeds, member):
    return pl.pallas_call(
        prepare_kernel,
        out_shape=(
            jax.ShapeDtypeStruct((SENT, D), jnp.bfloat16),
            jax.ShapeDtypeStruct((1, RB), jnp.int32),
        ),
        name="prepare",
    )(embeds, member.reshape(1, RB))


def meet_kernel(total, rows, pairs, itself, lists, fetched, *refs):
    blocks, refs = refs[:total], refs[total:]
    if lists:
        before, refs = refs[: len(lists) - 1], refs[len(lists) - 1 :]
    out_ref, held, across, down, row_best, column_best, table, waits, sems = refs
    for k in range(total):
        pltpu.make_async_copy(blocks[k], held.at[k], sems.at[k]).start()
    for p, (i, j) in enumerate(pairs):
        table[0, p] = i
        table[1, p] = j
        waits[p] = fetched[p]
    pairs = len(pairs)
    row_best[...] = jnp.full_like(row_best, LOW)
    column_best[...] = jnp.full_like(column_best, LOW)
    if lists:
        out_ref[...] = jnp.full_like(out_ref, ABSENT)

    def arrive(k):
        pltpu.make_async_copy(blocks[0], held.at[k], sems.at[k]).wait()
        across[k] = held[k, RB:SENT, 0:RB].astype(jnp.float32)[0:8]

    for k in range(rows):
        arrive(k)
        down[k] = jnp.transpose(jnp.broadcast_to(across[k, 0:1], (128, RB)))

    def meet(i, j, at, length, column, width, same):
        scores = lax.dot_general(
            held[i, at : at + length, :],
            held[j, column : column + width, :],
            (((1,), (1,)), ((), ())),
            preferred_element_type=jnp.float32,
        )
        here = jnp.concatenate([down[i, at : at + length, :]] * (width // 128), axis=1)
        keep = here == across[j, 0:1, column : column + width]
        if same:
            one = lax.broadcasted_iota(jnp.int32, (length, width), 0)
            keep = keep & (one != lax.broadcasted_iota(jnp.int32, (length, width), 1))
        scores = jnp.where(keep, scores, LOW)
        most = scores[:, 0:128]
        for q in range(1, width // 128):
            most = jnp.maximum(most, scores[:, 128 * q : 128 * q + 128])
        row_best[i, at : at + length, :] = jnp.maximum(row_best[i, at : at + length, :], most)
        top = jnp.max(scores.reshape(length // 8, 8, width), axis=0)
        span = slice(column, column + width)
        column_best[j, :, span] = jnp.maximum(column_best[j, :, span], top)

    def near(i, j):
        meet(i, j, 0, BAND, 0, HALF, False)
        meet(i, j, RB - BAND, BAND, HALF, HALF, False)

    def far(i, j):
        late = across[j, 0:1, HALF - 128 : HALF] >= down[i, BAND : BAND + 1, :]
        early = across[j, 0:1, HALF : HALF + 128] <= down[i, RB - BAND - 1 : RB - BAND, :]
        return jnp.where(late | early, 1.0, 0.0)

    def visit(first, length):
        pairs_here = [(table[0, first + u], table[1, first + u]) for u in range(length)]
        flags = functools.reduce(jnp.maximum, [far(i, j) for i, j in pairs_here])
        flag = jnp.max(flags)
        for i, j in pairs_here:
            near(i, j)

        @pl.when(flag > 0.0)
        def _():
            def rest(p, carry):
                i, j = table[0, p], table[1, p]
                meet(i, j, BAND, RB - BAND, 0, HALF, False)
                meet(i, j, 0, RB - BAND, HALF, HALF, False)
                return carry

            lax.fori_loop(first, first + length, rest, 0)

    if itself:
        meet(0, 0, 0, RB, 0, RB, True)

    def await_step(step, length):
        for u in range(length):
            block = waits[step * UNROLL + u]
            pl.when(block >= 0)(functools.partial(arrive, block))

    def some(step, carry):
        await_step(step, UNROLL)
        visit(step * UNROLL, UNROLL)
        return carry

    steps = pairs // UNROLL
    lax.fori_loop(0, steps, some, 0)
    if pairs > steps * UNROLL:
        await_step(steps, pairs - steps * UNROLL)
        visit(steps * UNROLL, pairs - steps * UNROLL)

    def found_in(k):
        found = jnp.max(column_best[k], axis=0, keepdims=True)
        if k < rows:
            turned = jnp.transpose(row_best[k])
            found = jnp.maximum(found, jnp.max(turned, axis=0, keepdims=True))
        return found

    if not lists:
        for k in range(total):
            out_ref[k : k + 1, :] = found_in(k)
        return
    here = [lax.axis_index(axis) for axis in AXES]
    for name in NAMES:
        found = jnp.full((1, RB), ABSENT, jnp.float32)
        if name in lists[0]:
            found = jnp.maximum(found, found_in(lists[0].index(name)))
        for ref, names in zip(before, lists[1:]):
            if name in names:
                at = names.index(name)
                found = jnp.maximum(found, ref[at : at + 1, :])
        out_ref[home(name, *here)] = found


def meet(held, meeting, lists=(), before=()):
    rows, names = members(meeting)
    pairs = [(i, j) for i, partners in meeting for j in partners]
    itself = (0, 0) in pairs
    pairs = sorted(
        ((names.index(i), names.index(j)) for i, j in pairs if i != j), key=lambda p: p[::-1]
    )
    seen, waits = set(range(len(rows))), []
    for i, j in pairs:
        waits.append(-1 if j in seen else j)
        seen.add(j)
    total = len(names)
    shape = (128, 1, RB) if lists else (total, RB)
    in_specs = [pl.BlockSpec(memory_space=pltpu.HBM)] * total
    if lists:
        in_specs += [pl.BlockSpec(memory_space=pltpu.VMEM)] * len(before)
    return pl.pallas_call(
        functools.partial(meet_kernel, total, len(rows), pairs, itself, lists, waits),
        out_shape=jax.ShapeDtypeStruct(shape, jnp.float32),
        in_specs=in_specs,
        scratch_shapes=[
            pltpu.VMEM((total, SENT, D), jnp.bfloat16),
            pltpu.VMEM((total, 8, RB), jnp.float32),
            pltpu.VMEM((len(rows), RB, 128), jnp.float32),
            pltpu.VMEM((len(rows), RB, 128), jnp.float32),
            pltpu.VMEM((total, 8, RB), jnp.float32),
            pltpu.SMEM((2, len(pairs)), jnp.int32),
            pltpu.SMEM((len(pairs),), jnp.int32),
            pltpu.SemaphoreType.DMA((total,)),
        ],
        compiler_params=pltpu.CompilerParams(vmem_limit_bytes=66_400_000),
        cost_estimate=pl.CostEstimate(
            flops=2 * RB * RB * D * len(pairs),
            bytes_accessed=total * SENT * D * 2,
            transcendentals=0,
        ),
        name=f"meet_{len(pairs)}",
    )(
        *[held[k] for k in names],
        *before,
    )


def finish_kernel(arrived_ref, target_ref, out_ref):
    best = jnp.max(arrived_ref[...], axis=0)
    column = jnp.transpose(jnp.broadcast_to(best, (128, RB)))[:, 0:1]
    above = lax.broadcasted_iota(jnp.int32, (RB, RB), 0)
    picked = jnp.where(above == target_ref[...], column, LOW)
    out_ref[...] = jnp.max(picked, axis=0, keepdims=True)


def finish(arrived, target):
    return pl.pallas_call(
        finish_kernel, out_shape=jax.ShapeDtypeStruct((1, RB), jnp.float32), name="finish"
    )(arrived, target)


def on_device(embeds, member):
    block, target = prepare(embeds, member)
    held = {0: block}
    before = []

    def go(first):
        for i in range(first, first + 3):
            held[i] = fetch(held[PARENT[i]], (UNIT[DIRS[0][i]], UNIT[DIRS[1][i]]))

    def share(slots):
        for i in slots:
            if i + OTHER in NAMES:
                held[i + OTHER] = flip(held[i])

    def after(slots):
        kept = lax.optimization_barrier((before[-1], *[held[i] for i in slots]))
        before[-1] = kept[0]
        held.update(zip(slots, kept[1:]))

    go(1)
    share((0, 1))
    go(4)
    before.append(meet(held, MEETINGS[0]))
    after((2, 3, 4, 5, 6))
    go(7)
    share((2, 3, 4, 5, 6))
    before.append(meet(held, MEETINGS[1]))
    after((7, 8, 9))
    go(10)
    share((7, 8, 9))
    before.append(meet(held, MEETINGS[2]))
    lists = tuple(members(meeting)[1] for meeting in (MEETINGS[-1],) + MEETINGS[:-1])
    outgoing = meet(held, MEETINGS[-1], lists, before)
    arrived = lax.all_to_all(outgoing, AXES, split_axis=0, concat_axis=0, tiled=True)
    return finish(arrived, target).reshape(-1)


def solution(mesh):
    in_specs = (P(AXES, None), P(AXES))
    return jax.shard_map(
        on_device, mesh=mesh, in_specs=in_specs, out_specs=P(AXES), check_vma=False
    )
```

profile of v0, /device:TPU:1, one launch (start us, length us, event | category | flops | bytes accessed | tf_op | source)
XLA Modules:
  0.0 106.5 jit_solution(13464252423348765255)
XLA Ops:
  0.0 3.1 %prepare.1 = (bf16[528,768]{1,0:T(8,128)(2,1)}, s32[1,512]{1,0:T(1,128)}) custom-call(bf16[512,768]{1,0:T(8,128)(2,1)} %embeds_ref.1, s32[1,512]{1,0:T(1,128)} %bitcast.2), custom_call_target="tpu_custom_call" | custom-call | tf_op jit(solution)/shard_map/prepare/pallas_call | solution.py:126
  3.2 2.1 %collective-permute-start = (bf16[528,768]{1,0:T(8,128)(2,1)}, bf16[528,768]{1,0:T(8,128)(2,1)}, u32[]{:S(2)}, u32[]{:S(2)}) collective-permute-start(bf16[528,768]{1,0:T(8,128)(2,1)} %get-tuple-element.17.refs_0_.refs_3_), channel_id=1, source_target_pairs={{0,4},{1,3},{2,6},{3,65},{4,8},{5,7},{6,10},{7,69},{8,12},{9,11},{... | collective-permute-start | bytes 2433032 | tf_op jit(solution)/shard_map/ppermute | solution.py:82
  5.3 1.2 %collective-permute-start.1 = (bf16[528,768]{1,0:T(8,128)(2,1)}, bf16[528,768]{1,0:T(8,128)(2,1)}, u32[]{:S(2)}, u32[]{:S(2)}) collective-permute-start(bf16[528,768]{1,0:T(8,128)(2,1)} %get-tuple-element.17.refs_0_.refs_3_), channel_id=1, source_target_pairs={{0,48},{1,17},{2,50},{3,19},{4,52},{5,21},{6,54},{7,23},{8,56},{9,... | collective-permute-start | bytes 2433032 | tf_op jit(solution)/shard_map/ppermute | solution.py:82
  6.5 1.4 %collective-permute-start.2 = (bf16[528,768]{1,0:T(8,128)(2,1)}, bf16[528,768]{1,0:T(8,128)(2,1)}, u32[]{:S(2)}, u32[]{:S(2)}) collective-permute-start(bf16[528,768]{1,0:T(8,128)(2,1)} %get-tuple-element.17.refs_0_.refs_3_), channel_id=1, source_target_pairs={{0,12},{1,67},{2,14},{3,1},{4,0},{5,71},{6,2},{7,5},{8,4},{9,75},{... | collective-permute-start | bytes 2433032 | tf_op jit(solution)/shard_map/ppermute | solution.py:82
  7.9 3.5 %collective-permute-start.3 = (bf16[528,768]{1,0:T(8,128)(2,1)}, bf16[528,768]{1,0:T(8,128)(2,1)}, u32[]{:S(2)}, u32[]{:S(2)}) collective-permute-start(bf16[528,768]{1,0:T(8,128)(2,1)} %get-tuple-element.17.refs_0_.refs_3_), channel_id=1, source_target_pairs={{0,1},{1,0},{2,3},{3,2},{4,5},{5,4},{6,7},{7,6},{8,9},{9,8},{10,11... | collective-permute-start | bytes 2433032 | tf_op jit(solution)/shard_map/ppermute | solution.py:86
  11.5 5.5 %collective-permute-done.refs_1_.refs_4_ = bf16[528,768]{1,0:T(8,128)(2,1)} collective-permute-done((bf16[528,768]{1,0:T(8,128)(2,1)}, bf16[528,768]{1,0:T(8,128)(2,1)}, u32[]{:S(2)}, u32[]{:S(2)}) %collective-permute-start) | collective-permute-done | bytes 811040 | tf_op jit(solution)/shard_map/ppermute | solution.py:82
  17.0 2.3 %collective-permute-start.4 = (bf16[528,768]{1,0:T(8,128)(2,1)}, bf16[528,768]{1,0:T(8,128)(2,1)}, u32[]{:S(2)}, u32[]{:S(2)}) collective-permute-start(bf16[528,768]{1,0:T(8,128)(2,1)} %collective-permute-done.refs_1_.refs_4_), channel_id=1, source_target_pairs={{0,1},{1,0},{2,3},{3,2},{4,5},{5,4},{6,7},{7,6},{8,9},{9,8},{10,11... | collective-permute-start | bytes 2433032 | tf_op jit(solution)/shard_map/ppermute | solution.py:86
  19.2 2.5 %collective-permute-start.6 = (bf16[528,768]{1,0:T(8,128)(2,1)}, bf16[528,768]{1,0:T(8,128)(2,1)}, u32[]{:S(2)}, u32[]{:S(2)}) collective-permute-start(bf16[528,768]{1,0:T(8,128)(2,1)} %collective-permute-done.refs_1_.refs_4_), channel_id=1, source_target_pairs={{0,16},{1,49},{2,18},{3,51},{4,20},{5,53},{6,22},{7,55},{8,24},{9,... | collective-permute-start | bytes 2433032 | tf_op jit(solution)/shard_map/ppermute | solution.py:82
  21.7 0.0 collective-permute-done.1.refs_2_.refs_5_.refs_3_
  21.7 1.7 %collective-permute-start.5 = (bf16[528,768]{1,0:T(8,128)(2,1)}, bf16[528,768]{1,0:T(8,128)(2,1)}, u32[]{:S(2)}, u32[]{:S(2)}) collective-permute-start(bf16[528,768]{1,0:T(8,128)(2,1)} %collective-permute-done.1.refs_2_.refs_5_.refs_3_), channel_id=1, source_target_pairs={{0,66},{1,13},{2,0},{3,15},{4,70},{5,1},{6,4},{7,3},{8,74},{9,5},{... | collective-permute-start | bytes 2433032 | tf_op jit(solution)/shard_map/ppermute | solution.py:82
  23.5 0.0 collective-permute-done.2.refs_3_.refs_6_
  23.5 0.0 collective-permute-start.7
  23.5 0.0 collective-permute-done.3.refs_4_.refs_7_.refs_10_.refs_6_
  23.5 0.0 collective-permute-done.4.refs_5_.refs_8_.refs_11_.refs_7_
  23.5 8.1 %meet_12.2.refs_11_ = f32[6,512]{1,0:T(8,128)} custom-call(bf16[528,768]{1,0:T(8,128)(2,1)} %get-tuple-element.17.refs_0_.refs_3_, bf16[528,768]{1,0:T(8,128)(2,1)} %collective-permute-done.refs_1_.refs_4_, bf16[528,768]{1,0:T(8,128)(2,1)} %collective-permute-done.1.refs_2_.refs_5_.refs_3_, bf16[528,768]{1,0:T(8,128)(2,1)} %collective-permute-done.2.refs_3_.refs_6_, ...), custom_call_target="tpu_custom_call" | custom-call | flops 4831838208 | bytes 4866048 | tf_op jit(solution)/shard_map/meet_12/pallas_call | solution.py:266
  31.6 0.0 collective-permute-done.6.refs_1_.refs_8_
  31.6 1.8 %collective-permute-done.5.refs_0_.refs_7_ = bf16[528,768]{1,0:T(8,128)(2,1)} collective-permute-done((bf16[528,768]{1,0:T(8,128)(2,1)}, bf16[528,768]{1,0:T(8,128)(2,1)}, u32[]{:S(2)}, u32[]{:S(2)}) %collective-permute-start.5) | collective-permute-done | bytes 811040 | tf_op jit(solution)/shard_map/ppermute | solution.py:82
  33.4 3.0 %collective-permute-done.7.refs_2_.refs_9_ = bf16[528,768]{1,0:T(8,128)(2,1)} collective-permute-done((bf16[528,768]{1,0:T(8,128)(2,1)}, bf16[528,768]{1,0:T(8,128)(2,1)}, u32[]{:S(2)}, u32[]{:S(2)}) %collective-permute-start.7) | collective-permute-done | bytes 811040 | tf_op jit(solution)/shard_map/ppermute | solution.py:82
  36.4 1.1 %collective-permute-start.10 = (bf16[528,768]{1,0:T(8,128)(2,1)}, bf16[528,768]{1,0:T(8,128)(2,1)}, u32[]{:S(2)}, u32[]{:S(2)}) collective-permute-start(bf16[528,768]{1,0:T(8,128)(2,1)} %collective-permute-done.1.refs_2_.refs_5_.refs_3_), channel_id=1, source_target_pairs={{0,1},{1,0},{2,3},{3,2},{4,5},{5,4},{6,7},{7,6},{8,9},{9,8},{10,11... | collective-permute-start | bytes 2433032 | tf_op jit(solution)/shard_map/ppermute | solution.py:86
  37.5 0.0 collective-permute-start.11
  37.5 0.5 collective-permute-start.12
  38.0 0.0 collective-permute-start.13
  38.1 0.5 collective-permute-start.14
  38.6 1.3 %collective-permute-done.10.refs_9_.refs_12_ = bf16[528,768]{1,0:T(8,128)(2,1)} collective-permute-done((bf16[528,768]{1,0:T(8,128)(2,1)}, bf16[528,768]{1,0:T(8,128)(2,1)}, u32[]{:S(2)}, u32[]{:S(2)}) %collective-permute-start.10) | collective-permute-done | bytes 811040 | tf_op jit(solution)/shard_map/ppermute | solution.py:86
  39.8 1.2 %collective-permute-start.15 = (bf16[528,768]{1,0:T(8,128)(2,1)}, bf16[528,768]{1,0:T(8,128)(2,1)}, u32[]{:S(2)}, u32[]{:S(2)}) collective-permute-start(bf16[528,768]{1,0:T(8,128)(2,1)} %collective-permute-done.7.refs_2_.refs_9_), channel_id=1, source_target_pairs={{0,48},{1,17},{2,50},{3,19},{4,52},{5,21},{6,54},{7,23},{8,56},{9,... | collective-permute-start | bytes 2433032 | tf_op jit(solution)/shard_map/ppermute | solution.py:82
  41.0 0.0 collective-permute-done.11.refs_10_.refs_13_.refs_8_
  41.0 0.2 collective-permute-start.16
  41.2 0.9 collective-permute-done.12.refs_11_.refs_14_
  42.1 1.7 %collective-permute-start.17 = (bf16[528,768]{1,0:T(8,128)(2,1)}, bf16[528,768]{1,0:T(8,128)(2,1)}, u32[]{:S(2)}, u32[]{:S(2)}) collective-permute-start(bf16[528,768]{1,0:T(8,128)(2,1)} %collective-permute-done.5.refs_0_.refs_7_), channel_id=1, source_target_pairs={{0,66},{1,13},{2,0},{3,15},{4,70},{5,1},{6,4},{7,3},{8,74},{9,5},{... | collective-permute-start | bytes 2433032 | tf_op jit(solution)/shard_map/ppermute | solution.py:82
  43.9 0.0 collective-permute-done.13.refs_12_.refs_15_
  43.9 0.6 collective-permute-done.14.refs_13_.refs_16_.refs_9_
  44.5 11.7 %meet_23.1.refs_12_ = f32[14,512]{1,0:T(8,128)} custom-call(bf16[528,768]{1,0:T(8,128)(2,1)} %collective-permute-done.5.refs_0_.refs_7_, bf16[528,768]{1,0:T(8,128)(2,1)} %collective-permute-done.6.refs_1_.refs_8_, bf16[528,768]{1,0:T(8,128)(2,1)} %collective-permute-done.7.refs_2_.refs_9_, bf16[528,768]{1,0:T(8,128)(2,1)} %get-tuple-element.17.refs_0_.refs_3_, ...), custom_call_target="tpu_custom_call" | custom-call | flops 9261023232 | bytes 11354112 | tf_op jit(solution)/shard_map/meet_23/pallas_call | solution.py:266
  56.1 0.0 collective-permute-done.15.refs_0_
  56.1 0.0 collective-permute-done.16.refs_1_.refs_4_
  56.2 0.0 collective-permute-done.17.refs_2_.refs_5_
  56.2 0.9 collective-permute-start.19
  57.1 1.0 collective-permute-start.8
  58.0 1.7 %collective-permute-start.9 = (bf16[528,768]{1,0:T(8,128)(2,1)}, bf16[528,768]{1,0:T(8,128)(2,1)}, u32[]{:S(2)}, u32[]{:S(2)}) collective-permute-start(bf16[528,768]{1,0:T(8,128)(2,1)} %collective-permute-done.6.refs_1_.refs_8_), channel_id=1, source_target_pairs={{0,12},{1,67},{2,14},{3,1},{4,0},{5,71},{6,2},{7,5},{8,4},{9,75},{... | collective-permute-start | bytes 2433032 | tf_op jit(solution)/shard_map/ppermute | solution.py:82
  59.7 2.2 %collective-permute-start.18 = (bf16[528,768]{1,0:T(8,128)(2,1)}, bf16[528,768]{1,0:T(8,128)(2,1)}, u32[]{:S(2)}, u32[]{:S(2)}) collective-permute-start(bf16[528,768]{1,0:T(8,128)(2,1)} %collective-permute-done.15.refs_0_), channel_id=1, source_target_pairs={{0,48},{1,17},{2,50},{3,19},{4,52},{5,21},{6,54},{7,23},{8,56},{9,... | collective-permute-start | bytes 2433032 | tf_op jit(solution)/shard_map/ppermute | solution.py:82
  62.0 0.0 collective-permute-done.19.refs_17_.refs_10_
  62.0 13.6 %meet_28.1.refs_13_ = f32[18,512]{1,0:T(8,128)} custom-call(bf16[528,768]{1,0:T(8,128)(2,1)} %collective-permute-done.15.refs_0_, bf16[528,768]{1,0:T(8,128)(2,1)} %collective-permute-done.16.refs_1_.refs_4_, bf16[528,768]{1,0:T(8,128)(2,1)} %collective-permute-done.17.refs_2_.refs_5_, bf16[528,768]{1,0:T(8,128)(2,1)} %get-tuple-element.17.refs_0_.refs_3_, ...), custom_call_target="tpu_custom_call" | custom-call | flops 11274289152 | bytes 14598144 | tf_op jit(solution)/shard_map/meet_28/pallas_call | solution.py:266
  75.6 0.0 collective-permute-done.8.refs_0_
  75.6 0.0 collective-permute-done.9.refs_1_
  75.6 0.0 collective-permute-done.18.refs_2_
  75.7 9.0 %meet_12.3 = f32[128,1,512]{2,1,0:T(1,128)} custom-call(bf16[528,768]{1,0:T(8,128)(2,1)} %collective-permute-done.8.refs_0_, bf16[528,768]{1,0:T(8,128)(2,1)} %collective-permute-done.9.refs_1_, bf16[528,768]{1,0:T(8,128)(2,1)} %collective-permute-done.18.refs_2_, bf16[528,768]{1,0:T(8,128)(2,1)} %collective-permute-done.1.refs_2_.refs_5_.refs_3_, ...), custom_call_target="tpu_custom_call" | custom-call | flops 4831838208 | bytes 8921088 | tf_op jit(solution)/shard_map/meet_12/pallas_call | solution.py:266
  84.6 19.9 %all_to_all.5.arrived_ref = f32[128,1,512]{2,1,0:T(1,128)} all-to-all(f32[128,1,512]{2,1,0:T(1,128)} %meet_12.3), channel_id=1, replica_groups=mesh['group'=8,'row'=16] {'group','row'}, dimensions={0} | all-to-all | bytes 524288 | tf_op jit(solution)/shard_map/all_to_all | solution.py:340
  104.6 1.9 %finish.1 = f32[1,512]{1,0:T(1,128)} custom-call(f32[128,1,512]{2,1,0:T(1,128)} %all_to_all.5.arrived_ref, s32[1,512]{1,0:T(1,128)} %get-tuple-element.28.target_ref), custom_call_target="tpu_custom_call" | custom-call | tf_op jit(solution)/shard_map/finish/pallas_call | solution.py:302
Async XLA Ops:
  3.2 13.8 %collective-permute-start = (bf16[528,768]{1,0:T(8,128)(2,1)}, bf16[528,768]{1,0:T(8,128)(2,1)}, u32[]{:S(2)}, u32[]{:S(2)}) collective-permute-start(bf16[528,768]{1,0:T(8,128)(2,1)} %get-tuple-element.17.refs_0_.refs_3_), channel_id=1, source_target_pairs={{0,4},{1,3},{2,6},{3,65},{4,8},{5,7},{6,10},{7,69},{8,12},{9,11},{... | collective-permute-start | bytes 2433032 | tf_op jit(solution)/shard_map/ppermute | solution.py:82
  5.3 16.4 %collective-permute-start.1 = (bf16[528,768]{1,0:T(8,128)(2,1)}, bf16[528,768]{1,0:T(8,128)(2,1)}, u32[]{:S(2)}, u32[]{:S(2)}) collective-permute-start(bf16[528,768]{1,0:T(8,128)(2,1)} %get-tuple-element.17.refs_0_.refs_3_), channel_id=1, source_target_pairs={{0,48},{1,17},{2,50},{3,19},{4,52},{5,21},{6,54},{7,23},{8,56},{9,... | collective-permute-start | bytes 2433032 | tf_op jit(solution)/shard_map/ppermute | solution.py:82
  6.5 17.0 %collective-permute-start.2 = (bf16[528,768]{1,0:T(8,128)(2,1)}, bf16[528,768]{1,0:T(8,128)(2,1)}, u32[]{:S(2)}, u32[]{:S(2)}) collective-permute-start(bf16[528,768]{1,0:T(8,128)(2,1)} %get-tuple-element.17.refs_0_.refs_3_), channel_id=1, source_target_pairs={{0,12},{1,67},{2,14},{3,1},{4,0},{5,71},{6,2},{7,5},{8,4},{9,75},{... | collective-permute-start | bytes 2433032 | tf_op jit(solution)/shard_map/ppermute | solution.py:82
  7.9 15.5 %collective-permute-start.3 = (bf16[528,768]{1,0:T(8,128)(2,1)}, bf16[528,768]{1,0:T(8,128)(2,1)}, u32[]{:S(2)}, u32[]{:S(2)}) collective-permute-start(bf16[528,768]{1,0:T(8,128)(2,1)} %get-tuple-element.17.refs_0_.refs_3_), channel_id=1, source_target_pairs={{0,1},{1,0},{2,3},{3,2},{4,5},{5,4},{6,7},{7,6},{8,9},{9,8},{10,11... | collective-permute-start | bytes 2433032 | tf_op jit(solution)/shard_map/ppermute | solution.py:86
  17.0 6.5 %collective-permute-start.4 = (bf16[528,768]{1,0:T(8,128)(2,1)}, bf16[528,768]{1,0:T(8,128)(2,1)}, u32[]{:S(2)}, u32[]{:S(2)}) collective-permute-start(bf16[528,768]{1,0:T(8,128)(2,1)} %collective-permute-done.refs_1_.refs_4_), channel_id=1, source_target_pairs={{0,1},{1,0},{2,3},{3,2},{4,5},{5,4},{6,7},{7,6},{8,9},{9,8},{10,11... | collective-permute-start | bytes 2433032 | tf_op jit(solution)/shard_map/ppermute | solution.py:86
  19.2 12.4 %collective-permute-start.6 = (bf16[528,768]{1,0:T(8,128)(2,1)}, bf16[528,768]{1,0:T(8,128)(2,1)}, u32[]{:S(2)}, u32[]{:S(2)}) collective-permute-start(bf16[528,768]{1,0:T(8,128)(2,1)} %collective-permute-done.refs_1_.refs_4_), channel_id=1, source_target_pairs={{0,16},{1,49},{2,18},{3,51},{4,20},{5,53},{6,22},{7,55},{8,24},{9,... | collective-permute-start | bytes 2433032 | tf_op jit(solution)/shard_map/ppermute | solution.py:82
  21.7 11.7 %collective-permute-start.5 = (bf16[528,768]{1,0:T(8,128)(2,1)}, bf16[528,768]{1,0:T(8,128)(2,1)}, u32[]{:S(2)}, u32[]{:S(2)}) collective-permute-start(bf16[528,768]{1,0:T(8,128)(2,1)} %collective-permute-done.1.refs_2_.refs_5_.refs_3_), channel_id=1, source_target_pairs={{0,66},{1,13},{2,0},{3,15},{4,70},{5,1},{6,4},{7,3},{8,74},{9,5},{... | collective-permute-start | bytes 2433032 | tf_op jit(solution)/shard_map/ppermute | solution.py:82
  23.5 12.9 %collective-permute-start.7 = (bf16[528,768]{1,0:T(8,128)(2,1)}, bf16[528,768]{1,0:T(8,128)(2,1)}, u32[]{:S(2)}, u32[]{:S(2)}) collective-permute-start(bf16[528,768]{1,0:T(8,128)(2,1)} %collective-permute-done.2.refs_3_.refs_6_), channel_id=1, source_target_pairs={{0,2},{1,5},{2,64},{3,7},{4,6},{5,9},{6,68},{7,11},{8,10},{9,13},{... | collective-permute-start | bytes 2433032 | tf_op jit(solution)/shard_map/ppermute | solution.py:82
  36.4 3.4 %collective-permute-start.10 = (bf16[528,768]{1,0:T(8,128)(2,1)}, bf16[528,768]{1,0:T(8,128)(2,1)}, u32[]{:S(2)}, u32[]{:S(2)}) collective-permute-start(bf16[528,768]{1,0:T(8,128)(2,1)} %collective-permute-done.1.refs_2_.refs_5_.refs_3_), channel_id=1, source_target_pairs={{0,1},{1,0},{2,3},{3,2},{4,5},{5,4},{6,7},{7,6},{8,9},{9,8},{10,11... | collective-permute-start | bytes 2433032 | tf_op jit(solution)/shard_map/ppermute | solution.py:86
  37.5 3.5 %collective-permute-start.11 = (bf16[528,768]{1,0:T(8,128)(2,1)}, bf16[528,768]{1,0:T(8,128)(2,1)}, u32[]{:S(2)}, u32[]{:S(2)}) collective-permute-start(bf16[528,768]{1,0:T(8,128)(2,1)} %collective-permute-done.2.refs_3_.refs_6_), channel_id=1, source_target_pairs={{0,1},{1,0},{2,3},{3,2},{4,5},{5,4},{6,7},{7,6},{8,9},{9,8},{10,11... | collective-permute-start | bytes 2433032 | tf_op jit(solution)/shard_map/ppermute | solution.py:86
  37.5 4.6 %collective-permute-start.12 = (bf16[528,768]{1,0:T(8,128)(2,1)}, bf16[528,768]{1,0:T(8,128)(2,1)}, u32[]{:S(2)}, u32[]{:S(2)}) collective-permute-start(bf16[528,768]{1,0:T(8,128)(2,1)} %collective-permute-done.5.refs_0_.refs_7_), channel_id=1, source_target_pairs={{0,1},{1,0},{2,3},{3,2},{4,5},{5,4},{6,7},{7,6},{8,9},{9,8},{10,11... | collective-permute-start | bytes 2433032 | tf_op jit(solution)/shard_map/ppermute | solution.py:86
  38.0 5.8 %collective-permute-start.13 = (bf16[528,768]{1,0:T(8,128)(2,1)}, bf16[528,768]{1,0:T(8,128)(2,1)}, u32[]{:S(2)}, u32[]{:S(2)}) collective-permute-start(bf16[528,768]{1,0:T(8,128)(2,1)} %collective-permute-done.6.refs_1_.refs_8_), channel_id=1, source_target_pairs={{0,1},{1,0},{2,3},{3,2},{4,5},{5,4},{6,7},{7,6},{8,9},{9,8},{10,11... | collective-permute-start | bytes 2433032 | tf_op jit(solution)/shard_map/ppermute | solution.py:86
  38.1 6.4 %collective-permute-start.14 = (bf16[528,768]{1,0:T(8,128)(2,1)}, bf16[528,768]{1,0:T(8,128)(2,1)}, u32[]{:S(2)}, u32[]{:S(2)}) collective-permute-start(bf16[528,768]{1,0:T(8,128)(2,1)} %collective-permute-done.7.refs_2_.refs_9_), channel_id=1, source_target_pairs={{0,1},{1,0},{2,3},{3,2},{4,5},{5,4},{6,7},{7,6},{8,9},{9,8},{10,11... | collective-permute-start | bytes 2433032 | tf_op jit(solution)/shard_map/ppermute | solution.py:86
  39.8 16.3 %collective-permute-start.15 = (bf16[528,768]{1,0:T(8,128)(2,1)}, bf16[528,768]{1,0:T(8,128)(2,1)}, u32[]{:S(2)}, u32[]{:S(2)}) collective-permute-start(bf16[528,768]{1,0:T(8,128)(2,1)} %collective-permute-done.7.refs_2_.refs_9_), channel_id=1, source_target_pairs={{0,48},{1,17},{2,50},{3,19},{4,52},{5,21},{6,54},{7,23},{8,56},{9,... | collective-permute-start | bytes 2433032 | tf_op jit(solution)/shard_map/ppermute | solution.py:82
  41.0 15.1 %collective-permute-start.16 = (bf16[528,768]{1,0:T(8,128)(2,1)}, bf16[528,768]{1,0:T(8,128)(2,1)}, u32[]{:S(2)}, u32[]{:S(2)}) collective-permute-start(bf16[528,768]{1,0:T(8,128)(2,1)} %collective-permute-done.5.refs_0_.refs_7_), channel_id=1, source_target_pairs={{0,4},{1,3},{2,6},{3,65},{4,8},{5,7},{6,10},{7,69},{8,12},{9,11},{... | collective-permute-start | bytes 2433032 | tf_op jit(solution)/shard_map/ppermute | solution.py:82
  42.1 14.0 %collective-permute-start.17 = (bf16[528,768]{1,0:T(8,128)(2,1)}, bf16[528,768]{1,0:T(8,128)(2,1)}, u32[]{:S(2)}, u32[]{:S(2)}) collective-permute-start(bf16[528,768]{1,0:T(8,128)(2,1)} %collective-permute-done.5.refs_0_.refs_7_), channel_id=1, source_target_pairs={{0,66},{1,13},{2,0},{3,15},{4,70},{5,1},{6,4},{7,3},{8,74},{9,5},{... | collective-permute-start | bytes 2433032 | tf_op jit(solution)/shard_map/ppermute | solution.py:82
  56.2 5.8 %collective-permute-start.19 = (bf16[528,768]{1,0:T(8,128)(2,1)}, bf16[528,768]{1,0:T(8,128)(2,1)}, u32[]{:S(2)}, u32[]{:S(2)}) collective-permute-start(bf16[528,768]{1,0:T(8,128)(2,1)} %collective-permute-done.15.refs_0_), channel_id=1, source_target_pairs={{0,1},{1,0},{2,3},{3,2},{4,5},{5,4},{6,7},{7,6},{8,9},{9,8},{10,11... | collective-permute-start | bytes 2433032 | tf_op jit(solution)/shard_map/ppermute | solution.py:86
  57.1 18.6 %collective-permute-start.8 = (bf16[528,768]{1,0:T(8,128)(2,1)}, bf16[528,768]{1,0:T(8,128)(2,1)}, u32[]{:S(2)}, u32[]{:S(2)}) collective-permute-start(bf16[528,768]{1,0:T(8,128)(2,1)} %collective-permute-done.6.refs_1_.refs_8_), channel_id=1, source_target_pairs={{0,4},{1,3},{2,6},{3,65},{4,8},{5,7},{6,10},{7,69},{8,12},{9,11},{... | collective-permute-start | bytes 2433032 | tf_op jit(solution)/shard_map/ppermute | solution.py:82
  58.0 17.6 %collective-permute-start.9 = (bf16[528,768]{1,0:T(8,128)(2,1)}, bf16[528,768]{1,0:T(8,128)(2,1)}, u32[]{:S(2)}, u32[]{:S(2)}) collective-permute-start(bf16[528,768]{1,0:T(8,128)(2,1)} %collective-permute-done.6.refs_1_.refs_8_), channel_id=1, source_target_pairs={{0,12},{1,67},{2,14},{3,1},{4,0},{5,71},{6,2},{7,5},{8,4},{9,75},{... | collective-permute-start | bytes 2433032 | tf_op jit(solution)/shard_map/ppermute | solution.py:82
  59.7 15.9 %collective-permute-start.18 = (bf16[528,768]{1,0:T(8,128)(2,1)}, bf16[528,768]{1,0:T(8,128)(2,1)}, u32[]{:S(2)}, u32[]{:S(2)}) collective-permute-start(bf16[528,768]{1,0:T(8,128)(2,1)} %collective-permute-done.15.refs_0_), channel_id=1, source_target_pairs={{0,48},{1,17},{2,50},{3,19},{4,52},{5,21},{6,54},{7,23},{8,56},{9,... | collective-permute-start | bytes 2433032 | tf_op jit(solution)/shard_map/ppermute | solution.py:82
where the time goes:
time: 105 us; the launch traced here: 106 us
  Pallas kernels  47.4 us (45%)
  starting transfers between devices  25.9 us (25%)
  blocking collectives  19.9 us (19%)
  waiting for transfers between devices  13.1 us (12%)
    pallas_call x4, Pallas kernels, meet(): pl.pallas_call(functools.partial(meet_kernel, total, len(rows), pairs, it...  42.4 us
    all_to_all x1, blocking collectives, on_device(): lax.all_to_all(outgoing, AXES, split_axis=0, concat_axis=0, tiled=True)  19.9 us
    ppermute x12, starting transfers between devices, fetch(): return lax.ppermute(block, AXES, sorted(pairs))  17.1 us
    ppermute x12, waiting for transfers between devices, fetch(): return lax.ppermute(block, AXES, sorted(pairs))  10.3 us
    ppermute x8, starting transfers between devices, flip(): return lax.ppermute(block, AXES, [(i, i ^ 1) for i in range(128)])  8.85 us
    pallas_call x1, Pallas kernels, prepare(): pl.pallas_call(prepare_kernel, out_shape=(jax.ShapeDtypeStruct((SENT, D),...  3.15 us
    ppermute x8, waiting for transfers between devices, flip(): return lax.ppermute(block, AXES, [(i, i ^ 1) for i in range(128)])  2.78 us
  transfers between devices with their start and end apart: 20, of which 6 were waited for; matrix products, arithmetic and copies ran while one was open for 0% of the time, Pallas kernels for 31%

commit v1 on v0

--- a/solution.py
+++ b/solution.py
@@ -319,17 +319,16 @@
                 held[i + OTHER] = flip(held[i])
 
     def after(slots):
-        kept = lax.optimization_barrier((before[-1], *[held[i] for i in slots]))
-        before[-1] = kept[0]
-        held.update(zip(slots, kept[1:]))
+        for i in slots:
+            before[-1], held[i] = lax.optimization_barrier((before[-1], held[i]))
 
     go(1)
-    share((0, 1))
+    share((0, 1, 2, 3))
     go(4)
     before.append(meet(held, MEETINGS[0]))
-    after((2, 3, 4, 5, 6))
+    after((4, 5, 6))
     go(7)
-    share((2, 3, 4, 5, 6))
+    share((4, 5, 6))
     before.append(meet(held, MEETINGS[1]))
     after((7, 8, 9))
     go(10)

time: 105 us -> 101 us (0.962); the launches traced: 106 us -> 101 us
  waiting for transfers between devices: 13.1 us -> 10.9 us
  blocking collectives: 19.9 us -> 17.8 us
  starting transfers between devices: 25.9 us -> 24.3 us
    all_to_all x1, blocking collectives: 19.9 us -> 17.8 us  [on_device(): lax.all_to_all(outgoing, AXES, split_axis=0, concat_axis=0, tiled=True)]
    ppermute x8, waiting for transfers between devices: 2.78 us -> 1.14 us  [flip(): return lax.ppermute(block, AXES, [(i, i ^ 1) for i in range(128)])]
    ppermute x12, starting transfers between devices: 17.1 us -> 15.8 us  [fetch(): return lax.ppermute(block, AXES, sorted(pairs))]
  transfers between devices with their start and end apart: 20 -> 20, of which waited for: 6 -> 5; matrix products, arithmetic and copies ran while one was open for 0% -> 0% of each run, Pallas kernels for 31% -> 33%
where the time goes in v1:
time: 101 us
  Pallas kernels  47.4 us (47%)
  starting transfers between devices  24.3 us (24%)
  blocking collectives  17.8 us (18%)
  waiting for transfers between devices  10.9 us (11%)
    pallas_call x4, Pallas kernels, meet(): pl.pallas_call(functools.partial(meet_kernel, total, len(rows), pairs, it...  42.4 us
    all_to_all x1, blocking collectives, on_device(): lax.all_to_all(outgoing, AXES, split_axis=0, concat_axis=0, tiled=True)  17.8 us
    ppermute x12, starting transfers between devices, fetch(): return lax.ppermute(block, AXES, sorted(pairs))  15.8 us
    ppermute x12, waiting for transfers between devices, fetch(): return lax.ppermute(block, AXES, sorted(pairs))  9.71 us
    ppermute x8, starting transfers between devices, flip(): return lax.ppermute(block, AXES, [(i, i ^ 1) for i in range(128)])  8.49 us
    pallas_call x1, Pallas kernels, prepare(): pl.pallas_call(prepare_kernel, out_shape=(jax.ShapeDtypeStruct((SENT, D),...  3.13 us
  transfers between devices with their start and end apart: 20, of which 5 were waited for; matrix products, arithmetic and copies ran while one was open for 0% of the time, Pallas kernels for 33%

profile of v1, /device:TPU:1, one launch (start us, length us, event | category | flops | bytes accessed | tf_op | source)
XLA Modules:
  0.0 100.5 jit_solution(13702044614819684547)
XLA Ops:
  0.0 3.1 %prepare.1 = (bf16[528,768]{1,0:T(8,128)(2,1)}, s32[1,512]{1,0:T(1,128)}) custom-call(bf16[512,768]{1,0:T(8,128)(2,1)} %embeds_ref.1, s32[1,512]{1,0:T(1,128)} %bitcast.2), custom_call_target="tpu_custom_call" | custom-call | tf_op jit(solution)/shard_map/prepare/pallas_call | solution.py:126
  3.1 2.1 %collective-permute-start = (bf16[528,768]{1,0:T(8,128)(2,1)}, bf16[528,768]{1,0:T(8,128)(2,1)}, u32[]{:S(2)}, u32[]{:S(2)}) collective-permute-start(bf16[528,768]{1,0:T(8,128)(2,1)} %get-tuple-element.19.refs_0_.refs_3_), channel_id=1, source_target_pairs={{0,4},{1,3},{2,6},{3,65},{4,8},{5,7},{6,10},{7,69},{8,12},{9,11},{... | collective-permute-start | bytes 2433032 | tf_op jit(solution)/shard_map/ppermute | solution.py:82
  5.3 1.2 %collective-permute-start.1 = (bf16[528,768]{1,0:T(8,128)(2,1)}, bf16[528,768]{1,0:T(8,128)(2,1)}, u32[]{:S(2)}, u32[]{:S(2)}) collective-permute-start(bf16[528,768]{1,0:T(8,128)(2,1)} %get-tuple-element.19.refs_0_.refs_3_), channel_id=1, source_target_pairs={{0,48},{1,17},{2,50},{3,19},{4,52},{5,21},{6,54},{7,23},{8,56},{9,... | collective-permute-start | bytes 2433032 | tf_op jit(solution)/shard_map/ppermute | solution.py:82
  6.5 1.4 %collective-permute-start.2 = (bf16[528,768]{1,0:T(8,128)(2,1)}, bf16[528,768]{1,0:T(8,128)(2,1)}, u32[]{:S(2)}, u32[]{:S(2)}) collective-permute-start(bf16[528,768]{1,0:T(8,128)(2,1)} %get-tuple-element.19.refs_0_.refs_3_), channel_id=1, source_target_pairs={{0,12},{1,67},{2,14},{3,1},{4,0},{5,71},{6,2},{7,5},{8,4},{9,75},{... | collective-permute-start | bytes 2433032 | tf_op jit(solution)/shard_map/ppermute | solution.py:82
  7.9 3.5 %collective-permute-start.3 = (bf16[528,768]{1,0:T(8,128)(2,1)}, bf16[528,768]{1,0:T(8,128)(2,1)}, u32[]{:S(2)}, u32[]{:S(2)}) collective-permute-start(bf16[528,768]{1,0:T(8,128)(2,1)} %get-tuple-element.19.refs_0_.refs_3_), channel_id=1, source_target_pairs={{0,1},{1,0},{2,3},{3,2},{4,5},{5,4},{6,7},{7,6},{8,9},{9,8},{10,11... | collective-permute-start | bytes 2433032 | tf_op jit(solution)/shard_map/ppermute | solution.py:86
  11.4 5.5 %collective-permute-done.refs_1_.refs_4_ = bf16[528,768]{1,0:T(8,128)(2,1)} collective-permute-done((bf16[528,768]{1,0:T(8,128)(2,1)}, bf16[528,768]{1,0:T(8,128)(2,1)}, u32[]{:S(2)}, u32[]{:S(2)}) %collective-permute-start) | collective-permute-done | bytes 811040 | tf_op jit(solution)/shard_map/ppermute | solution.py:82
  16.9 2.3 %collective-permute-start.4 = (bf16[528,768]{1,0:T(8,128)(2,1)}, bf16[528,768]{1,0:T(8,128)(2,1)}, u32[]{:S(2)}, u32[]{:S(2)}) collective-permute-start(bf16[528,768]{1,0:T(8,128)(2,1)} %collective-permute-done.refs_1_.refs_4_), channel_id=1, source_target_pairs={{0,1},{1,0},{2,3},{3,2},{4,5},{5,4},{6,7},{7,6},{8,9},{9,8},{10,11... | collective-permute-start | bytes 2433032 | tf_op jit(solution)/shard_map/ppermute | solution.py:86
  19.2 0.0 collective-permute-done.1.refs_2_.refs_5_.refs_3_
  19.2 2.7 %collective-permute-start.5 = (bf16[528,768]{1,0:T(8,128)(2,1)}, bf16[528,768]{1,0:T(8,128)(2,1)}, u32[]{:S(2)}, u32[]{:S(2)}) collective-permute-start(bf16[528,768]{1,0:T(8,128)(2,1)} %collective-permute-done.1.refs_2_.refs_5_.refs_3_), channel_id=1, source_target_pairs={{0,66},{1,13},{2,0},{3,15},{4,70},{5,1},{6,4},{7,3},{8,74},{9,5},{... | collective-permute-start | bytes 2433032 | tf_op jit(solution)/shard_map/ppermute | solution.py:82
  21.9 1.5 %collective-permute-start.6 = (bf16[528,768]{1,0:T(8,128)(2,1)}, bf16[528,768]{1,0:T(8,128)(2,1)}, u32[]{:S(2)}, u32[]{:S(2)}) collective-permute-start(bf16[528,768]{1,0:T(8,128)(2,1)} %collective-permute-done.refs_1_.refs_4_), channel_id=1, source_target_pairs={{0,16},{1,49},{2,18},{3,51},{4,20},{5,53},{6,22},{7,55},{8,24},{9,... | collective-permute-start | bytes 2433032 | tf_op jit(solution)/shard_map/ppermute | solution.py:82
  23.4 0.0 collective-permute-done.2.refs_3_.refs_6_
  23.4 0.0 collective-permute-start.9
  23.4 0.0 collective-permute-done.3.refs_4_.refs_7_.refs_10_.refs_6_
  23.5 0.4 collective-permute-start.10
  23.8 0.0 collective-permute-done.4.refs_5_.refs_8_.refs_11_.refs_7_
  23.8 0.2 collective-permute-start.11
  24.0 8.1 %meet_12.2.refs_11_ = f32[6,512]{1,0:T(8,128)} custom-call(bf16[528,768]{1,0:T(8,128)(2,1)} %get-tuple-element.19.refs_0_.refs_3_, bf16[528,768]{1,0:T(8,128)(2,1)} %collective-permute-done.refs_1_.refs_4_, bf16[528,768]{1,0:T(8,128)(2,1)} %collective-permute-done.1.refs_2_.refs_5_.refs_3_, bf16[528,768]{1,0:T(8,128)(2,1)} %collective-permute-done.2.refs_3_.refs_6_, ...), custom_call_target="tpu_custom_call" | custom-call | flops 4831838208 | bytes 4866048 | tf_op jit(solution)/shard_map/meet_12/pallas_call | solution.py:266
  32.2 0.0 collective-permute-done.5.refs_0_.refs_7_
  32.2 1.5 %collective-permute-done.6.refs_1_.refs_8_ = bf16[528,768]{1,0:T(8,128)(2,1)} collective-permute-done((bf16[528,768]{1,0:T(8,128)(2,1)}, bf16[528,768]{1,0:T(8,128)(2,1)}, u32[]{:S(2)}, u32[]{:S(2)}) %collective-permute-start.6) | collective-permute-done | bytes 811040 | tf_op jit(solution)/shard_map/ppermute | solution.py:82
  33.7 2.7 %collective-permute-done.9.refs_2_.refs_9_ = bf16[528,768]{1,0:T(8,128)(2,1)} collective-permute-done((bf16[528,768]{1,0:T(8,128)(2,1)}, bf16[528,768]{1,0:T(8,128)(2,1)}, u32[]{:S(2)}, u32[]{:S(2)}) %collective-permute-start.9) | collective-permute-done | bytes 811040 | tf_op jit(solution)/shard_map/ppermute | solution.py:82
  36.4 1.1 %collective-permute-start.14 = (bf16[528,768]{1,0:T(8,128)(2,1)}, bf16[528,768]{1,0:T(8,128)(2,1)}, u32[]{:S(2)}, u32[]{:S(2)}) collective-permute-start(bf16[528,768]{1,0:T(8,128)(2,1)} %collective-permute-done.9.refs_2_.refs_9_), channel_id=1, source_target_pairs={{0,1},{1,0},{2,3},{3,2},{4,5},{5,4},{6,7},{7,6},{8,9},{9,8},{10,11... | collective-permute-start | bytes 2433032 | tf_op jit(solution)/shard_map/ppermute | solution.py:86
  37.5 0.0 collective-permute-start.13
  37.5 0.5 collective-permute-start.12
  38.0 0.0 collective-permute-done.10.refs_9_.refs_12_
  38.0 1.2 %collective-permute-start.15 = (bf16[528,768]{1,0:T(8,128)(2,1)}, bf16[528,768]{1,0:T(8,128)(2,1)}, u32[]{:S(2)}, u32[]{:S(2)}) collective-permute-start(bf16[528,768]{1,0:T(8,128)(2,1)} %collective-permute-done.9.refs_2_.refs_9_), channel_id=1, source_target_pairs={{0,48},{1,17},{2,50},{3,19},{4,52},{5,21},{6,54},{7,23},{8,56},{9,... | collective-permute-start | bytes 2433032 | tf_op jit(solution)/shard_map/ppermute | solution.py:82
  39.2 0.0 collective-permute-done.11.refs_10_.refs_13_.refs_8_
  39.2 0.0 collective-permute-start.17
  39.2 0.6 collective-permute-done.14.refs_13_.refs_16_.refs_9_
  39.8 1.7 %collective-permute-start.18 = (bf16[528,768]{1,0:T(8,128)(2,1)}, bf16[528,768]{1,0:T(8,128)(2,1)}, u32[]{:S(2)}, u32[]{:S(2)}) collective-permute-start(bf16[528,768]{1,0:T(8,128)(2,1)} %collective-permute-done.5.refs_0_.refs_7_), channel_id=1, source_target_pairs={{0,66},{1,13},{2,0},{3,15},{4,70},{5,1},{6,4},{7,3},{8,74},{9,5},{... | collective-permute-start | bytes 2433032 | tf_op jit(solution)/shard_map/ppermute | solution.py:82
  41.5 0.0 collective-permute-done.13.refs_12_.refs_15_
  41.5 0.6 collective-permute-done.12.refs_11_.refs_14_
  42.1 11.7 %meet_23.1.refs_12_ = f32[14,512]{1,0:T(8,128)} custom-call(bf16[528,768]{1,0:T(8,128)(2,1)} %collective-permute-done.5.refs_0_.refs_7_, bf16[528,768]{1,0:T(8,128)(2,1)} %collective-permute-done.6.refs_1_.refs_8_, bf16[528,768]{1,0:T(8,128)(2,1)} %collective-permute-done.9.refs_2_.refs_9_, bf16[528,768]{1,0:T(8,128)(2,1)} %get-tuple-element.19.refs_0_.refs_3_, ...), custom_call_target="tpu_custom_call" | custom-call | flops 9261023232 | bytes 11354112 | tf_op jit(solution)/shard_map/meet_23/pallas_call | solution.py:266
  53.8 0.0 collective-permute-done.15.refs_0_
  53.8 0.5 collective-permute-start.19
  54.3 1.6 %collective-permute-start.7 = (bf16[528,768]{1,0:T(8,128)(2,1)}, bf16[528,768]{1,0:T(8,128)(2,1)}, u32[]{:S(2)}, u32[]{:S(2)}) collective-permute-start(bf16[528,768]{1,0:T(8,128)(2,1)} %collective-permute-done.6.refs_1_.refs_8_), channel_id=1, source_target_pairs={{0,4},{1,3},{2,6},{3,65},{4,8},{5,7},{6,10},{7,69},{8,12},{9,11},{... | collective-permute-start | bytes 2433032 | tf_op jit(solution)/shard_map/ppermute | solution.py:82
  55.9 1.1 %collective-permute-start.8 = (bf16[528,768]{1,0:T(8,128)(2,1)}, bf16[528,768]{1,0:T(8,128)(2,1)}, u32[]{:S(2)}, u32[]{:S(2)}) collective-permute-start(bf16[528,768]{1,0:T(8,128)(2,1)} %collective-permute-done.6.refs_1_.refs_8_), channel_id=1, source_target_pairs={{0,12},{1,67},{2,14},{3,1},{4,0},{5,71},{6,2},{7,5},{8,4},{9,75},{... | collective-permute-start | bytes 2433032 | tf_op jit(solution)/shard_map/ppermute | solution.py:82
  56.9 0.0 collective-permute-done.17.refs_1_.refs_4_
  56.9 1.2 %collective-permute-start.16 = (bf16[528,768]{1,0:T(8,128)(2,1)}, bf16[528,768]{1,0:T(8,128)(2,1)}, u32[]{:S(2)}, u32[]{:S(2)}) collective-permute-start(bf16[528,768]{1,0:T(8,128)(2,1)} %collective-permute-done.15.refs_0_), channel_id=1, source_target_pairs={{0,48},{1,17},{2,50},{3,19},{4,52},{5,21},{6,54},{7,23},{8,56},{9,... | collective-permute-start | bytes 2433032 | tf_op jit(solution)/shard_map/ppermute | solution.py:82
  58.2 0.0 collective-permute-done.18.refs_2_.refs_5_
  58.2 0.0 collective-permute-done.19.refs_17_.refs_10_
  58.2 13.6 %meet_28.1.refs_13_ = f32[18,512]{1,0:T(8,128)} custom-call(bf16[528,768]{1,0:T(8,128)(2,1)} %collective-permute-done.15.refs_0_, bf16[528,768]{1,0:T(8,128)(2,1)} %collective-permute-done.17.refs_1_.refs_4_, bf16[528,768]{1,0:T(8,128)(2,1)} %collective-permute-done.18.refs_2_.refs_5_, bf16[528,768]{1,0:T(8,128)(2,1)} %get-tuple-element.19.refs_0_.refs_3_, ...), custom_call_target="tpu_custom_call" | custom-call | flops 11274289152 | bytes 14598144 | tf_op jit(solution)/shard_map/meet_28/pallas_call | solution.py:266
  71.8 0.0 collective-permute-done.7.refs_0_
  71.8 0.0 collective-permute-done.8.refs_1_
  71.8 0.0 collective-permute-done.16.refs_2_
  71.8 9.0 %meet_12.3 = f32[128,1,512]{2,1,0:T(1,128)} custom-call(bf16[528,768]{1,0:T(8,128)(2,1)} %collective-permute-done.7.refs_0_, bf16[528,768]{1,0:T(8,128)(2,1)} %collective-permute-done.8.refs_1_, bf16[528,768]{1,0:T(8,128)(2,1)} %collective-permute-done.16.refs_2_, bf16[528,768]{1,0:T(8,128)(2,1)} %collective-permute-done.1.refs_2_.refs_5_.refs_3_, ...), custom_call_target="tpu_custom_call" | custom-call | flops 4831838208 | bytes 8921088 | tf_op jit(solution)/shard_map/meet_12/pallas_call | solution.py:266
  80.8 17.8 %all_to_all.5.arrived_ref = f32[128,1,512]{2,1,0:T(1,128)} all-to-all(f32[128,1,512]{2,1,0:T(1,128)} %meet_12.3), channel_id=1, replica_groups=mesh['group'=8,'row'=16] {'group','row'}, dimensions={0} | all-to-all | bytes 524288 | tf_op jit(solution)/shard_map/all_to_all | solution.py:339
  98.6 1.9 %finish.1 = f32[1,512]{1,0:T(1,128)} custom-call(f32[128,1,512]{2,1,0:T(1,128)} %all_to_all.5.arrived_ref, s32[1,512]{1,0:T(1,128)} %get-tuple-element.32.target_ref), custom_call_target="tpu_custom_call" | custom-call | tf_op jit(solution)/shard_map/finish/pallas_call | solution.py:302
Async XLA Ops:
  3.1 13.8 %collective-permute-start = (bf16[528,768]{1,0:T(8,128)(2,1)}, bf16[528,768]{1,0:T(8,128)(2,1)}, u32[]{:S(2)}, u32[]{:S(2)}) collective-permute-start(bf16[528,768]{1,0:T(8,128)(2,1)} %get-tuple-element.19.refs_0_.refs_3_), channel_id=1, source_target_pairs={{0,4},{1,3},{2,6},{3,65},{4,8},{5,7},{6,10},{7,69},{8,12},{9,11},{... | collective-permute-start | bytes 2433032 | tf_op jit(solution)/shard_map/ppermute | solution.py:82
  5.3 14.0 %collective-permute-start.1 = (bf16[528,768]{1,0:T(8,128)(2,1)}, bf16[528,768]{1,0:T(8,128)(2,1)}, u32[]{:S(2)}, u32[]{:S(2)}) collective-permute-start(bf16[528,768]{1,0:T(8,128)(2,1)} %get-tuple-element.19.refs_0_.refs_3_), channel_id=1, source_target_pairs={{0,48},{1,17},{2,50},{3,19},{4,52},{5,21},{6,54},{7,23},{8,56},{9,... | collective-permute-start | bytes 2433032 | tf_op jit(solution)/shard_map/ppermute | solution.py:82
  6.5 17.0 %collective-permute-start.2 = (bf16[528,768]{1,0:T(8,128)(2,1)}, bf16[528,768]{1,0:T(8,128)(2,1)}, u32[]{:S(2)}, u32[]{:S(2)}) collective-permute-start(bf16[528,768]{1,0:T(8,128)(2,1)} %get-tuple-element.19.refs_0_.refs_3_), channel_id=1, source_target_pairs={{0,12},{1,67},{2,14},{3,1},{4,0},{5,71},{6,2},{7,5},{8,4},{9,75},{... | collective-permute-start | bytes 2433032 | tf_op jit(solution)/shard_map/ppermute | solution.py:82
  7.9 15.5 %collective-permute-start.3 = (bf16[528,768]{1,0:T(8,128)(2,1)}, bf16[528,768]{1,0:T(8,128)(2,1)}, u32[]{:S(2)}, u32[]{:S(2)}) collective-permute-start(bf16[528,768]{1,0:T(8,128)(2,1)} %get-tuple-element.19.refs_0_.refs_3_), channel_id=1, source_target_pairs={{0,1},{1,0},{2,3},{3,2},{4,5},{5,4},{6,7},{7,6},{8,9},{9,8},{10,11... | collective-permute-start | bytes 2433032 | tf_op jit(solution)/shard_map/ppermute | solution.py:86
  16.9 6.9 %collective-permute-start.4 = (bf16[528,768]{1,0:T(8,128)(2,1)}, bf16[528,768]{1,0:T(8,128)(2,1)}, u32[]{:S(2)}, u32[]{:S(2)}) collective-permute-start(bf16[528,768]{1,0:T(8,128)(2,1)} %collective-permute-done.refs_1_.refs_4_), channel_id=1, source_target_pairs={{0,1},{1,0},{2,3},{3,2},{4,5},{5,4},{6,7},{7,6},{8,9},{9,8},{10,11... | collective-permute-start | bytes 2433032 | tf_op jit(solution)/shard_map/ppermute | solution.py:86
  19.2 13.0 %collective-permute-start.5 = (bf16[528,768]{1,0:T(8,128)(2,1)}, bf16[528,768]{1,0:T(8,128)(2,1)}, u32[]{:S(2)}, u32[]{:S(2)}) collective-permute-start(bf16[528,768]{1,0:T(8,128)(2,1)} %collective-permute-done.1.refs_2_.refs_5_.refs_3_), channel_id=1, source_target_pairs={{0,66},{1,13},{2,0},{3,15},{4,70},{5,1},{6,4},{7,3},{8,74},{9,5},{... | collective-permute-start | bytes 2433032 | tf_op jit(solution)/shard_map/ppermute | solution.py:82
  21.9 11.7 %collective-permute-start.6 = (bf16[528,768]{1,0:T(8,128)(2,1)}, bf16[528,768]{1,0:T(8,128)(2,1)}, u32[]{:S(2)}, u32[]{:S(2)}) collective-permute-start(bf16[528,768]{1,0:T(8,128)(2,1)} %collective-permute-done.refs_1_.refs_4_), channel_id=1, source_target_pairs={{0,16},{1,49},{2,18},{3,51},{4,20},{5,53},{6,22},{7,55},{8,24},{9,... | collective-permute-start | bytes 2433032 | tf_op jit(solution)/shard_map/ppermute | solution.py:82
  23.4 12.9 %collective-permute-start.9 = (bf16[528,768]{1,0:T(8,128)(2,1)}, bf16[528,768]{1,0:T(8,128)(2,1)}, u32[]{:S(2)}, u32[]{:S(2)}) collective-permute-start(bf16[528,768]{1,0:T(8,128)(2,1)} %collective-permute-done.2.refs_3_.refs_6_), channel_id=1, source_target_pairs={{0,2},{1,5},{2,64},{3,7},{4,6},{5,9},{6,68},{7,11},{8,10},{9,13},{... | collective-permute-start | bytes 2433032 | tf_op jit(solution)/shard_map/ppermute | solution.py:82
  23.5 14.6 %collective-permute-start.10 = (bf16[528,768]{1,0:T(8,128)(2,1)}, bf16[528,768]{1,0:T(8,128)(2,1)}, u32[]{:S(2)}, u32[]{:S(2)}) collective-permute-start(bf16[528,768]{1,0:T(8,128)(2,1)} %collective-permute-done.1.refs_2_.refs_5_.refs_3_), channel_id=1, source_target_pairs={{0,1},{1,0},{2,3},{3,2},{4,5},{5,4},{6,7},{7,6},{8,9},{9,8},{10,11... | collective-permute-start | bytes 2433032 | tf_op jit(solution)/shard_map/ppermute | solution.py:86
  23.8 15.4 %collective-permute-start.11 = (bf16[528,768]{1,0:T(8,128)(2,1)}, bf16[528,768]{1,0:T(8,128)(2,1)}, u32[]{:S(2)}, u32[]{:S(2)}) collective-permute-start(bf16[528,768]{1,0:T(8,128)(2,1)} %collective-permute-done.2.refs_3_.refs_6_), channel_id=1, source_target_pairs={{0,1},{1,0},{2,3},{3,2},{4,5},{5,4},{6,7},{7,6},{8,9},{9,8},{10,11... | collective-permute-start | bytes 2433032 | tf_op jit(solution)/shard_map/ppermute | solution.py:86
  36.4 3.4 %collective-permute-start.14 = (bf16[528,768]{1,0:T(8,128)(2,1)}, bf16[528,768]{1,0:T(8,128)(2,1)}, u32[]{:S(2)}, u32[]{:S(2)}) collective-permute-start(bf16[528,768]{1,0:T(8,128)(2,1)} %collective-permute-done.9.refs_2_.refs_9_), channel_id=1, source_target_pairs={{0,1},{1,0},{2,3},{3,2},{4,5},{5,4},{6,7},{7,6},{8,9},{9,8},{10,11... | collective-permute-start | bytes 2433032 | tf_op jit(solution)/shard_map/ppermute | solution.py:86
  37.5 4.0 %collective-permute-start.13 = (bf16[528,768]{1,0:T(8,128)(2,1)}, bf16[528,768]{1,0:T(8,128)(2,1)}, u32[]{:S(2)}, u32[]{:S(2)}) collective-permute-start(bf16[528,768]{1,0:T(8,128)(2,1)} %collective-permute-done.6.refs_1_.refs_8_), channel_id=1, source_target_pairs={{0,1},{1,0},{2,3},{3,2},{4,5},{5,4},{6,7},{7,6},{8,9},{9,8},{10,11... | collective-permute-start | bytes 2433032 | tf_op jit(solution)/shard_map/ppermute | solution.py:86
  37.5 4.6 %collective-permute-start.12 = (bf16[528,768]{1,0:T(8,128)(2,1)}, bf16[528,768]{1,0:T(8,128)(2,1)}, u32[]{:S(2)}, u32[]{:S(2)}) collective-permute-start(bf16[528,768]{1,0:T(8,128)(2,1)} %collective-permute-done.5.refs_0_.refs_7_), channel_id=1, source_target_pairs={{0,1},{1,0},{2,3},{3,2},{4,5},{5,4},{6,7},{7,6},{8,9},{9,8},{10,11... | collective-permute-start | bytes 2433032 | tf_op jit(solution)/shard_map/ppermute | solution.py:86
  38.0 15.8 %collective-permute-start.15 = (bf16[528,768]{1,0:T(8,128)(2,1)}, bf16[528,768]{1,0:T(8,128)(2,1)}, u32[]{:S(2)}, u32[]{:S(2)}) collective-permute-start(bf16[528,768]{1,0:T(8,128)(2,1)} %collective-permute-done.9.refs_2_.refs_9_), channel_id=1, source_target_pairs={{0,48},{1,17},{2,50},{3,19},{4,52},{5,21},{6,54},{7,23},{8,56},{9,... | collective-permute-start | bytes 2433032 | tf_op jit(solution)/shard_map/ppermute | solution.py:82
  39.2 17.7 %collective-permute-start.17 = (bf16[528,768]{1,0:T(8,128)(2,1)}, bf16[528,768]{1,0:T(8,128)(2,1)}, u32[]{:S(2)}, u32[]{:S(2)}) collective-permute-start(bf16[528,768]{1,0:T(8,128)(2,1)} %collective-permute-done.5.refs_0_.refs_7_), channel_id=1, source_target_pairs={{0,4},{1,3},{2,6},{3,65},{4,8},{5,7},{6,10},{7,69},{8,12},{9,11},{... | collective-permute-start | bytes 2433032 | tf_op jit(solution)/shard_map/ppermute | solution.py:82
  39.8 18.4 %collective-permute-start.18 = (bf16[528,768]{1,0:T(8,128)(2,1)}, bf16[528,768]{1,0:T(8,128)(2,1)}, u32[]{:S(2)}, u32[]{:S(2)}) collective-permute-start(bf16[528,768]{1,0:T(8,128)(2,1)} %collective-permute-done.5.refs_0_.refs_7_), channel_id=1, source_target_pairs={{0,66},{1,13},{2,0},{3,15},{4,70},{5,1},{6,4},{7,3},{8,74},{9,5},{... | collective-permute-start | bytes 2433032 | tf_op jit(solution)/shard_map/ppermute | solution.py:82
  53.8 4.3 %collective-permute-start.19 = (bf16[528,768]{1,0:T(8,128)(2,1)}, bf16[528,768]{1,0:T(8,128)(2,1)}, u32[]{:S(2)}, u32[]{:S(2)}) collective-permute-start(bf16[528,768]{1,0:T(8,128)(2,1)} %collective-permute-done.15.refs_0_), channel_id=1, source_target_pairs={{0,1},{1,0},{2,3},{3,2},{4,5},{5,4},{6,7},{7,6},{8,9},{9,8},{10,11... | collective-permute-start | bytes 2433032 | tf_op jit(solution)/shard_map/ppermute | solution.py:86
  54.3 17.5 %collective-permute-start.7 = (bf16[528,768]{1,0:T(8,128)(2,1)}, bf16[528,768]{1,0:T(8,128)(2,1)}, u32[]{:S(2)}, u32[]{:S(2)}) collective-permute-start(bf16[528,768]{1,0:T(8,128)(2,1)} %collective-permute-done.6.refs_1_.refs_8_), channel_id=1, source_target_pairs={{0,4},{1,3},{2,6},{3,65},{4,8},{5,7},{6,10},{7,69},{8,12},{9,11},{... | collective-permute-start | bytes 2433032 | tf_op jit(solution)/shard_map/ppermute | solution.py:82
  55.9 15.9 %collective-permute-start.8 = (bf16[528,768]{1,0:T(8,128)(2,1)}, bf16[528,768]{1,0:T(8,128)(2,1)}, u32[]{:S(2)}, u32[]{:S(2)}) collective-permute-start(bf16[528,768]{1,0:T(8,128)(2,1)} %collective-permute-done.6.refs_1_.refs_8_), channel_id=1, source_target_pairs={{0,12},{1,67},{2,14},{3,1},{4,0},{5,71},{6,2},{7,5},{8,4},{9,75},{... | collective-permute-start | bytes 2433032 | tf_op jit(solution)/shard_map/ppermute | solution.py:82
  56.9 14.9 %collective-permute-start.16 = (bf16[528,768]{1,0:T(8,128)(2,1)}, bf16[528,768]{1,0:T(8,128)(2,1)}, u32[]{:S(2)}, u32[]{:S(2)}) collective-permute-start(bf16[528,768]{1,0:T(8,128)(2,1)} %collective-permute-done.15.refs_0_), channel_id=1, source_target_pairs={{0,48},{1,17},{2,50},{3,19},{4,52},{5,21},{6,54},{7,23},{8,56},{9,... | collective-permute-start | bytes 2433032 | tf_op jit(solution)/shard_map/ppermute | solution.py:82

commit v2 on v1

--- a/solution.py
+++ b/solution.py
@@ -21,26 +21,30 @@
 AXES = ("group", "row")
 
 UNIT = ((1, 0, 0), (0, 1, 0), (0, 0, 1), (3, 0, 0), (0, 3, 0), (0, 0, 3))
-PARENT = (None,) + (0, 0, 0, 2, 1, 3, 6, 4, 4, 5, 5, 7)
+PARENT = (None,) + (0, 0, 0, 0, 2, 1, 4, 2, 5, 7, 9, 5)
 DIRS = (
-    (None,) + (5, 0, 2, 1, 3, 4, 0, 5, 1, 5, 2, 0),
-    (None,) + (4, 3, 1, 2, 0, 5, 3, 4, 2, 4, 1, 3),
+    (None,) + (4, 2, 5, 1, 3, 0, 5, 1, 3, 5, 4, 2),
+    (None,) + (1, 3, 0, 4, 2, 5, 0, 4, 2, 0, 1, 3),
 )
 SLOTS = len(PARENT)
 OTHER = 20
 MEETINGS = (
-    ((0, (0, 20)), (1, (0, 20, 21)), (2, (0, 1, 20, 21)), (3, (1, 2, 20, 21))),
+    ((0, (0, 20)), (1, (0, 20, 21)), (2, (0, 1, 20, 21, 22)), (3, (1, 2, 20, 21, 22, 23))),
     (
-        (4, (0, 1, 2, 3, 21, 22)),
-        (5, (2, 3, 4, 20, 21, 23, 24, 25)),
-        (6, (0, 1, 4, 5, 20, 22, 23, 25, 26)),
+        (4, (1, 20, 23)),
+        (5, (0, 1, 2, 3, 4, 21, 23, 24)),
+        (6, (0, 3, 4, 5, 21, 22, 26)),
     ),
     (
-        (7, (0, 3, 4, 5, 21, 22, 23, 24, 26, 27)),
-        (8, (3, 5, 6, 7, 20, 21, 24, 25, 27)),
-        (9, (0, 1, 2, 5, 6, 8, 22, 26, 27)),
+        (7, (1, 2, 5, 6, 23, 24, 27)),
+        (8, (5, 6, 20, 22, 27)),
+        (9, (0, 2, 3, 4, 6, 21, 24, 26)),
     ),
-    ((10, (2, 9, 20, 21, 23)), (11, (2, 8, 9, 20, 26)), (12, (23, 27))),
+    (
+        (10, (1, 6, 20, 21, 23, 24, 27)),
+        (11, (2, 6, 7, 8, 10, 21, 23, 26)),
+        (12, (1, 6, 20, 21, 23, 26, 27)),
+    ),
 )
 
 
@@ -103,11 +107,16 @@
 
 def prepare_kernel(embeds_ref, member_ref, block_ref, target_ref):
     member = member_ref[...].astype(jnp.float32)
-    column = jnp.transpose(jnp.broadcast_to(member, (128, RB)))[:, 0:1]
+    cluster = lax.broadcasted_iota(jnp.int32, (16, RB), 0).astype(jnp.float32)
+    hits = cluster == member
+    ones = jnp.where(hits, 1.0, 0.0)
     above = lax.broadcasted_iota(jnp.int32, (RB, RB), 0)
     across = lax.broadcasted_iota(jnp.int32, (RB, RB), 1)
-    before = (column < member) | ((column == member) & (above < across))
-    target = jnp.sum(before.astype(jnp.float32), axis=0, keepdims=True).astype(jnp.int32)
+    earlier = (above < across).astype(jnp.bfloat16)
+    rank = jnp.dot(ones.astype(jnp.bfloat16), earlier, preferred_element_type=jnp.float32)
+    counts = jnp.sum(ones, axis=1, keepdims=True)
+    parts = jnp.where(cluster < member, counts, 0.0) + jnp.where(hits, rank, 0.0)
+    target = jnp.sum(parts, axis=0, keepdims=True).astype(jnp.int32)
     target_ref[...] = target
     values = embeds_ref[...].astype(jnp.float32)
     total = jnp.sum(values * values, axis=1, keepdims=True)
@@ -116,10 +125,16 @@
     block_ref[0:RB, :] = jnp.dot(placer, normed, preferred_element_type=jnp.float32).astype(
         jnp.bfloat16
     )
-    ordered = jnp.sum(jnp.where(above == target, member, 0.0), axis=1, keepdims=True)
-    ordered = jnp.transpose(jnp.broadcast_to(ordered, (RB, 128)))[0:META]
+    upto = lax.broadcasted_iota(jnp.int32, (16, 16), 1) <= lax.broadcasted_iota(
+        jnp.int32, (16, 16), 0
+    )
+    spread = jnp.transpose(jnp.broadcast_to(counts, (16, 16)))
+    ends = jnp.sum(jnp.where(upto, spread, 0.0), axis=1, keepdims=True)
+    places = lax.broadcasted_iota(jnp.int32, (16, RB), 1).astype(jnp.float32)
+    passed = jnp.where(places >= ends, 1.0, 0.0)[0:GROUPS]
+    ordered = jnp.sum(passed, axis=0, keepdims=True)
     block_ref[RB:SENT, :] = jnp.zeros((META, D), jnp.bfloat16)
-    block_ref[RB:SENT, 0:RB] = ordered.astype(jnp.bfloat16)
+    block_ref[RB:SENT, 0:RB] = jnp.broadcast_to(ordered, (META, RB)).astype(jnp.bfloat16)
 
 
 def prepare(embeds, member):

time: 101 us -> 104 us (1.030)
  starting transfers between devices: 24.3 us -> 26.1 us
  blocking collectives: 17.8 us -> 18.9 us
  waiting for transfers between devices: 10.9 us -> 9.81 us
    ppermute x8 -> x7, starting transfers between devices: 8.49 us -> 9.71 us  [flip(): return lax.ppermute(block, AXES, [(i, i ^ 1) for i in range(128)])]
    all_to_all x1, blocking collectives: 17.8 us -> 18.9 us  [on_device(): lax.all_to_all(outgoing, AXES, split_axis=0, concat_axis=0, tiled=True)]
  transfers between devices with their start and end apart: 20 -> 19, of which waited for: 5 -> 7; matrix products, arithmetic and copies ran while one was open for 0% -> 0% of each run, Pallas kernels for 33% -> 29%
where the time goes in v2:
time: 104 us
  Pallas kernels  47.9 us (46%)
  starting transfers between devices  26.1 us (25%)
  blocking collectives  18.9 us (18%)
  waiting for transfers between devices  9.81 us (9%)
    pallas_call x4, Pallas kernels, meet(): pl.pallas_call(functools.partial(meet_kernel, total, len(rows), pairs, it...  43.1 us
    all_to_all x1, blocking collectives, on_device(): lax.all_to_all(outgoing, AXES, split_axis=0, concat_axis=0, tiled=True)  18.9 us
    ppermute x12, starting transfers between devices, fetch(): return lax.ppermute(block, AXES, sorted(pairs))  16.4 us
    ppermute x7, starting transfers between devices, flip(): return lax.ppermute(block, AXES, [(i, i ^ 1) for i in range(128)])  9.71 us
    ppermute x12, waiting for transfers between devices, fetch(): return lax.ppermute(block, AXES, sorted(pairs))  9.44 us
    pallas_call x1, Pallas kernels, prepare(): pl.pallas_call(prepare_kernel, out_shape=(jax.ShapeDtypeStruct((SENT, D),...  2.89 us
  transfers between devices with their start and end apart: 19, of which 7 were waited for; matrix products, arithmetic and copies ran while one was open for 0% of the time, Pallas kernels for 29%

profile of v2, /device:TPU:1, one launch (start us, length us, event | category | flops | bytes accessed | tf_op | source)
XLA Modules:
  0.0 103.7 jit_solution(4513590600495464058)
XLA Ops:
  0.0 2.9 %prepare.1 = (bf16[528,768]{1,0:T(8,128)(2,1)}, s32[1,512]{1,0:T(1,128)}) custom-call(bf16[512,768]{1,0:T(8,128)(2,1)} %embeds_ref.1, s32[1,512]{1,0:T(1,128)} %bitcast.2), custom_call_target="tpu_custom_call" | custom-call | tf_op jit(solution)/shard_map/prepare/pallas_call | solution.py:141
  2.9 3.6 %collective-permute-start = (bf16[528,768]{1,0:T(8,128)(2,1)}, bf16[528,768]{1,0:T(8,128)(2,1)}, u32[]{:S(2)}, u32[]{:S(2)}) collective-permute-start(bf16[528,768]{1,0:T(8,128)(2,1)} %get-tuple-element.19.refs_0_.refs_3_), channel_id=1, source_target_pairs={{0,2},{1,67},{2,64},{3,1},{4,6},{5,71},{6,68},{7,5},{8,10},{9,75},... | collective-permute-start | bytes 2433032 | tf_op jit(solution)/shard_map/ppermute | solution.py:86
  6.4 1.2 %collective-permute-start.1 = (bf16[528,768]{1,0:T(8,128)(2,1)}, bf16[528,768]{1,0:T(8,128)(2,1)}, u32[]{:S(2)}, u32[]{:S(2)}) collective-permute-start(bf16[528,768]{1,0:T(8,128)(2,1)} %get-tuple-element.19.refs_0_.refs_3_), channel_id=1, source_target_pairs={{0,12},{1,17},{2,14},{3,19},{4,0},{5,21},{6,2},{7,23},{8,4},{9,25}... | collective-permute-start | bytes 2433032 | tf_op jit(solution)/shard_map/ppermute | solution.py:86
  7.6 1.5 %collective-permute-start.2 = (bf16[528,768]{1,0:T(8,128)(2,1)}, bf16[528,768]{1,0:T(8,128)(2,1)S(1)}, u32[]{:S(2)}, u32[]{:S(2)}) collective-permute-start(bf16[528,768]{1,0:T(8,128)(2,1)} %get-tuple-element.19.refs_0_.refs_3_), channel_id=1, source_target_pairs={{0,4},{1,49},{2,6},{3,51},{4,8},{5,53},{6,10},{7,55},{8,12},{9,57}... | collective-permute-start | bytes 2433032 | tf_op jit(solution)/shard_map/ppermute | solution.py:86
  9.1 0.9 collective-permute-start.3
  10.0 6.0 %collective-permute-done.refs_1_.refs_4_.refs_3_ = bf16[528,768]{1,0:T(8,128)(2,1)} collective-permute-done((bf16[528,768]{1,0:T(8,128)(2,1)}, bf16[528,768]{1,0:T(8,128)(2,1)}, u32[]{:S(2)}, u32[]{:S(2)}) %collective-permute-start) | collective-permute-done | bytes 811040 | tf_op jit(solution)/shard_map/ppermute | solution.py:86
  16.0 2.1 %collective-permute-start.4 = (bf16[528,768]{1,0:T(8,128)(2,1)}, bf16[528,768]{1,0:T(8,128)(2,1)}, u32[]{:S(2)}, u32[]{:S(2)}) collective-permute-start(bf16[528,768]{1,0:T(8,128)(2,1)} %collective-permute-done.refs_1_.refs_4_.refs_3_), channel_id=1, source_target_pairs={{0,1},{1,0},{2,3},{3,2},{4,5},{5,4},{6,7},{7,6},{8,9},{9,8},{10,11... | collective-permute-start | bytes 2433032 | tf_op jit(solution)/shard_map/ppermute | solution.py:90
  18.1 1.2 %collective-permute-done.1.refs_2_.refs_5_.refs_4_ = bf16[528,768]{1,0:T(8,128)(2,1)} collective-permute-done((bf16[528,768]{1,0:T(8,128)(2,1)}, bf16[528,768]{1,0:T(8,128)(2,1)}, u32[]{:S(2)}, u32[]{:S(2)}) %collective-permute-start.1) | collective-permute-done | bytes 811040 | tf_op jit(solution)/shard_map/ppermute | solution.py:86
  19.3 0.8 collective-permute-start.5
  20.1 0.0 collective-permute-done.2.refs_3_.refs_6_
  20.1 0.0 copy-start
  20.1 0.9 copy-done
  21.0 3.6 %collective-permute-start.6 = (bf16[528,768]{1,0:T(8,128)(2,1)S(1)}, bf16[528,768]{1,0:T(8,128)(2,1)}, u32[]{:S(2)}, u32[]{:S(2)}) collective-permute-start(bf16[528,768]{1,0:T(8,128)(2,1)S(1)} %collective-permute-done.2.refs_3_.refs_6_), channel_id=1, source_target_pairs={{0,1},{1,0},{2,3},{3,2},{4,5},{5,4},{6,7},{7,6},{8,9},{9,8},{10,11... | collective-permute-start | bytes 2433032 | tf_op jit(solution)/shard_map/ppermute | solution.py:90
  24.6 1.3 %collective-permute-start.7 = (bf16[528,768]{1,0:T(8,128)(2,1)}, bf16[528,768]{1,0:T(8,128)(2,1)}, u32[]{:S(2)}, u32[]{:S(2)}) collective-permute-start(bf16[528,768]{1,0:T(8,128)(2,1)} %get-tuple-element.19.refs_0_.refs_3_), channel_id=1, source_target_pairs={{0,66},{1,3},{2,0},{3,65},{4,70},{5,7},{6,4},{7,69},{8,74},{9,11},... | collective-permute-start | bytes 2433032 | tf_op jit(solution)/shard_map/ppermute | solution.py:86
  25.9 0.0 collective-permute-done.3.refs_4_.refs_7_.refs_10_.refs_8_
  25.9 0.0 collective-permute-start.8
  25.9 0.0 collective-permute-done.4.refs_5_.refs_8_.refs_11_.refs_9_
  25.9 1.5 %collective-permute-start.9 = (bf16[528,768]{1,0:T(8,128)(2,1)}, bf16[528,768]{1,0:T(8,128)(2,1)}, u32[]{:S(2)}, u32[]{:S(2)}) collective-permute-start(bf16[528,768]{1,0:T(8,128)(2,1)} %collective-permute-done.refs_1_.refs_4_.refs_3_), channel_id=1, source_target_pairs={{0,48},{1,5},{2,50},{3,7},{4,52},{5,9},{6,54},{7,11},{8,56},{9,13}... | collective-permute-start | bytes 2433032 | tf_op jit(solution)/shard_map/ppermute | solution.py:86
  27.4 0.0 collective-permute-done.5.refs_6_.refs_9_.refs_12_
  27.4 0.0 collective-permute-done.6.refs_7_.refs_10_.refs_13_
  27.4 9.4 %meet_15.1.refs_14_ = f32[8,512]{1,0:T(8,128)} custom-call(bf16[528,768]{1,0:T(8,128)(2,1)} %get-tuple-element.19.refs_0_.refs_3_, bf16[528,768]{1,0:T(8,128)(2,1)} %collective-permute-done.refs_1_.refs_4_.refs_3_, bf16[528,768]{1,0:T(8,128)(2,1)} %collective-permute-done.1.refs_2_.refs_5_.refs_4_, bf16[528,768]{1,0:T(8,128)(2,1)} %copy-done, ...), custom_call_target="tpu_custom_call" | custom-call | flops 6039797760 | bytes 6488064 | tf_op jit(solution)/shard_map/meet_15/pallas_call | solution.py:281
  36.7 0.8 collective-permute-done.7.refs_0_.refs_7_
  37.5 0.1 collective-permute-done.8.refs_1_.refs_8_
  37.6 1.3 %collective-permute-done.9.refs_2_.refs_9_.refs_5_ = bf16[528,768]{1,0:T(8,128)(2,1)} collective-permute-done((bf16[528,768]{1,0:T(8,128)(2,1)}, bf16[528,768]{1,0:T(8,128)(2,1)}, u32[]{:S(2)}, u32[]{:S(2)}) %collective-permute-start.9) | collective-permute-done | bytes 811040 | tf_op jit(solution)/shard_map/ppermute | solution.py:86
  38.9 1.4 %collective-permute-start.11 = (bf16[528,768]{1,0:T(8,128)(2,1)}, bf16[528,768]{1,0:T(8,128)(2,1)}, u32[]{:S(2)}, u32[]{:S(2)}) collective-permute-start(bf16[528,768]{1,0:T(8,128)(2,1)} %collective-permute-done.9.refs_2_.refs_9_.refs_5_), channel_id=1, source_target_pairs={{0,1},{1,0},{2,3},{3,2},{4,5},{5,4},{6,7},{7,6},{8,9},{9,8},{10,11... | collective-permute-start | bytes 2433032 | tf_op jit(solution)/shard_map/ppermute | solution.py:90
  40.3 0.0 collective-permute-start.10
  40.3 2.7 %collective-permute-start.12 = (bf16[528,768]{1,0:T(8,128)(2,1)}, bf16[528,768]{1,0:T(8,128)(2,1)}, u32[]{:S(2)}, u32[]{:S(2)}) collective-permute-start(bf16[528,768]{1,0:T(8,128)(2,1)} %collective-permute-done.7.refs_0_.refs_7_), channel_id=1, source_target_pairs={{0,4},{1,49},{2,6},{3,51},{4,8},{5,53},{6,10},{7,55},{8,12},{9,57}... | collective-permute-start | bytes 2433032 | tf_op jit(solution)/shard_map/ppermute | solution.py:86
  43.0 0.1 collective-permute-start.14
  43.1 0.3 collective-permute-start.15
  43.4 0.0 collective-permute-done.11.refs_12_.refs_15_
  43.4 0.4 collective-permute-done.10.refs_11_.refs_14_
  43.8 9.9 %meet_18.1.refs_15_ = f32[13,512]{1,0:T(8,128)} custom-call(bf16[528,768]{1,0:T(8,128)(2,1)} %collective-permute-done.7.refs_0_.refs_7_, bf16[528,768]{1,0:T(8,128)(2,1)} %collective-permute-done.8.refs_1_.refs_8_, bf16[528,768]{1,0:T(8,128)(2,1)} %collective-permute-done.9.refs_2_.refs_9_.refs_5_, bf16[528,768]{1,0:T(8,128)(2,1)} %get-tuple-element.19.refs_0_.refs_3_, ...), custom_call_target="tpu_custom_call" | custom-call | flops 7247757312 | bytes 10543104 | tf_op jit(solution)/shard_map/meet_18/pallas_call | solution.py:281
  53.7 0.0 collective-permute-done.12.refs_0_.refs_6_
  53.7 0.9 collective-permute-start.18
  54.6 1.2 %collective-permute-start.17 = (bf16[528,768]{1,0:T(8,128)(2,1)}, bf16[528,768]{1,0:T(8,128)(2,1)}, u32[]{:S(2)}, u32[]{:S(2)}) collective-permute-start(bf16[528,768]{1,0:T(8,128)(2,1)} %collective-permute-done.8.refs_1_.refs_8_), channel_id=1, source_target_pairs={{0,12},{1,17},{2,14},{3,19},{4,0},{5,21},{6,2},{7,23},{8,4},{9,25}... | collective-permute-start | bytes 2433032 | tf_op jit(solution)/shard_map/ppermute | solution.py:86
  55.8 0.1 collective-permute-done.14.refs_1_.refs_7_
  56.0 0.0 collective-permute-done.15.refs_2_
  56.0 1.4 %collective-permute-start.16 = (bf16[528,768]{1,0:T(8,128)(2,1)}, bf16[528,768]{1,0:T(8,128)(2,1)}, u32[]{:S(2)}, u32[]{:S(2)}) collective-permute-start(bf16[528,768]{1,0:T(8,128)(2,1)} %collective-permute-done.15.refs_2_), channel_id=1, source_target_pairs={{0,2},{1,67},{2,64},{3,1},{4,6},{5,71},{6,68},{7,5},{8,10},{9,75},... | collective-permute-start | bytes 2433032 | tf_op jit(solution)/shard_map/ppermute | solution.py:86
  57.4 1.7 %collective-permute-start.13 = (bf16[528,768]{1,0:T(8,128)(2,1)}, bf16[528,768]{1,0:T(8,128)(2,1)}, u32[]{:S(2)}, u32[]{:S(2)}) collective-permute-start(bf16[528,768]{1,0:T(8,128)(2,1)} %collective-permute-done.12.refs_0_.refs_6_), channel_id=1, source_target_pairs={{0,4},{1,49},{2,6},{3,51},{4,8},{5,53},{6,10},{7,55},{8,12},{9,57}... | collective-permute-start | bytes 2433032 | tf_op jit(solution)/shard_map/ppermute | solution.py:86
  59.0 0.0 collective-permute-done.18.refs_16_.refs_13_
  59.0 11.2 %meet_20.1.refs_16_ = f32[17,512]{1,0:T(8,128)} custom-call(bf16[528,768]{1,0:T(8,128)(2,1)} %collective-permute-done.12.refs_0_.refs_6_, bf16[528,768]{1,0:T(8,128)(2,1)} %collective-permute-done.14.refs_1_.refs_7_, bf16[528,768]{1,0:T(8,128)(2,1)} %collective-permute-done.15.refs_2_, bf16[528,768]{1,0:T(8,128)(2,1)} %get-tuple-element.19.refs_0_.refs_3_, ...), custom_call_target="tpu_custom_call" | custom-call | flops 8053063680 | bytes 13787136 | tf_op jit(solution)/shard_map/meet_20/pallas_call | solution.py:281
  70.2 0.0 collective-permute-done.17.refs_2_
  70.2 0.0 collective-permute-done.16.refs_1_
  70.3 0.0 collective-permute-done.13.refs_0_
  70.3 12.6 %meet_22.1 = f32[128,1,512]{2,1,0:T(1,128)} custom-call(bf16[528,768]{1,0:T(8,128)(2,1)} %collective-permute-done.13.refs_0_, bf16[528,768]{1,0:T(8,128)(2,1)} %collective-permute-done.16.refs_1_, bf16[528,768]{1,0:T(8,128)(2,1)} %collective-permute-done.17.refs_2_, bf16[528,768]{1,0:T(8,128)(2,1)} %collective-permute-done.refs_1_.refs_4_.refs_3_, ...), custom_call_target="tpu_custom_call" | custom-call | flops 8858370048 | bytes 11354112 | tf_op jit(solution)/shard_map/meet_22/pallas_call | solution.py:281
  82.9 18.9 %all_to_all.5.arrived_ref = f32[128,1,512]{2,1,0:T(1,128)} all-to-all(f32[128,1,512]{2,1,0:T(1,128)} %meet_22.1), channel_id=1, replica_groups=mesh['group'=8,'row'=16] {'group','row'}, dimensions={0} | all-to-all | bytes 524288 | tf_op jit(solution)/shard_map/all_to_all | solution.py:354
  101.8 1.9 %finish.1 = f32[1,512]{1,0:T(1,128)} custom-call(f32[128,1,512]{2,1,0:T(1,128)} %all_to_all.5.arrived_ref, s32[1,512]{1,0:T(1,128)} %get-tuple-element.32.target_ref), custom_call_target="tpu_custom_call" | custom-call | tf_op jit(solution)/shard_map/finish/pallas_call | solution.py:317
Async XLA Ops:
  2.9 13.1 %collective-permute-start = (bf16[528,768]{1,0:T(8,128)(2,1)}, bf16[528,768]{1,0:T(8,128)(2,1)}, u32[]{:S(2)}, u32[]{:S(2)}) collective-permute-start(bf16[528,768]{1,0:T(8,128)(2,1)} %get-tuple-element.19.refs_0_.refs_3_), channel_id=1, source_target_pairs={{0,2},{1,67},{2,64},{3,1},{4,6},{5,71},{6,68},{7,5},{8,10},{9,75},... | collective-permute-start | bytes 2433032 | tf_op jit(solution)/shard_map/ppermute | solution.py:86
  6.4 12.8 %collective-permute-start.1 = (bf16[528,768]{1,0:T(8,128)(2,1)}, bf16[528,768]{1,0:T(8,128)(2,1)}, u32[]{:S(2)}, u32[]{:S(2)}) collective-permute-start(bf16[528,768]{1,0:T(8,128)(2,1)} %get-tuple-element.19.refs_0_.refs_3_), channel_id=1, source_target_pairs={{0,12},{1,17},{2,14},{3,19},{4,0},{5,21},{6,2},{7,23},{8,4},{9,25}... | collective-permute-start | bytes 2433032 | tf_op jit(solution)/shard_map/ppermute | solution.py:86
  7.6 12.4 %collective-permute-start.2 = (bf16[528,768]{1,0:T(8,128)(2,1)}, bf16[528,768]{1,0:T(8,128)(2,1)S(1)}, u32[]{:S(2)}, u32[]{:S(2)}) collective-permute-start(bf16[528,768]{1,0:T(8,128)(2,1)} %get-tuple-element.19.refs_0_.refs_3_), channel_id=1, source_target_pairs={{0,4},{1,49},{2,6},{3,51},{4,8},{5,53},{6,10},{7,55},{8,12},{9,57}... | collective-permute-start | bytes 2433032 | tf_op jit(solution)/shard_map/ppermute | solution.py:86
  9.1 16.8 %collective-permute-start.3 = (bf16[528,768]{1,0:T(8,128)(2,1)}, bf16[528,768]{1,0:T(8,128)(2,1)}, u32[]{:S(2)}, u32[]{:S(2)}) collective-permute-start(bf16[528,768]{1,0:T(8,128)(2,1)} %get-tuple-element.19.refs_0_.refs_3_), channel_id=1, source_target_pairs={{0,1},{1,0},{2,3},{3,2},{4,5},{5,4},{6,7},{7,6},{8,9},{9,8},{10,11... | collective-permute-start | bytes 2433032 | tf_op jit(solution)/shard_map/ppermute | solution.py:90
  16.0 9.9 %collective-permute-start.4 = (bf16[528,768]{1,0:T(8,128)(2,1)}, bf16[528,768]{1,0:T(8,128)(2,1)}, u32[]{:S(2)}, u32[]{:S(2)}) collective-permute-start(bf16[528,768]{1,0:T(8,128)(2,1)} %collective-permute-done.refs_1_.refs_4_.refs_3_), channel_id=1, source_target_pairs={{0,1},{1,0},{2,3},{3,2},{4,5},{5,4},{6,7},{7,6},{8,9},{9,8},{10,11... | collective-permute-start | bytes 2433032 | tf_op jit(solution)/shard_map/ppermute | solution.py:90
  19.3 8.1 %collective-permute-start.5 = (bf16[528,768]{1,0:T(8,128)(2,1)}, bf16[528,768]{1,0:T(8,128)(2,1)}, u32[]{:S(2)}, u32[]{:S(2)}) collective-permute-start(bf16[528,768]{1,0:T(8,128)(2,1)} %collective-permute-done.1.refs_2_.refs_5_.refs_4_), channel_id=1, source_target_pairs={{0,1},{1,0},{2,3},{3,2},{4,5},{5,4},{6,7},{7,6},{8,9},{9,8},{10,11... | collective-permute-start | bytes 2433032 | tf_op jit(solution)/shard_map/ppermute | solution.py:90
  20.1 0.9 copy-start
  21.0 6.4 %collective-permute-start.6 = (bf16[528,768]{1,0:T(8,128)(2,1)S(1)}, bf16[528,768]{1,0:T(8,128)(2,1)}, u32[]{:S(2)}, u32[]{:S(2)}) collective-permute-start(bf16[528,768]{1,0:T(8,128)(2,1)S(1)} %collective-permute-done.2.refs_3_.refs_6_), channel_id=1, source_target_pairs={{0,1},{1,0},{2,3},{3,2},{4,5},{5,4},{6,7},{7,6},{8,9},{9,8},{10,11... | collective-permute-start | bytes 2433032 | tf_op jit(solution)/shard_map/ppermute | solution.py:90
  24.6 12.9 %collective-permute-start.7 = (bf16[528,768]{1,0:T(8,128)(2,1)}, bf16[528,768]{1,0:T(8,128)(2,1)}, u32[]{:S(2)}, u32[]{:S(2)}) collective-permute-start(bf16[528,768]{1,0:T(8,128)(2,1)} %get-tuple-element.19.refs_0_.refs_3_), channel_id=1, source_target_pairs={{0,66},{1,3},{2,0},{3,65},{4,70},{5,7},{6,4},{7,69},{8,74},{9,11},... | collective-permute-start | bytes 2433032 | tf_op jit(solution)/shard_map/ppermute | solution.py:86
  25.9 11.7 %collective-permute-start.8 = (bf16[528,768]{1,0:T(8,128)(2,1)}, bf16[528,768]{1,0:T(8,128)(2,1)}, u32[]{:S(2)}, u32[]{:S(2)}) collective-permute-start(bf16[528,768]{1,0:T(8,128)(2,1)} %collective-permute-done.1.refs_2_.refs_5_.refs_4_), channel_id=1, source_target_pairs={{0,16},{1,13},{2,18},{3,15},{4,20},{5,1},{6,22},{7,3},{8,24},{9,5}... | collective-permute-start | bytes 2433032 | tf_op jit(solution)/shard_map/ppermute | solution.py:86
  25.9 13.0 %collective-permute-start.9 = (bf16[528,768]{1,0:T(8,128)(2,1)}, bf16[528,768]{1,0:T(8,128)(2,1)}, u32[]{:S(2)}, u32[]{:S(2)}) collective-permute-start(bf16[528,768]{1,0:T(8,128)(2,1)} %collective-permute-done.refs_1_.refs_4_.refs_3_), channel_id=1, source_target_pairs={{0,48},{1,5},{2,50},{3,7},{4,52},{5,9},{6,54},{7,11},{8,56},{9,13}... | collective-permute-start | bytes 2433032 | tf_op jit(solution)/shard_map/ppermute | solution.py:86
  38.9 4.5 %collective-permute-start.11 = (bf16[528,768]{1,0:T(8,128)(2,1)}, bf16[528,768]{1,0:T(8,128)(2,1)}, u32[]{:S(2)}, u32[]{:S(2)}) collective-permute-start(bf16[528,768]{1,0:T(8,128)(2,1)} %collective-permute-done.9.refs_2_.refs_9_.refs_5_), channel_id=1, source_target_pairs={{0,1},{1,0},{2,3},{3,2},{4,5},{5,4},{6,7},{7,6},{8,9},{9,8},{10,11... | collective-permute-start | bytes 2433032 | tf_op jit(solution)/shard_map/ppermute | solution.py:90
  40.3 3.4 %collective-permute-start.10 = (bf16[528,768]{1,0:T(8,128)(2,1)}, bf16[528,768]{1,0:T(8,128)(2,1)}, u32[]{:S(2)}, u32[]{:S(2)}) collective-permute-start(bf16[528,768]{1,0:T(8,128)(2,1)} %collective-permute-done.7.refs_0_.refs_7_), channel_id=1, source_target_pairs={{0,1},{1,0},{2,3},{3,2},{4,5},{5,4},{6,7},{7,6},{8,9},{9,8},{10,11... | collective-permute-start | bytes 2433032 | tf_op jit(solution)/shard_map/ppermute | solution.py:90
  40.3 13.4 %collective-permute-start.12 = (bf16[528,768]{1,0:T(8,128)(2,1)}, bf16[528,768]{1,0:T(8,128)(2,1)}, u32[]{:S(2)}, u32[]{:S(2)}) collective-permute-start(bf16[528,768]{1,0:T(8,128)(2,1)} %collective-permute-done.7.refs_0_.refs_7_), channel_id=1, source_target_pairs={{0,4},{1,49},{2,6},{3,51},{4,8},{5,53},{6,10},{7,55},{8,12},{9,57}... | collective-permute-start | bytes 2433032 | tf_op jit(solution)/shard_map/ppermute | solution.py:86
  43.0 12.9 %collective-permute-start.14 = (bf16[528,768]{1,0:T(8,128)(2,1)}, bf16[528,768]{1,0:T(8,128)(2,1)}, u32[]{:S(2)}, u32[]{:S(2)}) collective-permute-start(bf16[528,768]{1,0:T(8,128)(2,1)} %collective-permute-done.1.refs_2_.refs_5_.refs_4_), channel_id=1, source_target_pairs={{0,66},{1,3},{2,0},{3,65},{4,70},{5,7},{6,4},{7,69},{8,74},{9,11},... | collective-permute-start | bytes 2433032 | tf_op jit(solution)/shard_map/ppermute | solution.py:86
  43.1 12.9 %collective-permute-start.15 = (bf16[528,768]{1,0:T(8,128)(2,1)}, bf16[528,768]{1,0:T(8,128)(2,1)}, u32[]{:S(2)}, u32[]{:S(2)}) collective-permute-start(bf16[528,768]{1,0:T(8,128)(2,1)} %collective-permute-done.8.refs_1_.refs_8_), channel_id=1, source_target_pairs={{0,16},{1,13},{2,18},{3,15},{4,20},{5,1},{6,22},{7,3},{8,24},{9,5}... | collective-permute-start | bytes 2433032 | tf_op jit(solution)/shard_map/ppermute | solution.py:86
  53.7 5.3 %collective-permute-start.18 = (bf16[528,768]{1,0:T(8,128)(2,1)}, bf16[528,768]{1,0:T(8,128)(2,1)}, u32[]{:S(2)}, u32[]{:S(2)}) collective-permute-start(bf16[528,768]{1,0:T(8,128)(2,1)} %collective-permute-done.12.refs_0_.refs_6_), channel_id=1, source_target_pairs={{0,1},{1,0},{2,3},{3,2},{4,5},{5,4},{6,7},{7,6},{8,9},{9,8},{10,11... | collective-permute-start | bytes 2433032 | tf_op jit(solution)/shard_map/ppermute | solution.py:90
  54.6 15.6 %collective-permute-start.17 = (bf16[528,768]{1,0:T(8,128)(2,1)}, bf16[528,768]{1,0:T(8,128)(2,1)}, u32[]{:S(2)}, u32[]{:S(2)}) collective-permute-start(bf16[528,768]{1,0:T(8,128)(2,1)} %collective-permute-done.8.refs_1_.refs_8_), channel_id=1, source_target_pairs={{0,12},{1,17},{2,14},{3,19},{4,0},{5,21},{6,2},{7,23},{8,4},{9,25}... | collective-permute-start | bytes 2433032 | tf_op jit(solution)/shard_map/ppermute | solution.py:86
  56.0 14.3 %collective-permute-start.16 = (bf16[528,768]{1,0:T(8,128)(2,1)}, bf16[528,768]{1,0:T(8,128)(2,1)}, u32[]{:S(2)}, u32[]{:S(2)}) collective-permute-start(bf16[528,768]{1,0:T(8,128)(2,1)} %collective-permute-done.15.refs_2_), channel_id=1, source_target_pairs={{0,2},{1,67},{2,64},{3,1},{4,6},{5,71},{6,68},{7,5},{8,10},{9,75},... | collective-permute-start | bytes 2433032 | tf_op jit(solution)/shard_map/ppermute | solution.py:86
  57.4 12.9 %collective-permute-start.13 = (bf16[528,768]{1,0:T(8,128)(2,1)}, bf16[528,768]{1,0:T(8,128)(2,1)}, u32[]{:S(2)}, u32[]{:S(2)}) collective-permute-start(bf16[528,768]{1,0:T(8,128)(2,1)} %collective-permute-done.12.refs_0_.refs_6_), channel_id=1, source_target_pairs={{0,4},{1,49},{2,6},{3,51},{4,8},{5,53},{6,10},{7,55},{8,12},{9,57}... | collective-permute-start | bytes 2433032 | tf_op jit(solution)/shard_map/ppermute | solution.py:86

commit v3 on v1

--- a/solution.py
+++ b/solution.py
@@ -103,11 +103,16 @@
 
 def prepare_kernel(embeds_ref, member_ref, block_ref, target_ref):
     member = member_ref[...].astype(jnp.float32)
-    column = jnp.transpose(jnp.broadcast_to(member, (128, RB)))[:, 0:1]
+    cluster = lax.broadcasted_iota(jnp.int32, (16, RB), 0).astype(jnp.float32)
+    hits = cluster == member
+    ones = jnp.where(hits, 1.0, 0.0)
     above = lax.broadcasted_iota(jnp.int32, (RB, RB), 0)
     across = lax.broadcasted_iota(jnp.int32, (RB, RB), 1)
-    before = (column < member) | ((column == member) & (above < across))
-    target = jnp.sum(before.astype(jnp.float32), axis=0, keepdims=True).astype(jnp.int32)
+    earlier = (above < across).astype(jnp.bfloat16)
+    rank = jnp.dot(ones.astype(jnp.bfloat16), earlier, preferred_element_type=jnp.float32)
+    counts = jnp.sum(ones, axis=1, keepdims=True)
+    parts = jnp.where(cluster < member, counts, 0.0) + jnp.where(hits, rank, 0.0)
+    target = jnp.sum(parts, axis=0, keepdims=True).astype(jnp.int32)
     target_ref[...] = target
     values = embeds_ref[...].astype(jnp.float32)
     total = jnp.sum(values * values, axis=1, keepdims=True)
@@ -116,10 +121,16 @@
     block_ref[0:RB, :] = jnp.dot(placer, normed, preferred_element_type=jnp.float32).astype(
         jnp.bfloat16
     )
-    ordered = jnp.sum(jnp.where(above == target, member, 0.0), axis=1, keepdims=True)
-    ordered = jnp.transpose(jnp.broadcast_to(ordered, (RB, 128)))[0:META]
+    upto = lax.broadcasted_iota(jnp.int32, (16, 16), 1) <= lax.broadcasted_iota(
+        jnp.int32, (16, 16), 0
+    )
+    spread = jnp.transpose(jnp.broadcast_to(counts, (16, 16)))
+    ends = jnp.sum(jnp.where(upto, spread, 0.0), axis=1, keepdims=True)
+    places = lax.broadcasted_iota(jnp.int32, (16, RB), 1).astype(jnp.float32)
+    passed = jnp.where(places >= ends, 1.0, 0.0)[0:GROUPS]
+    ordered = jnp.sum(passed, axis=0, keepdims=True)
     block_ref[RB:SENT, :] = jnp.zeros((META, D), jnp.bfloat16)
-    block_ref[RB:SENT, 0:RB] = ordered.astype(jnp.bfloat16)
+    block_ref[RB:SENT, 0:RB] = jnp.broadcast_to(ordered, (META, RB)).astype(jnp.bfloat16)
 
 
 def prepare(embeds, member):
@@ -184,14 +195,14 @@
         meet(i, j, RB - BAND, BAND, HALF, HALF, False)
 
     def far(i, j):
-        late = across[j, 0:1, HALF - 128 : HALF] >= down[i, BAND : BAND + 1, :]
-        early = across[j, 0:1, HALF : HALF + 128] <= down[i, RB - BAND - 1 : RB - BAND, :]
-        return jnp.where(late | early, 1.0, 0.0)
+        below = across[j, 0:1, HALF - 128 : HALF] >= down[i, BAND : BAND + 1, :]
+        above = across[j, 0:1, HALF : HALF + 128] <= down[i, RB - BAND - 1 : RB - BAND, :]
+        return jnp.where(below, 1.0, 0.0), jnp.where(above, 1.0, 0.0)
 
     def visit(first, length):
         pairs_here = [(table[0, first + u], table[1, first + u]) for u in range(length)]
-        flags = functools.reduce(jnp.maximum, [far(i, j) for i, j in pairs_here])
-        flag = jnp.max(flags)
+        flags = [jnp.maximum(*far(i, j)) for i, j in pairs_here]
+        flag = jnp.max(functools.reduce(jnp.maximum, flags))
         for i, j in pairs_here:
             near(i, j)
 
@@ -199,8 +210,16 @@
         def _():
             def rest(p, carry):
                 i, j = table[0, p], table[1, p]
-                meet(i, j, BAND, RB - BAND, 0, HALF, False)
-                meet(i, j, 0, RB - BAND, HALF, HALF, False)
+                below, above = (jnp.max(lanes) for lanes in far(i, j))
+
+                @pl.when(below > 0.0)
+                def _():
+                    meet(i, j, BAND, RB - BAND, 0, HALF, False)
+
+                @pl.when(above > 0.0)
+                def _():
+                    meet(i, j, 0, RB - BAND, HALF, HALF, False)
+
                 return carry
 
             lax.fori_loop(first, first + length, rest, 0)

time: 101 us -> 101 us (level)
  no operation moved by 1% of the time
where the time goes in v3:
time: 101 us; the launch traced here: 100 us
  Pallas kernels  47.1 us (47%)
  starting transfers between devices  24.3 us (24%)
  blocking collectives  17.8 us (18%)
  waiting for transfers between devices  10.9 us (11%)
    pallas_call x4, Pallas kernels, meet(): pl.pallas_call(functools.partial(meet_kernel, total, len(rows), pairs, it...  42.4 us
    all_to_all x1, blocking collectives, on_device(): lax.all_to_all(outgoing, AXES, split_axis=0, concat_axis=0, tiled=True)  17.8 us
    ppermute x12, starting transfers between devices, fetch(): return lax.ppermute(block, AXES, sorted(pairs))  15.8 us
    ppermute x12, waiting for transfers between devices, fetch(): return lax.ppermute(block, AXES, sorted(pairs))  9.71 us
    ppermute x8, starting transfers between devices, flip(): return lax.ppermute(block, AXES, [(i, i ^ 1) for i in range(128)])  8.51 us
    pallas_call x1, Pallas kernels, prepare(): pl.pallas_call(prepare_kernel, out_shape=(jax.ShapeDtypeStruct((SENT, D),...  2.84 us
  transfers between devices with their start and end apart: 20, of which 5 were waited for; matrix products, arithmetic and copies ran while one was open for 0% of the time, Pallas kernels for 33%

profile of v3, /device:TPU:1, one launch (start us, length us, event | category | flops | bytes accessed | tf_op | source)
XLA Modules:
  0.0 100.2 jit_solution(12340884961257185828)
XLA Ops:
  0.0 2.8 %prepare.1 = (bf16[528,768]{1,0:T(8,128)(2,1)}, s32[1,512]{1,0:T(1,128)}) custom-call(bf16[512,768]{1,0:T(8,128)(2,1)} %embeds_ref.1, s32[1,512]{1,0:T(1,128)} %bitcast.2), custom_call_target="tpu_custom_call" | custom-call | tf_op jit(solution)/shard_map/prepare/pallas_call | solution.py:137
  2.8 2.1 %collective-permute-start = (bf16[528,768]{1,0:T(8,128)(2,1)}, bf16[528,768]{1,0:T(8,128)(2,1)}, u32[]{:S(2)}, u32[]{:S(2)}) collective-permute-start(bf16[528,768]{1,0:T(8,128)(2,1)} %get-tuple-element.19.refs_0_.refs_3_), channel_id=1, source_target_pairs={{0,4},{1,3},{2,6},{3,65},{4,8},{5,7},{6,10},{7,69},{8,12},{9,11},{... | collective-permute-start | bytes 2433032 | tf_op jit(solution)/shard_map/ppermute | solution.py:82
  5.0 1.2 %collective-permute-start.1 = (bf16[528,768]{1,0:T(8,128)(2,1)}, bf16[528,768]{1,0:T(8,128)(2,1)}, u32[]{:S(2)}, u32[]{:S(2)}) collective-permute-start(bf16[528,768]{1,0:T(8,128)(2,1)} %get-tuple-element.19.refs_0_.refs_3_), channel_id=1, source_target_pairs={{0,48},{1,17},{2,50},{3,19},{4,52},{5,21},{6,54},{7,23},{8,56},{9,... | collective-permute-start | bytes 2433032 | tf_op jit(solution)/shard_map/ppermute | solution.py:82
  6.2 1.4 %collective-permute-start.2 = (bf16[528,768]{1,0:T(8,128)(2,1)}, bf16[528,768]{1,0:T(8,128)(2,1)}, u32[]{:S(2)}, u32[]{:S(2)}) collective-permute-start(bf16[528,768]{1,0:T(8,128)(2,1)} %get-tuple-element.19.refs_0_.refs_3_), channel_id=1, source_target_pairs={{0,12},{1,67},{2,14},{3,1},{4,0},{5,71},{6,2},{7,5},{8,4},{9,75},{... | collective-permute-start | bytes 2433032 | tf_op jit(solution)/shard_map/ppermute | solution.py:82
  7.6 3.5 %collective-permute-start.3 = (bf16[528,768]{1,0:T(8,128)(2,1)}, bf16[528,768]{1,0:T(8,128)(2,1)}, u32[]{:S(2)}, u32[]{:S(2)}) collective-permute-start(bf16[528,768]{1,0:T(8,128)(2,1)} %get-tuple-element.19.refs_0_.refs_3_), channel_id=1, source_target_pairs={{0,1},{1,0},{2,3},{3,2},{4,5},{5,4},{6,7},{7,6},{8,9},{9,8},{10,11... | collective-permute-start | bytes 2433032 | tf_op jit(solution)/shard_map/ppermute | solution.py:86
  11.1 5.5 %collective-permute-done.refs_1_.refs_4_ = bf16[528,768]{1,0:T(8,128)(2,1)} collective-permute-done((bf16[528,768]{1,0:T(8,128)(2,1)}, bf16[528,768]{1,0:T(8,128)(2,1)}, u32[]{:S(2)}, u32[]{:S(2)}) %collective-permute-start) | collective-permute-done | bytes 811040 | tf_op jit(solution)/shard_map/ppermute | solution.py:82
  16.6 2.3 %collective-permute-start.4 = (bf16[528,768]{1,0:T(8,128)(2,1)}, bf16[528,768]{1,0:T(8,128)(2,1)}, u32[]{:S(2)}, u32[]{:S(2)}) collective-permute-start(bf16[528,768]{1,0:T(8,128)(2,1)} %collective-permute-done.refs_1_.refs_4_), channel_id=1, source_target_pairs={{0,1},{1,0},{2,3},{3,2},{4,5},{5,4},{6,7},{7,6},{8,9},{9,8},{10,11... | collective-permute-start | bytes 2433032 | tf_op jit(solution)/shard_map/ppermute | solution.py:86
  18.9 0.0 collective-permute-done.1.refs_2_.refs_5_.refs_3_
  18.9 2.7 %collective-permute-start.5 = (bf16[528,768]{1,0:T(8,128)(2,1)}, bf16[528,768]{1,0:T(8,128)(2,1)}, u32[]{:S(2)}, u32[]{:S(2)}) collective-permute-start(bf16[528,768]{1,0:T(8,128)(2,1)} %collective-permute-done.1.refs_2_.refs_5_.refs_3_), channel_id=1, source_target_pairs={{0,66},{1,13},{2,0},{3,15},{4,70},{5,1},{6,4},{7,3},{8,74},{9,5},{... | collective-permute-start | bytes 2433032 | tf_op jit(solution)/shard_map/ppermute | solution.py:82
  21.6 1.5 %collective-permute-start.6 = (bf16[528,768]{1,0:T(8,128)(2,1)}, bf16[528,768]{1,0:T(8,128)(2,1)}, u32[]{:S(2)}, u32[]{:S(2)}) collective-permute-start(bf16[528,768]{1,0:T(8,128)(2,1)} %collective-permute-done.refs_1_.refs_4_), channel_id=1, source_target_pairs={{0,16},{1,49},{2,18},{3,51},{4,20},{5,53},{6,22},{7,55},{8,24},{9,... | collective-permute-start | bytes 2433032 | tf_op jit(solution)/shard_map/ppermute | solution.py:82
  23.1 0.0 collective-permute-done.2.refs_3_.refs_6_
  23.1 0.0 collective-permute-start.9
  23.1 0.0 collective-permute-done.3.refs_4_.refs_7_.refs_10_.refs_6_
  23.1 0.4 collective-permute-start.10
  23.5 0.0 collective-permute-done.4.refs_5_.refs_8_.refs_11_.refs_7_
  23.5 0.2 collective-permute-start.11
  23.7 8.1 %meet_12.2.refs_11_ = f32[6,512]{1,0:T(8,128)} custom-call(bf16[528,768]{1,0:T(8,128)(2,1)} %get-tuple-element.19.refs_0_.refs_3_, bf16[528,768]{1,0:T(8,128)(2,1)} %collective-permute-done.refs_1_.refs_4_, bf16[528,768]{1,0:T(8,128)(2,1)} %collective-permute-done.1.refs_2_.refs_5_.refs_3_, bf16[528,768]{1,0:T(8,128)(2,1)} %collective-permute-done.2.refs_3_.refs_6_, ...), custom_call_target="tpu_custom_call" | custom-call | flops 4831838208 | bytes 4866048 | tf_op jit(solution)/shard_map/meet_12/pallas_call | solution.py:285
  31.9 0.0 collective-permute-done.5.refs_0_.refs_7_
  31.9 1.5 %collective-permute-done.6.refs_1_.refs_8_ = bf16[528,768]{1,0:T(8,128)(2,1)} collective-permute-done((bf16[528,768]{1,0:T(8,128)(2,1)}, bf16[528,768]{1,0:T(8,128)(2,1)}, u32[]{:S(2)}, u32[]{:S(2)}) %collective-permute-start.6) | collective-permute-done | bytes 811040 | tf_op jit(solution)/shard_map/ppermute | solution.py:82
  33.3 2.7 %collective-permute-done.9.refs_2_.refs_9_ = bf16[528,768]{1,0:T(8,128)(2,1)} collective-permute-done((bf16[528,768]{1,0:T(8,128)(2,1)}, bf16[528,768]{1,0:T(8,128)(2,1)}, u32[]{:S(2)}, u32[]{:S(2)}) %collective-permute-start.9) | collective-permute-done | bytes 811040 | tf_op jit(solution)/shard_map/ppermute | solution.py:82
  36.1 1.2 %collective-permute-start.14 = (bf16[528,768]{1,0:T(8,128)(2,1)}, bf16[528,768]{1,0:T(8,128)(2,1)}, u32[]{:S(2)}, u32[]{:S(2)}) collective-permute-start(bf16[528,768]{1,0:T(8,128)(2,1)} %collective-permute-done.9.refs_2_.refs_9_), channel_id=1, source_target_pairs={{0,1},{1,0},{2,3},{3,2},{4,5},{5,4},{6,7},{7,6},{8,9},{9,8},{10,11... | collective-permute-start | bytes 2433032 | tf_op jit(solution)/shard_map/ppermute | solution.py:86
  37.2 0.0 collective-permute-start.13
  37.2 0.5 collective-permute-start.12
  37.7 0.0 collective-permute-done.10.refs_9_.refs_12_
  37.7 1.2 %collective-permute-start.15 = (bf16[528,768]{1,0:T(8,128)(2,1)}, bf16[528,768]{1,0:T(8,128)(2,1)}, u32[]{:S(2)}, u32[]{:S(2)}) collective-permute-start(bf16[528,768]{1,0:T(8,128)(2,1)} %collective-permute-done.9.refs_2_.refs_9_), channel_id=1, source_target_pairs={{0,48},{1,17},{2,50},{3,19},{4,52},{5,21},{6,54},{7,23},{8,56},{9,... | collective-permute-start | bytes 2433032 | tf_op jit(solution)/shard_map/ppermute | solution.py:82
  38.9 0.0 collective-permute-done.11.refs_10_.refs_13_.refs_8_
  38.9 0.0 collective-permute-start.17
  39.0 0.6 collective-permute-done.14.refs_13_.refs_16_.refs_9_
  39.5 1.7 %collective-permute-start.18 = (bf16[528,768]{1,0:T(8,128)(2,1)}, bf16[528,768]{1,0:T(8,128)(2,1)}, u32[]{:S(2)}, u32[]{:S(2)}) collective-permute-start(bf16[528,768]{1,0:T(8,128)(2,1)} %collective-permute-done.5.refs_0_.refs_7_), channel_id=1, source_target_pairs={{0,66},{1,13},{2,0},{3,15},{4,70},{5,1},{6,4},{7,3},{8,74},{9,5},{... | collective-permute-start | bytes 2433032 | tf_op jit(solution)/shard_map/ppermute | solution.py:82
  41.3 0.0 collective-permute-done.13.refs_12_.refs_15_
  41.3 0.6 collective-permute-done.12.refs_11_.refs_14_
  41.8 11.7 %meet_23.1.refs_12_ = f32[14,512]{1,0:T(8,128)} custom-call(bf16[528,768]{1,0:T(8,128)(2,1)} %collective-permute-done.5.refs_0_.refs_7_, bf16[528,768]{1,0:T(8,128)(2,1)} %collective-permute-done.6.refs_1_.refs_8_, bf16[528,768]{1,0:T(8,128)(2,1)} %collective-permute-done.9.refs_2_.refs_9_, bf16[528,768]{1,0:T(8,128)(2,1)} %get-tuple-element.19.refs_0_.refs_3_, ...), custom_call_target="tpu_custom_call" | custom-call | flops 9261023232 | bytes 11354112 | tf_op jit(solution)/shard_map/meet_23/pallas_call | solution.py:285
  53.5 0.0 collective-permute-done.15.refs_0_
  53.5 0.5 collective-permute-start.19
  54.0 1.6 %collective-permute-start.7 = (bf16[528,768]{1,0:T(8,128)(2,1)}, bf16[528,768]{1,0:T(8,128)(2,1)}, u32[]{:S(2)}, u32[]{:S(2)}) collective-permute-start(bf16[528,768]{1,0:T(8,128)(2,1)} %collective-permute-done.6.refs_1_.refs_8_), channel_id=1, source_target_pairs={{0,4},{1,3},{2,6},{3,65},{4,8},{5,7},{6,10},{7,69},{8,12},{9,11},{... | collective-permute-start | bytes 2433032 | tf_op jit(solution)/shard_map/ppermute | solution.py:82
  55.6 1.1 %collective-permute-start.8 = (bf16[528,768]{1,0:T(8,128)(2,1)}, bf16[528,768]{1,0:T(8,128)(2,1)}, u32[]{:S(2)}, u32[]{:S(2)}) collective-permute-start(bf16[528,768]{1,0:T(8,128)(2,1)} %collective-permute-done.6.refs_1_.refs_8_), channel_id=1, source_target_pairs={{0,12},{1,67},{2,14},{3,1},{4,0},{5,71},{6,2},{7,5},{8,4},{9,75},{... | collective-permute-start | bytes 2433032 | tf_op jit(solution)/shard_map/ppermute | solution.py:82
  56.6 0.0 collective-permute-done.17.refs_1_.refs_4_
  56.7 1.2 %collective-permute-start.16 = (bf16[528,768]{1,0:T(8,128)(2,1)}, bf16[528,768]{1,0:T(8,128)(2,1)}, u32[]{:S(2)}, u32[]{:S(2)}) collective-permute-start(bf16[528,768]{1,0:T(8,128)(2,1)} %collective-permute-done.15.refs_0_), channel_id=1, source_target_pairs={{0,48},{1,17},{2,50},{3,19},{4,52},{5,21},{6,54},{7,23},{8,56},{9,... | collective-permute-start | bytes 2433032 | tf_op jit(solution)/shard_map/ppermute | solution.py:82
  57.9 0.0 collective-permute-done.18.refs_2_.refs_5_
  57.9 0.0 collective-permute-done.19.refs_17_.refs_10_
  57.9 13.6 %meet_28.1.refs_13_ = f32[18,512]{1,0:T(8,128)} custom-call(bf16[528,768]{1,0:T(8,128)(2,1)} %collective-permute-done.15.refs_0_, bf16[528,768]{1,0:T(8,128)(2,1)} %collective-permute-done.17.refs_1_.refs_4_, bf16[528,768]{1,0:T(8,128)(2,1)} %collective-permute-done.18.refs_2_.refs_5_, bf16[528,768]{1,0:T(8,128)(2,1)} %get-tuple-element.19.refs_0_.refs_3_, ...), custom_call_target="tpu_custom_call" | custom-call | flops 11274289152 | bytes 14598144 | tf_op jit(solution)/shard_map/meet_28/pallas_call | solution.py:285
  71.5 0.0 collective-permute-done.7.refs_0_
  71.5 0.0 collective-permute-done.8.refs_1_
  71.5 0.0 collective-permute-done.16.refs_2_
  71.5 8.9 %meet_12.3 = f32[128,1,512]{2,1,0:T(1,128)} custom-call(bf16[528,768]{1,0:T(8,128)(2,1)} %collective-permute-done.7.refs_0_, bf16[528,768]{1,0:T(8,128)(2,1)} %collective-permute-done.8.refs_1_, bf16[528,768]{1,0:T(8,128)(2,1)} %collective-permute-done.16.refs_2_, bf16[528,768]{1,0:T(8,128)(2,1)} %collective-permute-done.1.refs_2_.refs_5_.refs_3_, ...), custom_call_target="tpu_custom_call" | custom-call | flops 4831838208 | bytes 8921088 | tf_op jit(solution)/shard_map/meet_12/pallas_call | solution.py:285
  80.5 17.8 %all_to_all.5.arrived_ref = f32[128,1,512]{2,1,0:T(1,128)} all-to-all(f32[128,1,512]{2,1,0:T(1,128)} %meet_12.3), channel_id=1, replica_groups=mesh['group'=8,'row'=16] {'group','row'}, dimensions={0} | all-to-all | bytes 524288 | tf_op jit(solution)/shard_map/all_to_all | solution.py:358
  98.3 1.9 %finish.1 = f32[1,512]{1,0:T(1,128)} custom-call(f32[128,1,512]{2,1,0:T(1,128)} %all_to_all.5.arrived_ref, s32[1,512]{1,0:T(1,128)} %get-tuple-element.32.target_ref), custom_call_target="tpu_custom_call" | custom-call | tf_op jit(solution)/shard_map/finish/pallas_call | solution.py:321
Async XLA Ops:
  2.8 13.8 %collective-permute-start = (bf16[528,768]{1,0:T(8,128)(2,1)}, bf16[528,768]{1,0:T(8,128)(2,1)}, u32[]{:S(2)}, u32[]{:S(2)}) collective-permute-start(bf16[528,768]{1,0:T(8,128)(2,1)} %get-tuple-element.19.refs_0_.refs_3_), channel_id=1, source_target_pairs={{0,4},{1,3},{2,6},{3,65},{4,8},{5,7},{6,10},{7,69},{8,12},{9,11},{... | collective-permute-start | bytes 2433032 | tf_op jit(solution)/shard_map/ppermute | solution.py:82
  5.0 14.0 %collective-permute-start.1 = (bf16[528,768]{1,0:T(8,128)(2,1)}, bf16[528,768]{1,0:T(8,128)(2,1)}, u32[]{:S(2)}, u32[]{:S(2)}) collective-permute-start(bf16[528,768]{1,0:T(8,128)(2,1)} %get-tuple-element.19.refs_0_.refs_3_), channel_id=1, source_target_pairs={{0,48},{1,17},{2,50},{3,19},{4,52},{5,21},{6,54},{7,23},{8,56},{9,... | collective-permute-start | bytes 2433032 | tf_op jit(solution)/shard_map/ppermute | solution.py:82
  6.2 17.0 %collective-permute-start.2 = (bf16[528,768]{1,0:T(8,128)(2,1)}, bf16[528,768]{1,0:T(8,128)(2,1)}, u32[]{:S(2)}, u32[]{:S(2)}) collective-permute-start(bf16[528,768]{1,0:T(8,128)(2,1)} %get-tuple-element.19.refs_0_.refs_3_), channel_id=1, source_target_pairs={{0,12},{1,67},{2,14},{3,1},{4,0},{5,71},{6,2},{7,5},{8,4},{9,75},{... | collective-permute-start | bytes 2433032 | tf_op jit(solution)/shard_map/ppermute | solution.py:82
  7.6 15.5 %collective-permute-start.3 = (bf16[528,768]{1,0:T(8,128)(2,1)}, bf16[528,768]{1,0:T(8,128)(2,1)}, u32[]{:S(2)}, u32[]{:S(2)}) collective-permute-start(bf16[528,768]{1,0:T(8,128)(2,1)} %get-tuple-element.19.refs_0_.refs_3_), channel_id=1, source_target_pairs={{0,1},{1,0},{2,3},{3,2},{4,5},{5,4},{6,7},{7,6},{8,9},{9,8},{10,11... | collective-permute-start | bytes 2433032 | tf_op jit(solution)/shard_map/ppermute | solution.py:86
  16.6 6.9 %collective-permute-start.4 = (bf16[528,768]{1,0:T(8,128)(2,1)}, bf16[528,768]{1,0:T(8,128)(2,1)}, u32[]{:S(2)}, u32[]{:S(2)}) collective-permute-start(bf16[528,768]{1,0:T(8,128)(2,1)} %collective-permute-done.refs_1_.refs_4_), channel_id=1, source_target_pairs={{0,1},{1,0},{2,3},{3,2},{4,5},{5,4},{6,7},{7,6},{8,9},{9,8},{10,11... | collective-permute-start | bytes 2433032 | tf_op jit(solution)/shard_map/ppermute | solution.py:86
  18.9 13.0 %collective-permute-start.5 = (bf16[528,768]{1,0:T(8,128)(2,1)}, bf16[528,768]{1,0:T(8,128)(2,1)}, u32[]{:S(2)}, u32[]{:S(2)}) collective-permute-start(bf16[528,768]{1,0:T(8,128)(2,1)} %collective-permute-done.1.refs_2_.refs_5_.refs_3_), channel_id=1, source_target_pairs={{0,66},{1,13},{2,0},{3,15},{4,70},{5,1},{6,4},{7,3},{8,74},{9,5},{... | collective-permute-start | bytes 2433032 | tf_op jit(solution)/shard_map/ppermute | solution.py:82
  21.6 11.7 %collective-permute-start.6 = (bf16[528,768]{1,0:T(8,128)(2,1)}, bf16[528,768]{1,0:T(8,128)(2,1)}, u32[]{:S(2)}, u32[]{:S(2)}) collective-permute-start(bf16[528,768]{1,0:T(8,128)(2,1)} %collective-permute-done.refs_1_.refs_4_), channel_id=1, source_target_pairs={{0,16},{1,49},{2,18},{3,51},{4,20},{5,53},{6,22},{7,55},{8,24},{9,... | collective-permute-start | bytes 2433032 | tf_op jit(solution)/shard_map/ppermute | solution.py:82
  23.1 12.9 %collective-permute-start.9 = (bf16[528,768]{1,0:T(8,128)(2,1)}, bf16[528,768]{1,0:T(8,128)(2,1)}, u32[]{:S(2)}, u32[]{:S(2)}) collective-permute-start(bf16[528,768]{1,0:T(8,128)(2,1)} %collective-permute-done.2.refs_3_.refs_6_), channel_id=1, source_target_pairs={{0,2},{1,5},{2,64},{3,7},{4,6},{5,9},{6,68},{7,11},{8,10},{9,13},{... | collective-permute-start | bytes 2433032 | tf_op jit(solution)/shard_map/ppermute | solution.py:82
  23.1 14.6 %collective-permute-start.10 = (bf16[528,768]{1,0:T(8,128)(2,1)}, bf16[528,768]{1,0:T(8,128)(2,1)}, u32[]{:S(2)}, u32[]{:S(2)}) collective-permute-start(bf16[528,768]{1,0:T(8,128)(2,1)} %collective-permute-done.1.refs_2_.refs_5_.refs_3_), channel_id=1, source_target_pairs={{0,1},{1,0},{2,3},{3,2},{4,5},{5,4},{6,7},{7,6},{8,9},{9,8},{10,11... | collective-permute-start | bytes 2433032 | tf_op jit(solution)/shard_map/ppermute | solution.py:86
  23.5 15.4 %collective-permute-start.11 = (bf16[528,768]{1,0:T(8,128)(2,1)}, bf16[528,768]{1,0:T(8,128)(2,1)}, u32[]{:S(2)}, u32[]{:S(2)}) collective-permute-start(bf16[528,768]{1,0:T(8,128)(2,1)} %collective-permute-done.2.refs_3_.refs_6_), channel_id=1, source_target_pairs={{0,1},{1,0},{2,3},{3,2},{4,5},{5,4},{6,7},{7,6},{8,9},{9,8},{10,11... | collective-permute-start | bytes 2433032 | tf_op jit(solution)/shard_map/ppermute | solution.py:86
  36.1 3.4 %collective-permute-start.14 = (bf16[528,768]{1,0:T(8,128)(2,1)}, bf16[528,768]{1,0:T(8,128)(2,1)}, u32[]{:S(2)}, u32[]{:S(2)}) collective-permute-start(bf16[528,768]{1,0:T(8,128)(2,1)} %collective-permute-done.9.refs_2_.refs_9_), channel_id=1, source_target_pairs={{0,1},{1,0},{2,3},{3,2},{4,5},{5,4},{6,7},{7,6},{8,9},{9,8},{10,11... | collective-permute-start | bytes 2433032 | tf_op jit(solution)/shard_map/ppermute | solution.py:86
  37.2 4.0 %collective-permute-start.13 = (bf16[528,768]{1,0:T(8,128)(2,1)}, bf16[528,768]{1,0:T(8,128)(2,1)}, u32[]{:S(2)}, u32[]{:S(2)}) collective-permute-start(bf16[528,768]{1,0:T(8,128)(2,1)} %collective-permute-done.6.refs_1_.refs_8_), channel_id=1, source_target_pairs={{0,1},{1,0},{2,3},{3,2},{4,5},{5,4},{6,7},{7,6},{8,9},{9,8},{10,11... | collective-permute-start | bytes 2433032 | tf_op jit(solution)/shard_map/ppermute | solution.py:86
  37.2 4.6 %collective-permute-start.12 = (bf16[528,768]{1,0:T(8,128)(2,1)}, bf16[528,768]{1,0:T(8,128)(2,1)}, u32[]{:S(2)}, u32[]{:S(2)}) collective-permute-start(bf16[528,768]{1,0:T(8,128)(2,1)} %collective-permute-done.5.refs_0_.refs_7_), channel_id=1, source_target_pairs={{0,1},{1,0},{2,3},{3,2},{4,5},{5,4},{6,7},{7,6},{8,9},{9,8},{10,11... | collective-permute-start | bytes 2433032 | tf_op jit(solution)/shard_map/ppermute | solution.py:86
  37.7 15.8 %collective-permute-start.15 = (bf16[528,768]{1,0:T(8,128)(2,1)}, bf16[528,768]{1,0:T(8,128)(2,1)}, u32[]{:S(2)}, u32[]{:S(2)}) collective-permute-start(bf16[528,768]{1,0:T(8,128)(2,1)} %collective-permute-done.9.refs_2_.refs_9_), channel_id=1, source_target_pairs={{0,48},{1,17},{2,50},{3,19},{4,52},{5,21},{6,54},{7,23},{8,56},{9,... | collective-permute-start | bytes 2433032 | tf_op jit(solution)/shard_map/ppermute | solution.py:82
  38.9 17.7 %collective-permute-start.17 = (bf16[528,768]{1,0:T(8,128)(2,1)}, bf16[528,768]{1,0:T(8,128)(2,1)}, u32[]{:S(2)}, u32[]{:S(2)}) collective-permute-start(bf16[528,768]{1,0:T(8,128)(2,1)} %collective-permute-done.5.refs_0_.refs_7_), channel_id=1, source_target_pairs={{0,4},{1,3},{2,6},{3,65},{4,8},{5,7},{6,10},{7,69},{8,12},{9,11},{... | collective-permute-start | bytes 2433032 | tf_op jit(solution)/shard_map/ppermute | solution.py:82
  39.5 18.4 %collective-permute-start.18 = (bf16[528,768]{1,0:T(8,128)(2,1)}, bf16[528,768]{1,0:T(8,128)(2,1)}, u32[]{:S(2)}, u32[]{:S(2)}) collective-permute-start(bf16[528,768]{1,0:T(8,128)(2,1)} %collective-permute-done.5.refs_0_.refs_7_), channel_id=1, source_target_pairs={{0,66},{1,13},{2,0},{3,15},{4,70},{5,1},{6,4},{7,3},{8,74},{9,5},{... | collective-permute-start | bytes 2433032 | tf_op jit(solution)/shard_map/ppermute | solution.py:82
  53.5 4.3 %collective-permute-start.19 = (bf16[528,768]{1,0:T(8,128)(2,1)}, bf16[528,768]{1,0:T(8,128)(2,1)}, u32[]{:S(2)}, u32[]{:S(2)}) collective-permute-start(bf16[528,768]{1,0:T(8,128)(2,1)} %collective-permute-done.15.refs_0_), channel_id=1, source_target_pairs={{0,1},{1,0},{2,3},{3,2},{4,5},{5,4},{6,7},{7,6},{8,9},{9,8},{10,11... | collective-permute-start | bytes 2433032 | tf_op jit(solution)/shard_map/ppermute | solution.py:86
  54.0 17.5 %collective-permute-start.7 = (bf16[528,768]{1,0:T(8,128)(2,1)}, bf16[528,768]{1,0:T(8,128)(2,1)}, u32[]{:S(2)}, u32[]{:S(2)}) collective-permute-start(bf16[528,768]{1,0:T(8,128)(2,1)} %collective-permute-done.6.refs_1_.refs_8_), channel_id=1, source_target_pairs={{0,4},{1,3},{2,6},{3,65},{4,8},{5,7},{6,10},{7,69},{8,12},{9,11},{... | collective-permute-start | bytes 2433032 | tf_op jit(solution)/shard_map/ppermute | solution.py:82
  55.6 15.9 %collective-permute-start.8 = (bf16[528,768]{1,0:T(8,128)(2,1)}, bf16[528,768]{1,0:T(8,128)(2,1)}, u32[]{:S(2)}, u32[]{:S(2)}) collective-permute-start(bf16[528,768]{1,0:T(8,128)(2,1)} %collective-permute-done.6.refs_1_.refs_8_), channel_id=1, source_target_pairs={{0,12},{1,67},{2,14},{3,1},{4,0},{5,71},{6,2},{7,5},{8,4},{9,75},{... | collective-permute-start | bytes 2433032 | tf_op jit(solution)/shard_map/ppermute | solution.py:82
  56.7 14.9 %collective-permute-start.16 = (bf16[528,768]{1,0:T(8,128)(2,1)}, bf16[528,768]{1,0:T(8,128)(2,1)}, u32[]{:S(2)}, u32[]{:S(2)}) collective-permute-start(bf16[528,768]{1,0:T(8,128)(2,1)} %collective-permute-done.15.refs_0_), channel_id=1, source_target_pairs={{0,48},{1,17},{2,50},{3,19},{4,52},{5,21},{6,54},{7,23},{8,56},{9,... | collective-permute-start | bytes 2433032 | tf_op jit(solution)/shard_map/ppermute | solution.py:82

commit v4 on v3

--- a/solution.py
+++ b/solution.py
@@ -87,18 +87,16 @@
 
 
 def home(name, group, row):
-    x, y, z = lax.rem(group, 4), lax.div(group, 4) * 2 + lax.rem(lax.div(row, 2), 2), lax.div(row, 4)
-    core = lax.rem(row, 2)
+    x, y, z, core = group & 3, ((group >> 2) << 1) | ((row >> 1) & 1), row >> 2, row & 1
     table = offsets()
     swap = 1 if name >= OTHER else 0
     at = []
     for axis, here in enumerate((x, y, z)):
         first = table[swap][name % OTHER][axis]
         second = table[1 - swap][name % OTHER][axis]
-        at.append(lax.rem(here + jnp.where(core == 0, first, second), 4))
-    core = 1 - core if swap else core
-    group = lax.div(at[1], 2) * 4 + at[0]
-    return group * 16 + (at[2] * 2 + lax.rem(at[1], 2)) * 2 + core
+        at.append((here + first + core * (second - first)) & 3)
+    group = ((at[1] >> 1) << 2) | at[0]
+    return (group << 4) | (at[2] << 2) | ((at[1] & 1) << 1) | (core ^ swap)
 
 
 def prepare_kernel(embeds_ref, member_ref, block_ref, target_ref):
@@ -160,6 +158,20 @@
     column_best[...] = jnp.full_like(column_best, LOW)
     if lists:
         out_ref[...] = jnp.full_like(out_ref, ABSENT)
+        here = [lax.axis_index(axis) for axis in AXES]
+        homes = {name: home(name, *here) for name in NAMES}
+
+        def found_before(name):
+            found = jnp.full((1, RB), ABSENT, jnp.float32)
+            for ref, names in zip(before, lists[1:]):
+                if name in names:
+                    at = names.index(name)
+                    found = jnp.maximum(found, ref[at : at + 1, :])
+            return found
+
+        for name in NAMES:
+            if name not in lists[0]:
+                out_ref[homes[name]] = found_before(name)
 
     def arrive(k):
         pltpu.make_async_copy(blocks[0], held.at[k], sems.at[k]).wait()
@@ -254,16 +266,8 @@
         for k in range(total):
             out_ref[k : k + 1, :] = found_in(k)
         return
-    here = [lax.axis_index(axis) for axis in AXES]
-    for name in NAMES:
-        found = jnp.full((1, RB), ABSENT, jnp.float32)
-        if name in lists[0]:
-            found = jnp.maximum(found, found_in(lists[0].index(name)))
-        for ref, names in zip(before, lists[1:]):
-            if name in names:
-                at = names.index(name)
-                found = jnp.maximum(found, ref[at : at + 1, :])
-        out_ref[home(name, *here)] = found
+    for k, name in enumerate(lists[0]):
+        out_ref[homes[name]] = jnp.maximum(found_in(k), found_before(name))
 
 
 def meet(held, meeting, lists=(), before=()):

time: 101 us -> 100 us (0.990); the launches traced: 100 us -> 100 us
  no operation moved by 1% of the time
where the time goes in v4:
time: 100 us
  Pallas kernels  47.1 us (47%)
  starting transfers between devices  24.3 us (24%)
  blocking collectives  17.8 us (18%)
  waiting for transfers between devices  10.9 us (11%)
    pallas_call x4, Pallas kernels, meet(): pl.pallas_call(functools.partial(meet_kernel, total, len(rows), pairs, it...  42.4 us
    all_to_all x1, blocking collectives, on_device(): lax.all_to_all(outgoing, AXES, split_axis=0, concat_axis=0, tiled=True)  17.8 us
    ppermute x12, starting transfers between devices, fetch(): return lax.ppermute(block, AXES, sorted(pairs))  15.8 us
    ppermute x12, waiting for transfers between devices, fetch(): return lax.ppermute(block, AXES, sorted(pairs))  9.71 us
    ppermute x8, starting transfers between devices, flip(): return lax.ppermute(block, AXES, [(i, i ^ 1) for i in range(128)])  8.51 us
    pallas_call x1, Pallas kernels, prepare(): pl.pallas_call(prepare_kernel, out_shape=(jax.ShapeDtypeStruct((SENT, D),...  2.84 us
  transfers between devices with their start and end apart: 20, of which 5 were waited for; matrix products, arithmetic and copies ran while one was open for 0% of the time, Pallas kernels for 33%

profile of v4, /device:TPU:1, one launch (start us, length us, event | category | flops | bytes accessed | tf_op | source)
XLA Modules:
  0.0 100.2 jit_solution(7980459098849228494)
XLA Ops:
  0.0 2.8 %prepare.1 = (bf16[528,768]{1,0:T(8,128)(2,1)}, s32[1,512]{1,0:T(1,128)}) custom-call(bf16[512,768]{1,0:T(8,128)(2,1)} %embeds_ref.1, s32[1,512]{1,0:T(1,128)} %bitcast.2), custom_call_target="tpu_custom_call" | custom-call | tf_op jit(solution)/shard_map/prepare/pallas_call | solution.py:135
  2.8 2.1 %collective-permute-start = (bf16[528,768]{1,0:T(8,128)(2,1)}, bf16[528,768]{1,0:T(8,128)(2,1)}, u32[]{:S(2)}, u32[]{:S(2)}) collective-permute-start(bf16[528,768]{1,0:T(8,128)(2,1)} %get-tuple-element.19.refs_0_.refs_3_), channel_id=1, source_target_pairs={{0,4},{1,3},{2,6},{3,65},{4,8},{5,7},{6,10},{7,69},{8,12},{9,11},{... | collective-permute-start | bytes 2433032 | tf_op jit(solution)/shard_map/ppermute | solution.py:82
  5.0 1.2 %collective-permute-start.1 = (bf16[528,768]{1,0:T(8,128)(2,1)}, bf16[528,768]{1,0:T(8,128)(2,1)}, u32[]{:S(2)}, u32[]{:S(2)}) collective-permute-start(bf16[528,768]{1,0:T(8,128)(2,1)} %get-tuple-element.19.refs_0_.refs_3_), channel_id=1, source_target_pairs={{0,48},{1,17},{2,50},{3,19},{4,52},{5,21},{6,54},{7,23},{8,56},{9,... | collective-permute-start | bytes 2433032 | tf_op jit(solution)/shard_map/ppermute | solution.py:82
  6.2 1.4 %collective-permute-start.2 = (bf16[528,768]{1,0:T(8,128)(2,1)}, bf16[528,768]{1,0:T(8,128)(2,1)}, u32[]{:S(2)}, u32[]{:S(2)}) collective-permute-start(bf16[528,768]{1,0:T(8,128)(2,1)} %get-tuple-element.19.refs_0_.refs_3_), channel_id=1, source_target_pairs={{0,12},{1,67},{2,14},{3,1},{4,0},{5,71},{6,2},{7,5},{8,4},{9,75},{... | collective-permute-start | bytes 2433032 | tf_op jit(solution)/shard_map/ppermute | solution.py:82
  7.6 3.5 %collective-permute-start.3 = (bf16[528,768]{1,0:T(8,128)(2,1)}, bf16[528,768]{1,0:T(8,128)(2,1)}, u32[]{:S(2)}, u32[]{:S(2)}) collective-permute-start(bf16[528,768]{1,0:T(8,128)(2,1)} %get-tuple-element.19.refs_0_.refs_3_), channel_id=1, source_target_pairs={{0,1},{1,0},{2,3},{3,2},{4,5},{5,4},{6,7},{7,6},{8,9},{9,8},{10,11... | collective-permute-start | bytes 2433032 | tf_op jit(solution)/shard_map/ppermute | solution.py:86
  11.1 5.5 %collective-permute-done.refs_1_.refs_4_ = bf16[528,768]{1,0:T(8,128)(2,1)} collective-permute-done((bf16[528,768]{1,0:T(8,128)(2,1)}, bf16[528,768]{1,0:T(8,128)(2,1)}, u32[]{:S(2)}, u32[]{:S(2)}) %collective-permute-start) | collective-permute-done | bytes 811040 | tf_op jit(solution)/shard_map/ppermute | solution.py:82
  16.6 2.3 %collective-permute-start.4 = (bf16[528,768]{1,0:T(8,128)(2,1)}, bf16[528,768]{1,0:T(8,128)(2,1)}, u32[]{:S(2)}, u32[]{:S(2)}) collective-permute-start(bf16[528,768]{1,0:T(8,128)(2,1)} %collective-permute-done.refs_1_.refs_4_), channel_id=1, source_target_pairs={{0,1},{1,0},{2,3},{3,2},{4,5},{5,4},{6,7},{7,6},{8,9},{9,8},{10,11... | collective-permute-start | bytes 2433032 | tf_op jit(solution)/shard_map/ppermute | solution.py:86
  18.9 0.0 collective-permute-done.1.refs_2_.refs_5_.refs_3_
  18.9 2.7 %collective-permute-start.5 = (bf16[528,768]{1,0:T(8,128)(2,1)}, bf16[528,768]{1,0:T(8,128)(2,1)}, u32[]{:S(2)}, u32[]{:S(2)}) collective-permute-start(bf16[528,768]{1,0:T(8,128)(2,1)} %collective-permute-done.1.refs_2_.refs_5_.refs_3_), channel_id=1, source_target_pairs={{0,66},{1,13},{2,0},{3,15},{4,70},{5,1},{6,4},{7,3},{8,74},{9,5},{... | collective-permute-start | bytes 2433032 | tf_op jit(solution)/shard_map/ppermute | solution.py:82
  21.6 1.5 %collective-permute-start.6 = (bf16[528,768]{1,0:T(8,128)(2,1)}, bf16[528,768]{1,0:T(8,128)(2,1)}, u32[]{:S(2)}, u32[]{:S(2)}) collective-permute-start(bf16[528,768]{1,0:T(8,128)(2,1)} %collective-permute-done.refs_1_.refs_4_), channel_id=1, source_target_pairs={{0,16},{1,49},{2,18},{3,51},{4,20},{5,53},{6,22},{7,55},{8,24},{9,... | collective-permute-start | bytes 2433032 | tf_op jit(solution)/shard_map/ppermute | solution.py:82
  23.1 0.0 collective-permute-done.2.refs_3_.refs_6_
  23.1 0.0 collective-permute-start.9
  23.1 0.0 collective-permute-done.3.refs_4_.refs_7_.refs_10_.refs_6_
  23.1 0.4 collective-permute-start.10
  23.5 0.0 collective-permute-done.4.refs_5_.refs_8_.refs_11_.refs_7_
  23.5 0.2 collective-permute-start.11
  23.7 8.1 %meet_12.2.refs_11_ = f32[6,512]{1,0:T(8,128)} custom-call(bf16[528,768]{1,0:T(8,128)(2,1)} %get-tuple-element.19.refs_0_.refs_3_, bf16[528,768]{1,0:T(8,128)(2,1)} %collective-permute-done.refs_1_.refs_4_, bf16[528,768]{1,0:T(8,128)(2,1)} %collective-permute-done.1.refs_2_.refs_5_.refs_3_, bf16[528,768]{1,0:T(8,128)(2,1)} %collective-permute-done.2.refs_3_.refs_6_, ...), custom_call_target="tpu_custom_call" | custom-call | flops 4831838208 | bytes 4866048 | tf_op jit(solution)/shard_map/meet_12/pallas_call | solution.py:289
  31.9 0.0 collective-permute-done.5.refs_0_.refs_7_
  31.9 1.5 %collective-permute-done.6.refs_1_.refs_8_ = bf16[528,768]{1,0:T(8,128)(2,1)} collective-permute-done((bf16[528,768]{1,0:T(8,128)(2,1)}, bf16[528,768]{1,0:T(8,128)(2,1)}, u32[]{:S(2)}, u32[]{:S(2)}) %collective-permute-start.6) | collective-permute-done | bytes 811040 | tf_op jit(solution)/shard_map/ppermute | solution.py:82
  33.3 2.7 %collective-permute-done.9.refs_2_.refs_9_ = bf16[528,768]{1,0:T(8,128)(2,1)} collective-permute-done((bf16[528,768]{1,0:T(8,128)(2,1)}, bf16[528,768]{1,0:T(8,128)(2,1)}, u32[]{:S(2)}, u32[]{:S(2)}) %collective-permute-start.9) | collective-permute-done | bytes 811040 | tf_op jit(solution)/shard_map/ppermute | solution.py:82
  36.1 1.2 %collective-permute-start.14 = (bf16[528,768]{1,0:T(8,128)(2,1)}, bf16[528,768]{1,0:T(8,128)(2,1)}, u32[]{:S(2)}, u32[]{:S(2)}) collective-permute-start(bf16[528,768]{1,0:T(8,128)(2,1)} %collective-permute-done.9.refs_2_.refs_9_), channel_id=1, source_target_pairs={{0,1},{1,0},{2,3},{3,2},{4,5},{5,4},{6,7},{7,6},{8,9},{9,8},{10,11... | collective-permute-start | bytes 2433032 | tf_op jit(solution)/shard_map/ppermute | solution.py:86
  37.2 0.0 collective-permute-start.13
  37.2 0.5 collective-permute-start.12
  37.7 0.0 collective-permute-done.10.refs_9_.refs_12_
  37.7 1.2 %collective-permute-start.15 = (bf16[528,768]{1,0:T(8,128)(2,1)}, bf16[528,768]{1,0:T(8,128)(2,1)}, u32[]{:S(2)}, u32[]{:S(2)}) collective-permute-start(bf16[528,768]{1,0:T(8,128)(2,1)} %collective-permute-done.9.refs_2_.refs_9_), channel_id=1, source_target_pairs={{0,48},{1,17},{2,50},{3,19},{4,52},{5,21},{6,54},{7,23},{8,56},{9,... | collective-permute-start | bytes 2433032 | tf_op jit(solution)/shard_map/ppermute | solution.py:82
  38.9 0.0 collective-permute-done.11.refs_10_.refs_13_.refs_8_
  38.9 0.0 collective-permute-start.17
  39.0 0.6 collective-permute-done.14.refs_13_.refs_16_.refs_9_
  39.5 1.7 %collective-permute-start.18 = (bf16[528,768]{1,0:T(8,128)(2,1)}, bf16[528,768]{1,0:T(8,128)(2,1)}, u32[]{:S(2)}, u32[]{:S(2)}) collective-permute-start(bf16[528,768]{1,0:T(8,128)(2,1)} %collective-permute-done.5.refs_0_.refs_7_), channel_id=1, source_target_pairs={{0,66},{1,13},{2,0},{3,15},{4,70},{5,1},{6,4},{7,3},{8,74},{9,5},{... | collective-permute-start | bytes 2433032 | tf_op jit(solution)/shard_map/ppermute | solution.py:82
  41.3 0.0 collective-permute-done.13.refs_12_.refs_15_
  41.3 0.6 collective-permute-done.12.refs_11_.refs_14_
  41.8 11.7 %meet_23.1.refs_12_ = f32[14,512]{1,0:T(8,128)} custom-call(bf16[528,768]{1,0:T(8,128)(2,1)} %collective-permute-done.5.refs_0_.refs_7_, bf16[528,768]{1,0:T(8,128)(2,1)} %collective-permute-done.6.refs_1_.refs_8_, bf16[528,768]{1,0:T(8,128)(2,1)} %collective-permute-done.9.refs_2_.refs_9_, bf16[528,768]{1,0:T(8,128)(2,1)} %get-tuple-element.19.refs_0_.refs_3_, ...), custom_call_target="tpu_custom_call" | custom-call | flops 9261023232 | bytes 11354112 | tf_op jit(solution)/shard_map/meet_23/pallas_call | solution.py:289
  53.5 0.0 collective-permute-done.15.refs_0_
  53.5 0.5 collective-permute-start.19
  54.0 1.6 %collective-permute-start.7 = (bf16[528,768]{1,0:T(8,128)(2,1)}, bf16[528,768]{1,0:T(8,128)(2,1)}, u32[]{:S(2)}, u32[]{:S(2)}) collective-permute-start(bf16[528,768]{1,0:T(8,128)(2,1)} %collective-permute-done.6.refs_1_.refs_8_), channel_id=1, source_target_pairs={{0,4},{1,3},{2,6},{3,65},{4,8},{5,7},{6,10},{7,69},{8,12},{9,11},{... | collective-permute-start | bytes 2433032 | tf_op jit(solution)/shard_map/ppermute | solution.py:82
  55.6 1.1 %collective-permute-start.8 = (bf16[528,768]{1,0:T(8,128)(2,1)}, bf16[528,768]{1,0:T(8,128)(2,1)}, u32[]{:S(2)}, u32[]{:S(2)}) collective-permute-start(bf16[528,768]{1,0:T(8,128)(2,1)} %collective-permute-done.6.refs_1_.refs_8_), channel_id=1, source_target_pairs={{0,12},{1,67},{2,14},{3,1},{4,0},{5,71},{6,2},{7,5},{8,4},{9,75},{... | collective-permute-start | bytes 2433032 | tf_op jit(solution)/shard_map/ppermute | solution.py:82
  56.6 0.0 collective-permute-done.17.refs_1_.refs_4_
  56.7 1.2 %collective-permute-start.16 = (bf16[528,768]{1,0:T(8,128)(2,1)}, bf16[528,768]{1,0:T(8,128)(2,1)}, u32[]{:S(2)}, u32[]{:S(2)}) collective-permute-start(bf16[528,768]{1,0:T(8,128)(2,1)} %collective-permute-done.15.refs_0_), channel_id=1, source_target_pairs={{0,48},{1,17},{2,50},{3,19},{4,52},{5,21},{6,54},{7,23},{8,56},{9,... | collective-permute-start | bytes 2433032 | tf_op jit(solution)/shard_map/ppermute | solution.py:82
  57.9 0.0 collective-permute-done.18.refs_2_.refs_5_
  57.9 0.0 collective-permute-done.19.refs_17_.refs_10_
  57.9 13.6 %meet_28.1.refs_13_ = f32[18,512]{1,0:T(8,128)} custom-call(bf16[528,768]{1,0:T(8,128)(2,1)} %collective-permute-done.15.refs_0_, bf16[528,768]{1,0:T(8,128)(2,1)} %collective-permute-done.17.refs_1_.refs_4_, bf16[528,768]{1,0:T(8,128)(2,1)} %collective-permute-done.18.refs_2_.refs_5_, bf16[528,768]{1,0:T(8,128)(2,1)} %get-tuple-element.19.refs_0_.refs_3_, ...), custom_call_target="tpu_custom_call" | custom-call | flops 11274289152 | bytes 14598144 | tf_op jit(solution)/shard_map/meet_28/pallas_call | solution.py:289
  71.5 0.0 collective-permute-done.7.refs_0_
  71.5 0.0 collective-permute-done.8.refs_1_
  71.5 0.0 collective-permute-done.16.refs_2_
  71.5 9.0 %meet_12.3 = f32[128,1,512]{2,1,0:T(1,128)} custom-call(bf16[528,768]{1,0:T(8,128)(2,1)} %collective-permute-done.7.refs_0_, bf16[528,768]{1,0:T(8,128)(2,1)} %collective-permute-done.8.refs_1_, bf16[528,768]{1,0:T(8,128)(2,1)} %collective-permute-done.16.refs_2_, bf16[528,768]{1,0:T(8,128)(2,1)} %collective-permute-done.1.refs_2_.refs_5_.refs_3_, ...), custom_call_target="tpu_custom_call" | custom-call | flops 4831838208 | bytes 8921088 | tf_op jit(solution)/shard_map/meet_12/pallas_call | solution.py:289
  80.5 17.8 %all_to_all.5.arrived_ref = f32[128,1,512]{2,1,0:T(1,128)} all-to-all(f32[128,1,512]{2,1,0:T(1,128)} %meet_12.3), channel_id=1, replica_groups=mesh['group'=8,'row'=16] {'group','row'}, dimensions={0} | all-to-all | bytes 524288 | tf_op jit(solution)/shard_map/all_to_all | solution.py:362
  98.3 1.9 %finish.1 = f32[1,512]{1,0:T(1,128)} custom-call(f32[128,1,512]{2,1,0:T(1,128)} %all_to_all.5.arrived_ref, s32[1,512]{1,0:T(1,128)} %get-tuple-element.32.target_ref), custom_call_target="tpu_custom_call" | custom-call | tf_op jit(solution)/shard_map/finish/pallas_call | solution.py:325
Async XLA Ops:
  2.8 13.8 %collective-permute-start = (bf16[528,768]{1,0:T(8,128)(2,1)}, bf16[528,768]{1,0:T(8,128)(2,1)}, u32[]{:S(2)}, u32[]{:S(2)}) collective-permute-start(bf16[528,768]{1,0:T(8,128)(2,1)} %get-tuple-element.19.refs_0_.refs_3_), channel_id=1, source_target_pairs={{0,4},{1,3},{2,6},{3,65},{4,8},{5,7},{6,10},{7,69},{8,12},{9,11},{... | collective-permute-start | bytes 2433032 | tf_op jit(solution)/shard_map/ppermute | solution.py:82
  5.0 14.0 %collective-permute-start.1 = (bf16[528,768]{1,0:T(8,128)(2,1)}, bf16[528,768]{1,0:T(8,128)(2,1)}, u32[]{:S(2)}, u32[]{:S(2)}) collective-permute-start(bf16[528,768]{1,0:T(8,128)(2,1)} %get-tuple-element.19.refs_0_.refs_3_), channel_id=1, source_target_pairs={{0,48},{1,17},{2,50},{3,19},{4,52},{5,21},{6,54},{7,23},{8,56},{9,... | collective-permute-start | bytes 2433032 | tf_op jit(solution)/shard_map/ppermute | solution.py:82
  6.2 17.0 %collective-permute-start.2 = (bf16[528,768]{1,0:T(8,128)(2,1)}, bf16[528,768]{1,0:T(8,128)(2,1)}, u32[]{:S(2)}, u32[]{:S(2)}) collective-permute-start(bf16[528,768]{1,0:T(8,128)(2,1)} %get-tuple-element.19.refs_0_.refs_3_), channel_id=1, source_target_pairs={{0,12},{1,67},{2,14},{3,1},{4,0},{5,71},{6,2},{7,5},{8,4},{9,75},{... | collective-permute-start | bytes 2433032 | tf_op jit(solution)/shard_map/ppermute | solution.py:82
  7.6 15.5 %collective-permute-start.3 = (bf16[528,768]{1,0:T(8,128)(2,1)}, bf16[528,768]{1,0:T(8,128)(2,1)}, u32[]{:S(2)}, u32[]{:S(2)}) collective-permute-start(bf16[528,768]{1,0:T(8,128)(2,1)} %get-tuple-element.19.refs_0_.refs_3_), channel_id=1, source_target_pairs={{0,1},{1,0},{2,3},{3,2},{4,5},{5,4},{6,7},{7,6},{8,9},{9,8},{10,11... | collective-permute-start | bytes 2433032 | tf_op jit(solution)/shard_map/ppermute | solution.py:86
  16.6 6.9 %collective-permute-start.4 = (bf16[528,768]{1,0:T(8,128)(2,1)}, bf16[528,768]{1,0:T(8,128)(2,1)}, u32[]{:S(2)}, u32[]{:S(2)}) collective-permute-start(bf16[528,768]{1,0:T(8,128)(2,1)} %collective-permute-done.refs_1_.refs_4_), channel_id=1, source_target_pairs={{0,1},{1,0},{2,3},{3,2},{4,5},{5,4},{6,7},{7,6},{8,9},{9,8},{10,11... | collective-permute-start | bytes 2433032 | tf_op jit(solution)/shard_map/ppermute | solution.py:86
  18.9 13.0 %collective-permute-start.5 = (bf16[528,768]{1,0:T(8,128)(2,1)}, bf16[528,768]{1,0:T(8,128)(2,1)}, u32[]{:S(2)}, u32[]{:S(2)}) collective-permute-start(bf16[528,768]{1,0:T(8,128)(2,1)} %collective-permute-done.1.refs_2_.refs_5_.refs_3_), channel_id=1, source_target_pairs={{0,66},{1,13},{2,0},{3,15},{4,70},{5,1},{6,4},{7,3},{8,74},{9,5},{... | collective-permute-start | bytes 2433032 | tf_op jit(solution)/shard_map/ppermute | solution.py:82
  21.6 11.7 %collective-permute-start.6 = (bf16[528,768]{1,0:T(8,128)(2,1)}, bf16[528,768]{1,0:T(8,128)(2,1)}, u32[]{:S(2)}, u32[]{:S(2)}) collective-permute-start(bf16[528,768]{1,0:T(8,128)(2,1)} %collective-permute-done.refs_1_.refs_4_), channel_id=1, source_target_pairs={{0,16},{1,49},{2,18},{3,51},{4,20},{5,53},{6,22},{7,55},{8,24},{9,... | collective-permute-start | bytes 2433032 | tf_op jit(solution)/shard_map/ppermute | solution.py:82
  23.1 12.9 %collective-permute-start.9 = (bf16[528,768]{1,0:T(8,128)(2,1)}, bf16[528,768]{1,0:T(8,128)(2,1)}, u32[]{:S(2)}, u32[]{:S(2)}) collective-permute-start(bf16[528,768]{1,0:T(8,128)(2,1)} %collective-permute-done.2.refs_3_.refs_6_), channel_id=1, source_target_pairs={{0,2},{1,5},{2,64},{3,7},{4,6},{5,9},{6,68},{7,11},{8,10},{9,13},{... | collective-permute-start | bytes 2433032 | tf_op jit(solution)/shard_map/ppermute | solution.py:82
  23.1 14.6 %collective-permute-start.10 = (bf16[528,768]{1,0:T(8,128)(2,1)}, bf16[528,768]{1,0:T(8,128)(2,1)}, u32[]{:S(2)}, u32[]{:S(2)}) collective-permute-start(bf16[528,768]{1,0:T(8,128)(2,1)} %collective-permute-done.1.refs_2_.refs_5_.refs_3_), channel_id=1, source_target_pairs={{0,1},{1,0},{2,3},{3,2},{4,5},{5,4},{6,7},{7,6},{8,9},{9,8},{10,11... | collective-permute-start | bytes 2433032 | tf_op jit(solution)/shard_map/ppermute | solution.py:86
  23.5 15.4 %collective-permute-start.11 = (bf16[528,768]{1,0:T(8,128)(2,1)}, bf16[528,768]{1,0:T(8,128)(2,1)}, u32[]{:S(2)}, u32[]{:S(2)}) collective-permute-start(bf16[528,768]{1,0:T(8,128)(2,1)} %collective-permute-done.2.refs_3_.refs_6_), channel_id=1, source_target_pairs={{0,1},{1,0},{2,3},{3,2},{4,5},{5,4},{6,7},{7,6},{8,9},{9,8},{10,11... | collective-permute-start | bytes 2433032 | tf_op jit(solution)/shard_map/ppermute | solution.py:86
  36.1 3.4 %collective-permute-start.14 = (bf16[528,768]{1,0:T(8,128)(2,1)}, bf16[528,768]{1,0:T(8,128)(2,1)}, u32[]{:S(2)}, u32[]{:S(2)}) collective-permute-start(bf16[528,768]{1,0:T(8,128)(2,1)} %collective-permute-done.9.refs_2_.refs_9_), channel_id=1, source_target_pairs={{0,1},{1,0},{2,3},{3,2},{4,5},{5,4},{6,7},{7,6},{8,9},{9,8},{10,11... | collective-permute-start | bytes 2433032 | tf_op jit(solution)/shard_map/ppermute | solution.py:86
  37.2 4.0 %collective-permute-start.13 = (bf16[528,768]{1,0:T(8,128)(2,1)}, bf16[528,768]{1,0:T(8,128)(2,1)}, u32[]{:S(2)}, u32[]{:S(2)}) collective-permute-start(bf16[528,768]{1,0:T(8,128)(2,1)} %collective-permute-done.6.refs_1_.refs_8_), channel_id=1, source_target_pairs={{0,1},{1,0},{2,3},{3,2},{4,5},{5,4},{6,7},{7,6},{8,9},{9,8},{10,11... | collective-permute-start | bytes 2433032 | tf_op jit(solution)/shard_map/ppermute | solution.py:86
  37.2 4.6 %collective-permute-start.12 = (bf16[528,768]{1,0:T(8,128)(2,1)}, bf16[528,768]{1,0:T(8,128)(2,1)}, u32[]{:S(2)}, u32[]{:S(2)}) collective-permute-start(bf16[528,768]{1,0:T(8,128)(2,1)} %collective-permute-done.5.refs_0_.refs_7_), channel_id=1, source_target_pairs={{0,1},{1,0},{2,3},{3,2},{4,5},{5,4},{6,7},{7,6},{8,9},{9,8},{10,11... | collective-permute-start | bytes 2433032 | tf_op jit(solution)/shard_map/ppermute | solution.py:86
  37.7 15.8 %collective-permute-start.15 = (bf16[528,768]{1,0:T(8,128)(2,1)}, bf16[528,768]{1,0:T(8,128)(2,1)}, u32[]{:S(2)}, u32[]{:S(2)}) collective-permute-start(bf16[528,768]{1,0:T(8,128)(2,1)} %collective-permute-done.9.refs_2_.refs_9_), channel_id=1, source_target_pairs={{0,48},{1,17},{2,50},{3,19},{4,52},{5,21},{6,54},{7,23},{8,56},{9,... | collective-permute-start | bytes 2433032 | tf_op jit(solution)/shard_map/ppermute | solution.py:82
  38.9 17.7 %collective-permute-start.17 = (bf16[528,768]{1,0:T(8,128)(2,1)}, bf16[528,768]{1,0:T(8,128)(2,1)}, u32[]{:S(2)}, u32[]{:S(2)}) collective-permute-start(bf16[528,768]{1,0:T(8,128)(2,1)} %collective-permute-done.5.refs_0_.refs_7_), channel_id=1, source_target_pairs={{0,4},{1,3},{2,6},{3,65},{4,8},{5,7},{6,10},{7,69},{8,12},{9,11},{... | collective-permute-start | bytes 2433032 | tf_op jit(solution)/shard_map/ppermute | solution.py:82
  39.5 18.4 %collective-permute-start.18 = (bf16[528,768]{1,0:T(8,128)(2,1)}, bf16[528,768]{1,0:T(8,128)(2,1)}, u32[]{:S(2)}, u32[]{:S(2)}) collective-permute-start(bf16[528,768]{1,0:T(8,128)(2,1)} %collective-permute-done.5.refs_0_.refs_7_), channel_id=1, source_target_pairs={{0,66},{1,13},{2,0},{3,15},{4,70},{5,1},{6,4},{7,3},{8,74},{9,5},{... | collective-permute-start | bytes 2433032 | tf_op jit(solution)/shard_map/ppermute | solution.py:82
  53.5 4.3 %collective-permute-start.19 = (bf16[528,768]{1,0:T(8,128)(2,1)}, bf16[528,768]{1,0:T(8,128)(2,1)}, u32[]{:S(2)}, u32[]{:S(2)}) collective-permute-start(bf16[528,768]{1,0:T(8,128)(2,1)} %collective-permute-done.15.refs_0_), channel_id=1, source_target_pairs={{0,1},{1,0},{2,3},{3,2},{4,5},{5,4},{6,7},{7,6},{8,9},{9,8},{10,11... | collective-permute-start | bytes 2433032 | tf_op jit(solution)/shard_map/ppermute | solution.py:86
  54.0 17.5 %collective-permute-start.7 = (bf16[528,768]{1,0:T(8,128)(2,1)}, bf16[528,768]{1,0:T(8,128)(2,1)}, u32[]{:S(2)}, u32[]{:S(2)}) collective-permute-start(bf16[528,768]{1,0:T(8,128)(2,1)} %collective-permute-done.6.refs_1_.refs_8_), channel_id=1, source_target_pairs={{0,4},{1,3},{2,6},{3,65},{4,8},{5,7},{6,10},{7,69},{8,12},{9,11},{... | collective-permute-start | bytes 2433032 | tf_op jit(solution)/shard_map/ppermute | solution.py:82
  55.6 15.9 %collective-permute-start.8 = (bf16[528,768]{1,0:T(8,128)(2,1)}, bf16[528,768]{1,0:T(8,128)(2,1)}, u32[]{:S(2)}, u32[]{:S(2)}) collective-permute-start(bf16[528,768]{1,0:T(8,128)(2,1)} %collective-permute-done.6.refs_1_.refs_8_), channel_id=1, source_target_pairs={{0,12},{1,67},{2,14},{3,1},{4,0},{5,71},{6,2},{7,5},{8,4},{9,75},{... | collective-permute-start | bytes 2433032 | tf_op jit(solution)/shard_map/ppermute | solution.py:82
  56.7 14.9 %collective-permute-start.16 = (bf16[528,768]{1,0:T(8,128)(2,1)}, bf16[528,768]{1,0:T(8,128)(2,1)}, u32[]{:S(2)}, u32[]{:S(2)}) collective-permute-start(bf16[528,768]{1,0:T(8,128)(2,1)} %collective-permute-done.15.refs_0_), channel_id=1, source_target_pairs={{0,48},{1,17},{2,50},{3,19},{4,52},{5,21},{6,54},{7,23},{8,56},{9,... | collective-permute-start | bytes 2433032 | tf_op jit(solution)/shard_map/ppermute | solution.py:82

commit v5 on v4

--- a/solution.py
+++ b/solution.py
@@ -146,7 +146,7 @@
     blocks, refs = refs[:total], refs[total:]
     if lists:
         before, refs = refs[: len(lists) - 1], refs[len(lists) - 1 :]
-    out_ref, held, across, down, row_best, column_best, table, waits, sems = refs
+    out_ref, held, across, down, row_best, column_best, table, waits, sems, *refs = refs
     for k in range(total):
         pltpu.make_async_copy(blocks[k], held.at[k], sems.at[k]).start()
     for p, (i, j) in enumerate(pairs):
@@ -157,6 +157,13 @@
     row_best[...] = jnp.full_like(row_best, LOW)
     column_best[...] = jnp.full_like(column_best, LOW)
     if lists:
+        copies = [
+            pltpu.make_async_copy(ref, found, refs[-1].at[at])
+            for at, (ref, found) in enumerate(zip(before, refs[:-1]))
+        ]
+        before = refs[:-1]
+        for copy in copies:
+            copy.start()
         out_ref[...] = jnp.full_like(out_ref, ABSENT)
         here = [lax.axis_index(axis) for axis in AXES]
         homes = {name: home(name, *here) for name in NAMES}
@@ -169,6 +176,8 @@
                     found = jnp.maximum(found, ref[at : at + 1, :])
             return found
 
+        for copy in copies:
+            copy.wait()
         for name in NAMES:
             if name not in lists[0]:
                 out_ref[homes[name]] = found_before(name)
@@ -285,7 +294,7 @@
     shape = (128, 1, RB) if lists else (total, RB)
     in_specs = [pl.BlockSpec(memory_space=pltpu.HBM)] * total
     if lists:
-        in_specs += [pl.BlockSpec(memory_space=pltpu.VMEM)] * len(before)
+        in_specs += [pl.BlockSpec(memory_space=pltpu.HBM)] * len(before)
     return pl.pallas_call(
         functools.partial(meet_kernel, total, len(rows), pairs, itself, lists, waits),
         out_shape=jax.ShapeDtypeStruct(shape, jnp.float32),
@@ -299,7 +308,9 @@
             pltpu.SMEM((2, len(pairs)), jnp.int32),
             pltpu.SMEM((len(pairs),), jnp.int32),
             pltpu.SemaphoreType.DMA((total,)),
-        ],
+        ]
+        + [pltpu.VMEM(ref.shape, jnp.float32) for ref in before]
+        + ([pltpu.SemaphoreType.DMA((len(before),))] if lists else []),
         compiler_params=pltpu.CompilerParams(vmem_limit_bytes=66_400_000),
         cost_estimate=pl.CostEstimate(
             flops=2 * RB * RB * D * len(pairs),

time: 100 us -> 102 us (1.020); the launches traced: 100 us -> 101 us
  no operation moved by 1% of the time
where the time goes in v5:
time: 102 us; the launch traced here: 101 us
  Pallas kernels  47.8 us (47%)
  starting transfers between devices  24.3 us (24%)
  blocking collectives  17.8 us (17%)
  waiting for transfers between devices  10.9 us (11%)
    pallas_call x4, Pallas kernels, meet(): pl.pallas_call(functools.partial(meet_kernel, total, len(rows), pairs, it...  43.1 us
    all_to_all x1, blocking collectives, on_device(): lax.all_to_all(outgoing, AXES, split_axis=0, concat_axis=0, tiled=True)  17.8 us
    ppermute x12, starting transfers between devices, fetch(): return lax.ppermute(block, AXES, sorted(pairs))  15.8 us
    ppermute x12, waiting for transfers between devices, fetch(): return lax.ppermute(block, AXES, sorted(pairs))  9.71 us
    ppermute x8, starting transfers between devices, flip(): return lax.ppermute(block, AXES, [(i, i ^ 1) for i in range(128)])  8.51 us
    pallas_call x1, Pallas kernels, prepare(): pl.pallas_call(prepare_kernel, out_shape=(jax.ShapeDtypeStruct((SENT, D),...  2.84 us
  transfers between devices with their start and end apart: 20, of which 5 were waited for; matrix products, arithmetic and copies ran while one was open for 0% of the time, Pallas kernels for 33%

profile of v5, /device:TPU:1, one launch (start us, length us, event | category | flops | bytes accessed | tf_op | source)
XLA Modules:
  0.0 100.9 jit_solution(2460912335112442229)
XLA Ops:
  0.0 2.8 %prepare.1 = (bf16[528,768]{1,0:T(8,128)(2,1)}, s32[1,512]{1,0:T(1,128)}) custom-call(bf16[512,768]{1,0:T(8,128)(2,1)} %embeds_ref.1, s32[1,512]{1,0:T(1,128)} %bitcast.2), custom_call_target="tpu_custom_call" | custom-call | tf_op jit(solution)/shard_map/prepare/pallas_call | solution.py:135
  2.8 2.1 %collective-permute-start = (bf16[528,768]{1,0:T(8,128)(2,1)}, bf16[528,768]{1,0:T(8,128)(2,1)}, u32[]{:S(2)}, u32[]{:S(2)}) collective-permute-start(bf16[528,768]{1,0:T(8,128)(2,1)} %get-tuple-element.19.refs_0_.refs_3_), channel_id=1, source_target_pairs={{0,4},{1,3},{2,6},{3,65},{4,8},{5,7},{6,10},{7,69},{8,12},{9,11},{... | collective-permute-start | bytes 2433032 | tf_op jit(solution)/shard_map/ppermute | solution.py:82
  5.0 1.2 %collective-permute-start.1 = (bf16[528,768]{1,0:T(8,128)(2,1)}, bf16[528,768]{1,0:T(8,128)(2,1)}, u32[]{:S(2)}, u32[]{:S(2)}) collective-permute-start(bf16[528,768]{1,0:T(8,128)(2,1)} %get-tuple-element.19.refs_0_.refs_3_), channel_id=1, source_target_pairs={{0,48},{1,17},{2,50},{3,19},{4,52},{5,21},{6,54},{7,23},{8,56},{9,... | collective-permute-start | bytes 2433032 | tf_op jit(solution)/shard_map/ppermute | solution.py:82
  6.2 1.4 %collective-permute-start.2 = (bf16[528,768]{1,0:T(8,128)(2,1)}, bf16[528,768]{1,0:T(8,128)(2,1)}, u32[]{:S(2)}, u32[]{:S(2)}) collective-permute-start(bf16[528,768]{1,0:T(8,128)(2,1)} %get-tuple-element.19.refs_0_.refs_3_), channel_id=1, source_target_pairs={{0,12},{1,67},{2,14},{3,1},{4,0},{5,71},{6,2},{7,5},{8,4},{9,75},{... | collective-permute-start | bytes 2433032 | tf_op jit(solution)/shard_map/ppermute | solution.py:82
  7.6 3.5 %collective-permute-start.3 = (bf16[528,768]{1,0:T(8,128)(2,1)}, bf16[528,768]{1,0:T(8,128)(2,1)}, u32[]{:S(2)}, u32[]{:S(2)}) collective-permute-start(bf16[528,768]{1,0:T(8,128)(2,1)} %get-tuple-element.19.refs_0_.refs_3_), channel_id=1, source_target_pairs={{0,1},{1,0},{2,3},{3,2},{4,5},{5,4},{6,7},{7,6},{8,9},{9,8},{10,11... | collective-permute-start | bytes 2433032 | tf_op jit(solution)/shard_map/ppermute | solution.py:86
  11.1 5.5 %collective-permute-done.refs_1_.refs_4_ = bf16[528,768]{1,0:T(8,128)(2,1)} collective-permute-done((bf16[528,768]{1,0:T(8,128)(2,1)}, bf16[528,768]{1,0:T(8,128)(2,1)}, u32[]{:S(2)}, u32[]{:S(2)}) %collective-permute-start) | collective-permute-done | bytes 811040 | tf_op jit(solution)/shard_map/ppermute | solution.py:82
  16.6 2.3 %collective-permute-start.4 = (bf16[528,768]{1,0:T(8,128)(2,1)}, bf16[528,768]{1,0:T(8,128)(2,1)}, u32[]{:S(2)}, u32[]{:S(2)}) collective-permute-start(bf16[528,768]{1,0:T(8,128)(2,1)} %collective-permute-done.refs_1_.refs_4_), channel_id=1, source_target_pairs={{0,1},{1,0},{2,3},{3,2},{4,5},{5,4},{6,7},{7,6},{8,9},{9,8},{10,11... | collective-permute-start | bytes 2433032 | tf_op jit(solution)/shard_map/ppermute | solution.py:86
  18.9 0.0 collective-permute-done.1.refs_2_.refs_5_.refs_3_
  18.9 2.7 %collective-permute-start.5 = (bf16[528,768]{1,0:T(8,128)(2,1)}, bf16[528,768]{1,0:T(8,128)(2,1)}, u32[]{:S(2)}, u32[]{:S(2)}) collective-permute-start(bf16[528,768]{1,0:T(8,128)(2,1)} %collective-permute-done.1.refs_2_.refs_5_.refs_3_), channel_id=1, source_target_pairs={{0,66},{1,13},{2,0},{3,15},{4,70},{5,1},{6,4},{7,3},{8,74},{9,5},{... | collective-permute-start | bytes 2433032 | tf_op jit(solution)/shard_map/ppermute | solution.py:82
  21.6 1.5 %collective-permute-start.6 = (bf16[528,768]{1,0:T(8,128)(2,1)}, bf16[528,768]{1,0:T(8,128)(2,1)}, u32[]{:S(2)}, u32[]{:S(2)}) collective-permute-start(bf16[528,768]{1,0:T(8,128)(2,1)} %collective-permute-done.refs_1_.refs_4_), channel_id=1, source_target_pairs={{0,16},{1,49},{2,18},{3,51},{4,20},{5,53},{6,22},{7,55},{8,24},{9,... | collective-permute-start | bytes 2433032 | tf_op jit(solution)/shard_map/ppermute | solution.py:82
  23.1 0.0 collective-permute-done.2.refs_3_.refs_6_
  23.1 0.0 collective-permute-start.9
  23.1 0.0 collective-permute-done.3.refs_4_.refs_7_.refs_10_.refs_6_
  23.1 0.4 collective-permute-start.10
  23.5 0.0 collective-permute-done.4.refs_5_.refs_8_.refs_11_.refs_7_
  23.5 0.2 collective-permute-start.11
  23.7 8.1 %meet_12.2.refs_11_ = f32[6,512]{1,0:T(8,128)} custom-call(bf16[528,768]{1,0:T(8,128)(2,1)} %get-tuple-element.19.refs_0_.refs_3_, bf16[528,768]{1,0:T(8,128)(2,1)} %collective-permute-done.refs_1_.refs_4_, bf16[528,768]{1,0:T(8,128)(2,1)} %collective-permute-done.1.refs_2_.refs_5_.refs_3_, bf16[528,768]{1,0:T(8,128)(2,1)} %collective-permute-done.2.refs_3_.refs_6_, ...), custom_call_target="tpu_custom_call" | custom-call | flops 4831838208 | bytes 4866048 | tf_op jit(solution)/shard_map/meet_12/pallas_call | solution.py:298
  31.9 0.0 collective-permute-done.5.refs_0_.refs_7_
  31.9 1.5 %collective-permute-done.6.refs_1_.refs_8_ = bf16[528,768]{1,0:T(8,128)(2,1)} collective-permute-done((bf16[528,768]{1,0:T(8,128)(2,1)}, bf16[528,768]{1,0:T(8,128)(2,1)}, u32[]{:S(2)}, u32[]{:S(2)}) %collective-permute-start.6) | collective-permute-done | bytes 811040 | tf_op jit(solution)/shard_map/ppermute | solution.py:82
  33.3 2.7 %collective-permute-done.9.refs_2_.refs_9_ = bf16[528,768]{1,0:T(8,128)(2,1)} collective-permute-done((bf16[528,768]{1,0:T(8,128)(2,1)}, bf16[528,768]{1,0:T(8,128)(2,1)}, u32[]{:S(2)}, u32[]{:S(2)}) %collective-permute-start.9) | collective-permute-done | bytes 811040 | tf_op jit(solution)/shard_map/ppermute | solution.py:82
  36.1 1.2 %collective-permute-start.14 = (bf16[528,768]{1,0:T(8,128)(2,1)}, bf16[528,768]{1,0:T(8,128)(2,1)}, u32[]{:S(2)}, u32[]{:S(2)}) collective-permute-start(bf16[528,768]{1,0:T(8,128)(2,1)} %collective-permute-done.9.refs_2_.refs_9_), channel_id=1, source_target_pairs={{0,1},{1,0},{2,3},{3,2},{4,5},{5,4},{6,7},{7,6},{8,9},{9,8},{10,11... | collective-permute-start | bytes 2433032 | tf_op jit(solution)/shard_map/ppermute | solution.py:86
  37.2 0.0 collective-permute-start.13
  37.2 0.5 collective-permute-start.12
  37.7 0.0 collective-permute-done.10.refs_9_.refs_12_
  37.7 1.2 %collective-permute-start.15 = (bf16[528,768]{1,0:T(8,128)(2,1)}, bf16[528,768]{1,0:T(8,128)(2,1)}, u32[]{:S(2)}, u32[]{:S(2)}) collective-permute-start(bf16[528,768]{1,0:T(8,128)(2,1)} %collective-permute-done.9.refs_2_.refs_9_), channel_id=1, source_target_pairs={{0,48},{1,17},{2,50},{3,19},{4,52},{5,21},{6,54},{7,23},{8,56},{9,... | collective-permute-start | bytes 2433032 | tf_op jit(solution)/shard_map/ppermute | solution.py:82
  38.9 0.0 collective-permute-done.11.refs_10_.refs_13_.refs_8_
  38.9 0.0 collective-permute-start.17
  39.0 0.6 collective-permute-done.14.refs_13_.refs_16_.refs_9_
  39.5 1.7 %collective-permute-start.18 = (bf16[528,768]{1,0:T(8,128)(2,1)}, bf16[528,768]{1,0:T(8,128)(2,1)}, u32[]{:S(2)}, u32[]{:S(2)}) collective-permute-start(bf16[528,768]{1,0:T(8,128)(2,1)} %collective-permute-done.5.refs_0_.refs_7_), channel_id=1, source_target_pairs={{0,66},{1,13},{2,0},{3,15},{4,70},{5,1},{6,4},{7,3},{8,74},{9,5},{... | collective-permute-start | bytes 2433032 | tf_op jit(solution)/shard_map/ppermute | solution.py:82
  41.3 0.0 collective-permute-done.13.refs_12_.refs_15_
  41.3 0.6 collective-permute-done.12.refs_11_.refs_14_
  41.8 11.7 %meet_23.1.refs_12_ = f32[14,512]{1,0:T(8,128)} custom-call(bf16[528,768]{1,0:T(8,128)(2,1)} %collective-permute-done.5.refs_0_.refs_7_, bf16[528,768]{1,0:T(8,128)(2,1)} %collective-permute-done.6.refs_1_.refs_8_, bf16[528,768]{1,0:T(8,128)(2,1)} %collective-permute-done.9.refs_2_.refs_9_, bf16[528,768]{1,0:T(8,128)(2,1)} %get-tuple-element.19.refs_0_.refs_3_, ...), custom_call_target="tpu_custom_call" | custom-call | flops 9261023232 | bytes 11354112 | tf_op jit(solution)/shard_map/meet_23/pallas_call | solution.py:298
  53.5 0.0 collective-permute-done.15.refs_0_
  53.5 0.5 collective-permute-start.19
  54.0 1.6 %collective-permute-start.7 = (bf16[528,768]{1,0:T(8,128)(2,1)}, bf16[528,768]{1,0:T(8,128)(2,1)}, u32[]{:S(2)}, u32[]{:S(2)}) collective-permute-start(bf16[528,768]{1,0:T(8,128)(2,1)} %collective-permute-done.6.refs_1_.refs_8_), channel_id=1, source_target_pairs={{0,4},{1,3},{2,6},{3,65},{4,8},{5,7},{6,10},{7,69},{8,12},{9,11},{... | collective-permute-start | bytes 2433032 | tf_op jit(solution)/shard_map/ppermute | solution.py:82
  55.6 1.1 %collective-permute-start.8 = (bf16[528,768]{1,0:T(8,128)(2,1)}, bf16[528,768]{1,0:T(8,128)(2,1)}, u32[]{:S(2)}, u32[]{:S(2)}) collective-permute-start(bf16[528,768]{1,0:T(8,128)(2,1)} %collective-permute-done.6.refs_1_.refs_8_), channel_id=1, source_target_pairs={{0,12},{1,67},{2,14},{3,1},{4,0},{5,71},{6,2},{7,5},{8,4},{9,75},{... | collective-permute-start | bytes 2433032 | tf_op jit(solution)/shard_map/ppermute | solution.py:82
  56.6 0.0 collective-permute-done.17.refs_1_.refs_4_
  56.7 1.2 %collective-permute-start.16 = (bf16[528,768]{1,0:T(8,128)(2,1)}, bf16[528,768]{1,0:T(8,128)(2,1)}, u32[]{:S(2)}, u32[]{:S(2)}) collective-permute-start(bf16[528,768]{1,0:T(8,128)(2,1)} %collective-permute-done.15.refs_0_), channel_id=1, source_target_pairs={{0,48},{1,17},{2,50},{3,19},{4,52},{5,21},{6,54},{7,23},{8,56},{9,... | collective-permute-start | bytes 2433032 | tf_op jit(solution)/shard_map/ppermute | solution.py:82
  57.9 0.0 collective-permute-done.18.refs_2_.refs_5_
  57.9 0.0 collective-permute-done.19.refs_17_.refs_10_
  57.9 13.6 %meet_28.1.refs_13_ = f32[18,512]{1,0:T(8,128)} custom-call(bf16[528,768]{1,0:T(8,128)(2,1)} %collective-permute-done.15.refs_0_, bf16[528,768]{1,0:T(8,128)(2,1)} %collective-permute-done.17.refs_1_.refs_4_, bf16[528,768]{1,0:T(8,128)(2,1)} %collective-permute-done.18.refs_2_.refs_5_, bf16[528,768]{1,0:T(8,128)(2,1)} %get-tuple-element.19.refs_0_.refs_3_, ...), custom_call_target="tpu_custom_call" | custom-call | flops 11274289152 | bytes 14598144 | tf_op jit(solution)/shard_map/meet_28/pallas_call | solution.py:298
  71.5 0.0 collective-permute-done.7.refs_0_
  71.5 0.0 collective-permute-done.8.refs_1_
  71.5 0.0 collective-permute-done.16.refs_2_
  71.5 9.7 %meet_12.3 = f32[128,1,512]{2,1,0:T(1,128)} custom-call(bf16[528,768]{1,0:T(8,128)(2,1)} %collective-permute-done.7.refs_0_, bf16[528,768]{1,0:T(8,128)(2,1)} %collective-permute-done.8.refs_1_, bf16[528,768]{1,0:T(8,128)(2,1)} %collective-permute-done.16.refs_2_, bf16[528,768]{1,0:T(8,128)(2,1)} %collective-permute-done.1.refs_2_.refs_5_.refs_3_, ...), custom_call_target="tpu_custom_call" | custom-call | flops 4831838208 | bytes 8921088 | tf_op jit(solution)/shard_map/meet_12/pallas_call | solution.py:298
  81.2 17.8 %all_to_all.5.arrived_ref = f32[128,1,512]{2,1,0:T(1,128)} all-to-all(f32[128,1,512]{2,1,0:T(1,128)} %meet_12.3), channel_id=1, replica_groups=mesh['group'=8,'row'=16] {'group','row'}, dimensions={0} | all-to-all | bytes 524288 | tf_op jit(solution)/shard_map/all_to_all | solution.py:373
  99.0 1.9 %finish.1 = f32[1,512]{1,0:T(1,128)} custom-call(f32[128,1,512]{2,1,0:T(1,128)} %all_to_all.5.arrived_ref, s32[1,512]{1,0:T(1,128)} %get-tuple-element.32.target_ref), custom_call_target="tpu_custom_call" | custom-call | tf_op jit(solution)/shard_map/finish/pallas_call | solution.py:336
Async XLA Ops:
  2.8 13.8 %collective-permute-start = (bf16[528,768]{1,0:T(8,128)(2,1)}, bf16[528,768]{1,0:T(8,128)(2,1)}, u32[]{:S(2)}, u32[]{:S(2)}) collective-permute-start(bf16[528,768]{1,0:T(8,128)(2,1)} %get-tuple-element.19.refs_0_.refs_3_), channel_id=1, source_target_pairs={{0,4},{1,3},{2,6},{3,65},{4,8},{5,7},{6,10},{7,69},{8,12},{9,11},{... | collective-permute-start | bytes 2433032 | tf_op jit(solution)/shard_map/ppermute | solution.py:82
  5.0 14.0 %collective-permute-start.1 = (bf16[528,768]{1,0:T(8,128)(2,1)}, bf16[528,768]{1,0:T(8,128)(2,1)}, u32[]{:S(2)}, u32[]{:S(2)}) collective-permute-start(bf16[528,768]{1,0:T(8,128)(2,1)} %get-tuple-element.19.refs_0_.refs_3_), channel_id=1, source_target_pairs={{0,48},{1,17},{2,50},{3,19},{4,52},{5,21},{6,54},{7,23},{8,56},{9,... | collective-permute-start | bytes 2433032 | tf_op jit(solution)/shard_map/ppermute | solution.py:82
  6.2 17.0 %collective-permute-start.2 = (bf16[528,768]{1,0:T(8,128)(2,1)}, bf16[528,768]{1,0:T(8,128)(2,1)}, u32[]{:S(2)}, u32[]{:S(2)}) collective-permute-start(bf16[528,768]{1,0:T(8,128)(2,1)} %get-tuple-element.19.refs_0_.refs_3_), channel_id=1, source_target_pairs={{0,12},{1,67},{2,14},{3,1},{4,0},{5,71},{6,2},{7,5},{8,4},{9,75},{... | collective-permute-start | bytes 2433032 | tf_op jit(solution)/shard_map/ppermute | solution.py:82
  7.6 15.5 %collective-permute-start.3 = (bf16[528,768]{1,0:T(8,128)(2,1)}, bf16[528,768]{1,0:T(8,128)(2,1)}, u32[]{:S(2)}, u32[]{:S(2)}) collective-permute-start(bf16[528,768]{1,0:T(8,128)(2,1)} %get-tuple-element.19.refs_0_.refs_3_), channel_id=1, source_target_pairs={{0,1},{1,0},{2,3},{3,2},{4,5},{5,4},{6,7},{7,6},{8,9},{9,8},{10,11... | collective-permute-start | bytes 2433032 | tf_op jit(solution)/shard_map/ppermute | solution.py:86
  16.6 6.9 %collective-permute-start.4 = (bf16[528,768]{1,0:T(8,128)(2,1)}, bf16[528,768]{1,0:T(8,128)(2,1)}, u32[]{:S(2)}, u32[]{:S(2)}) collective-permute-start(bf16[528,768]{1,0:T(8,128)(2,1)} %collective-permute-done.refs_1_.refs_4_), channel_id=1, source_target_pairs={{0,1},{1,0},{2,3},{3,2},{4,5},{5,4},{6,7},{7,6},{8,9},{9,8},{10,11... | collective-permute-start | bytes 2433032 | tf_op jit(solution)/shard_map/ppermute | solution.py:86
  18.9 13.0 %collective-permute-start.5 = (bf16[528,768]{1,0:T(8,128)(2,1)}, bf16[528,768]{1,0:T(8,128)(2,1)}, u32[]{:S(2)}, u32[]{:S(2)}) collective-permute-start(bf16[528,768]{1,0:T(8,128)(2,1)} %collective-permute-done.1.refs_2_.refs_5_.refs_3_), channel_id=1, source_target_pairs={{0,66},{1,13},{2,0},{3,15},{4,70},{5,1},{6,4},{7,3},{8,74},{9,5},{... | collective-permute-start | bytes 2433032 | tf_op jit(solution)/shard_map/ppermute | solution.py:82
  21.6 11.7 %collective-permute-start.6 = (bf16[528,768]{1,0:T(8,128)(2,1)}, bf16[528,768]{1,0:T(8,128)(2,1)}, u32[]{:S(2)}, u32[]{:S(2)}) collective-permute-start(bf16[528,768]{1,0:T(8,128)(2,1)} %collective-permute-done.refs_1_.refs_4_), channel_id=1, source_target_pairs={{0,16},{1,49},{2,18},{3,51},{4,20},{5,53},{6,22},{7,55},{8,24},{9,... | collective-permute-start | bytes 2433032 | tf_op jit(solution)/shard_map/ppermute | solution.py:82
  23.1 12.9 %collective-permute-start.9 = (bf16[528,768]{1,0:T(8,128)(2,1)}, bf16[528,768]{1,0:T(8,128)(2,1)}, u32[]{:S(2)}, u32[]{:S(2)}) collective-permute-start(bf16[528,768]{1,0:T(8,128)(2,1)} %collective-permute-done.2.refs_3_.refs_6_), channel_id=1, source_target_pairs={{0,2},{1,5},{2,64},{3,7},{4,6},{5,9},{6,68},{7,11},{8,10},{9,13},{... | collective-permute-start | bytes 2433032 | tf_op jit(solution)/shard_map/ppermute | solution.py:82
  23.1 14.6 %collective-permute-start.10 = (bf16[528,768]{1,0:T(8,128)(2,1)}, bf16[528,768]{1,0:T(8,128)(2,1)}, u32[]{:S(2)}, u32[]{:S(2)}) collective-permute-start(bf16[528,768]{1,0:T(8,128)(2,1)} %collective-permute-done.1.refs_2_.refs_5_.refs_3_), channel_id=1, source_target_pairs={{0,1},{1,0},{2,3},{3,2},{4,5},{5,4},{6,7},{7,6},{8,9},{9,8},{10,11... | collective-permute-start | bytes 2433032 | tf_op jit(solution)/shard_map/ppermute | solution.py:86
  23.5 15.4 %collective-permute-start.11 = (bf16[528,768]{1,0:T(8,128)(2,1)}, bf16[528,768]{1,0:T(8,128)(2,1)}, u32[]{:S(2)}, u32[]{:S(2)}) collective-permute-start(bf16[528,768]{1,0:T(8,128)(2,1)} %collective-permute-done.2.refs_3_.refs_6_), channel_id=1, source_target_pairs={{0,1},{1,0},{2,3},{3,2},{4,5},{5,4},{6,7},{7,6},{8,9},{9,8},{10,11... | collective-permute-start | bytes 2433032 | tf_op jit(solution)/shard_map/ppermute | solution.py:86
  36.1 3.4 %collective-permute-start.14 = (bf16[528,768]{1,0:T(8,128)(2,1)}, bf16[528,768]{1,0:T(8,128)(2,1)}, u32[]{:S(2)}, u32[]{:S(2)}) collective-permute-start(bf16[528,768]{1,0:T(8,128)(2,1)} %collective-permute-done.9.refs_2_.refs_9_), channel_id=1, source_target_pairs={{0,1},{1,0},{2,3},{3,2},{4,5},{5,4},{6,7},{7,6},{8,9},{9,8},{10,11... | collective-permute-start | bytes 2433032 | tf_op jit(solution)/shard_map/ppermute | solution.py:86
  37.2 4.0 %collective-permute-start.13 = (bf16[528,768]{1,0:T(8,128)(2,1)}, bf16[528,768]{1,0:T(8,128)(2,1)}, u32[]{:S(2)}, u32[]{:S(2)}) collective-permute-start(bf16[528,768]{1,0:T(8,128)(2,1)} %collective-permute-done.6.refs_1_.refs_8_), channel_id=1, source_target_pairs={{0,1},{1,0},{2,3},{3,2},{4,5},{5,4},{6,7},{7,6},{8,9},{9,8},{10,11... | collective-permute-start | bytes 2433032 | tf_op jit(solution)/shard_map/ppermute | solution.py:86
  37.2 4.6 %collective-permute-start.12 = (bf16[528,768]{1,0:T(8,128)(2,1)}, bf16[528,768]{1,0:T(8,128)(2,1)}, u32[]{:S(2)}, u32[]{:S(2)}) collective-permute-start(bf16[528,768]{1,0:T(8,128)(2,1)} %collective-permute-done.5.refs_0_.refs_7_), channel_id=1, source_target_pairs={{0,1},{1,0},{2,3},{3,2},{4,5},{5,4},{6,7},{7,6},{8,9},{9,8},{10,11... | collective-permute-start | bytes 2433032 | tf_op jit(solution)/shard_map/ppermute | solution.py:86
  37.7 15.8 %collective-permute-start.15 = (bf16[528,768]{1,0:T(8,128)(2,1)}, bf16[528,768]{1,0:T(8,128)(2,1)}, u32[]{:S(2)}, u32[]{:S(2)}) collective-permute-start(bf16[528,768]{1,0:T(8,128)(2,1)} %collective-permute-done.9.refs_2_.refs_9_), channel_id=1, source_target_pairs={{0,48},{1,17},{2,50},{3,19},{4,52},{5,21},{6,54},{7,23},{8,56},{9,... | collective-permute-start | bytes 2433032 | tf_op jit(solution)/shard_map/ppermute | solution.py:82
  38.9 17.7 %collective-permute-start.17 = (bf16[528,768]{1,0:T(8,128)(2,1)}, bf16[528,768]{1,0:T(8,128)(2,1)}, u32[]{:S(2)}, u32[]{:S(2)}) collective-permute-start(bf16[528,768]{1,0:T(8,128)(2,1)} %collective-permute-done.5.refs_0_.refs_7_), channel_id=1, source_target_pairs={{0,4},{1,3},{2,6},{3,65},{4,8},{5,7},{6,10},{7,69},{8,12},{9,11},{... | collective-permute-start | bytes 2433032 | tf_op jit(solution)/shard_map/ppermute | solution.py:82
  39.5 18.4 %collective-permute-start.18 = (bf16[528,768]{1,0:T(8,128)(2,1)}, bf16[528,768]{1,0:T(8,128)(2,1)}, u32[]{:S(2)}, u32[]{:S(2)}) collective-permute-start(bf16[528,768]{1,0:T(8,128)(2,1)} %collective-permute-done.5.refs_0_.refs_7_), channel_id=1, source_target_pairs={{0,66},{1,13},{2,0},{3,15},{4,70},{5,1},{6,4},{7,3},{8,74},{9,5},{... | collective-permute-start | bytes 2433032 | tf_op jit(solution)/shard_map/ppermute | solution.py:82
  53.5 4.3 %collective-permute-start.19 = (bf16[528,768]{1,0:T(8,128)(2,1)}, bf16[528,768]{1,0:T(8,128)(2,1)}, u32[]{:S(2)}, u32[]{:S(2)}) collective-permute-start(bf16[528,768]{1,0:T(8,128)(2,1)} %collective-permute-done.15.refs_0_), channel_id=1, source_target_pairs={{0,1},{1,0},{2,3},{3,2},{4,5},{5,4},{6,7},{7,6},{8,9},{9,8},{10,11... | collective-permute-start | bytes 2433032 | tf_op jit(solution)/shard_map/ppermute | solution.py:86
  54.0 17.5 %collective-permute-start.7 = (bf16[528,768]{1,0:T(8,128)(2,1)}, bf16[528,768]{1,0:T(8,128)(2,1)}, u32[]{:S(2)}, u32[]{:S(2)}) collective-permute-start(bf16[528,768]{1,0:T(8,128)(2,1)} %collective-permute-done.6.refs_1_.refs_8_), channel_id=1, source_target_pairs={{0,4},{1,3},{2,6},{3,65},{4,8},{5,7},{6,10},{7,69},{8,12},{9,11},{... | collective-permute-start | bytes 2433032 | tf_op jit(solution)/shard_map/ppermute | solution.py:82
  55.6 15.9 %collective-permute-start.8 = (bf16[528,768]{1,0:T(8,128)(2,1)}, bf16[528,768]{1,0:T(8,128)(2,1)}, u32[]{:S(2)}, u32[]{:S(2)}) collective-permute-start(bf16[528,768]{1,0:T(8,128)(2,1)} %collective-permute-done.6.refs_1_.refs_8_), channel_id=1, source_target_pairs={{0,12},{1,67},{2,14},{3,1},{4,0},{5,71},{6,2},{7,5},{8,4},{9,75},{... | collective-permute-start | bytes 2433032 | tf_op jit(solution)/shard_map/ppermute | solution.py:82
  56.7 14.9 %collective-permute-start.16 = (bf16[528,768]{1,0:T(8,128)(2,1)}, bf16[528,768]{1,0:T(8,128)(2,1)}, u32[]{:S(2)}, u32[]{:S(2)}) collective-permute-start(bf16[528,768]{1,0:T(8,128)(2,1)} %collective-permute-done.15.refs_0_), channel_id=1, source_target_pairs={{0,48},{1,17},{2,50},{3,19},{4,52},{5,21},{6,54},{7,23},{8,56},{9,... | collective-permute-start | bytes 2433032 | tf_op jit(solution)/shard_map/ppermute | solution.py:82

commit v6 on v4

--- a/solution.py
+++ b/solution.py
@@ -13,7 +13,7 @@
 GROUPS = 8
 META = 16
 SENT = RB + META
-UNROLL = 4
+UNROLL = 7
 HALF = 256
 BAND = 384
 ABSENT = -4.0

time: 100 us -> 100 us (level)
  no operation moved by 1% of the time
where the time goes in v6:
time: 100 us
  Pallas kernels  46.8 us (47%)
  starting transfers between devices  24.3 us (24%)
  blocking collectives  17.8 us (18%)
  waiting for transfers between devices  11.1 us (11%)
    pallas_call x4, Pallas kernels, meet(): pl.pallas_call(functools.partial(meet_kernel, total, len(rows), pairs, it...  42.1 us
    all_to_all x1, blocking collectives, on_device(): lax.all_to_all(outgoing, AXES, split_axis=0, concat_axis=0, tiled=True)  17.8 us
    ppermute x12, starting transfers between devices, fetch(): return lax.ppermute(block, AXES, sorted(pairs))  15.8 us
    ppermute x12, waiting for transfers between devices, fetch(): return lax.ppermute(block, AXES, sorted(pairs))  9.93 us
    ppermute x8, starting transfers between devices, flip(): return lax.ppermute(block, AXES, [(i, i ^ 1) for i in range(128)])  8.51 us
    pallas_call x1, Pallas kernels, prepare(): pl.pallas_call(prepare_kernel, out_shape=(jax.ShapeDtypeStruct((SENT, D),...  2.84 us
  transfers between devices with their start and end apart: 20, of which 5 were waited for; matrix products, arithmetic and copies ran while one was open for 0% of the time, Pallas kernels for 33%

profile of v6, /device:TPU:1, one launch (start us, length us, event | category | flops | bytes accessed | tf_op | source)
XLA Modules:
  0.0 100.1 jit_solution(6942820547950635952)
XLA Ops:
  0.0 2.8 %prepare.1 = (bf16[528,768]{1,0:T(8,128)(2,1)}, s32[1,512]{1,0:T(1,128)}) custom-call(bf16[512,768]{1,0:T(8,128)(2,1)} %embeds_ref.1, s32[1,512]{1,0:T(1,128)} %bitcast.2), custom_call_target="tpu_custom_call" | custom-call | tf_op jit(solution)/shard_map/prepare/pallas_call | solution.py:135
  2.8 2.1 %collective-permute-start = (bf16[528,768]{1,0:T(8,128)(2,1)}, bf16[528,768]{1,0:T(8,128)(2,1)}, u32[]{:S(2)}, u32[]{:S(2)}) collective-permute-start(bf16[528,768]{1,0:T(8,128)(2,1)} %get-tuple-element.19.refs_0_.refs_3_), channel_id=1, source_target_pairs={{0,4},{1,3},{2,6},{3,65},{4,8},{5,7},{6,10},{7,69},{8,12},{9,11},{... | collective-permute-start | bytes 2433032 | tf_op jit(solution)/shard_map/ppermute | solution.py:82
  5.0 1.2 %collective-permute-start.1 = (bf16[528,768]{1,0:T(8,128)(2,1)}, bf16[528,768]{1,0:T(8,128)(2,1)}, u32[]{:S(2)}, u32[]{:S(2)}) collective-permute-start(bf16[528,768]{1,0:T(8,128)(2,1)} %get-tuple-element.19.refs_0_.refs_3_), channel_id=1, source_target_pairs={{0,48},{1,17},{2,50},{3,19},{4,52},{5,21},{6,54},{7,23},{8,56},{9,... | collective-permute-start | bytes 2433032 | tf_op jit(solution)/shard_map/ppermute | solution.py:82
  6.2 1.4 %collective-permute-start.2 = (bf16[528,768]{1,0:T(8,128)(2,1)}, bf16[528,768]{1,0:T(8,128)(2,1)}, u32[]{:S(2)}, u32[]{:S(2)}) collective-permute-start(bf16[528,768]{1,0:T(8,128)(2,1)} %get-tuple-element.19.refs_0_.refs_3_), channel_id=1, source_target_pairs={{0,12},{1,67},{2,14},{3,1},{4,0},{5,71},{6,2},{7,5},{8,4},{9,75},{... | collective-permute-start | bytes 2433032 | tf_op jit(solution)/shard_map/ppermute | solution.py:82
  7.6 3.5 %collective-permute-start.3 = (bf16[528,768]{1,0:T(8,128)(2,1)}, bf16[528,768]{1,0:T(8,128)(2,1)}, u32[]{:S(2)}, u32[]{:S(2)}) collective-permute-start(bf16[528,768]{1,0:T(8,128)(2,1)} %get-tuple-element.19.refs_0_.refs_3_), channel_id=1, source_target_pairs={{0,1},{1,0},{2,3},{3,2},{4,5},{5,4},{6,7},{7,6},{8,9},{9,8},{10,11... | collective-permute-start | bytes 2433032 | tf_op jit(solution)/shard_map/ppermute | solution.py:86
  11.1 5.5 %collective-permute-done.refs_1_.refs_4_ = bf16[528,768]{1,0:T(8,128)(2,1)} collective-permute-done((bf16[528,768]{1,0:T(8,128)(2,1)}, bf16[528,768]{1,0:T(8,128)(2,1)}, u32[]{:S(2)}, u32[]{:S(2)}) %collective-permute-start) | collective-permute-done | bytes 811040 | tf_op jit(solution)/shard_map/ppermute | solution.py:82
  16.6 2.3 %collective-permute-start.4 = (bf16[528,768]{1,0:T(8,128)(2,1)}, bf16[528,768]{1,0:T(8,128)(2,1)}, u32[]{:S(2)}, u32[]{:S(2)}) collective-permute-start(bf16[528,768]{1,0:T(8,128)(2,1)} %collective-permute-done.refs_1_.refs_4_), channel_id=1, source_target_pairs={{0,1},{1,0},{2,3},{3,2},{4,5},{5,4},{6,7},{7,6},{8,9},{9,8},{10,11... | collective-permute-start | bytes 2433032 | tf_op jit(solution)/shard_map/ppermute | solution.py:86
  18.9 0.0 collective-permute-done.1.refs_2_.refs_5_.refs_3_
  18.9 2.7 %collective-permute-start.5 = (bf16[528,768]{1,0:T(8,128)(2,1)}, bf16[528,768]{1,0:T(8,128)(2,1)}, u32[]{:S(2)}, u32[]{:S(2)}) collective-permute-start(bf16[528,768]{1,0:T(8,128)(2,1)} %collective-permute-done.1.refs_2_.refs_5_.refs_3_), channel_id=1, source_target_pairs={{0,66},{1,13},{2,0},{3,15},{4,70},{5,1},{6,4},{7,3},{8,74},{9,5},{... | collective-permute-start | bytes 2433032 | tf_op jit(solution)/shard_map/ppermute | solution.py:82
  21.6 1.5 %collective-permute-start.6 = (bf16[528,768]{1,0:T(8,128)(2,1)}, bf16[528,768]{1,0:T(8,128)(2,1)}, u32[]{:S(2)}, u32[]{:S(2)}) collective-permute-start(bf16[528,768]{1,0:T(8,128)(2,1)} %collective-permute-done.refs_1_.refs_4_), channel_id=1, source_target_pairs={{0,16},{1,49},{2,18},{3,51},{4,20},{5,53},{6,22},{7,55},{8,24},{9,... | collective-permute-start | bytes 2433032 | tf_op jit(solution)/shard_map/ppermute | solution.py:82
  23.1 0.0 collective-permute-done.2.refs_3_.refs_6_
  23.1 0.0 collective-permute-start.9
  23.1 0.0 collective-permute-done.3.refs_4_.refs_7_.refs_10_.refs_6_
  23.1 0.4 collective-permute-start.10
  23.5 0.0 collective-permute-done.4.refs_5_.refs_8_.refs_11_.refs_7_
  23.5 0.2 collective-permute-start.11
  23.7 7.9 %meet_12.2.refs_11_ = f32[6,512]{1,0:T(8,128)} custom-call(bf16[528,768]{1,0:T(8,128)(2,1)} %get-tuple-element.19.refs_0_.refs_3_, bf16[528,768]{1,0:T(8,128)(2,1)} %collective-permute-done.refs_1_.refs_4_, bf16[528,768]{1,0:T(8,128)(2,1)} %collective-permute-done.1.refs_2_.refs_5_.refs_3_, bf16[528,768]{1,0:T(8,128)(2,1)} %collective-permute-done.2.refs_3_.refs_6_, ...), custom_call_target="tpu_custom_call" | custom-call | flops 4831838208 | bytes 4866048 | tf_op jit(solution)/shard_map/meet_12/pallas_call | solution.py:289
  31.7 0.0 collective-permute-done.5.refs_0_.refs_7_
  31.7 1.7 %collective-permute-done.6.refs_1_.refs_8_ = bf16[528,768]{1,0:T(8,128)(2,1)} collective-permute-done((bf16[528,768]{1,0:T(8,128)(2,1)}, bf16[528,768]{1,0:T(8,128)(2,1)}, u32[]{:S(2)}, u32[]{:S(2)}) %collective-permute-start.6) | collective-permute-done | bytes 811040 | tf_op jit(solution)/shard_map/ppermute | solution.py:82
  33.3 2.7 %collective-permute-done.9.refs_2_.refs_9_ = bf16[528,768]{1,0:T(8,128)(2,1)} collective-permute-done((bf16[528,768]{1,0:T(8,128)(2,1)}, bf16[528,768]{1,0:T(8,128)(2,1)}, u32[]{:S(2)}, u32[]{:S(2)}) %collective-permute-start.9) | collective-permute-done | bytes 811040 | tf_op jit(solution)/shard_map/ppermute | solution.py:82
  36.1 1.2 %collective-permute-start.14 = (bf16[528,768]{1,0:T(8,128)(2,1)}, bf16[528,768]{1,0:T(8,128)(2,1)}, u32[]{:S(2)}, u32[]{:S(2)}) collective-permute-start(bf16[528,768]{1,0:T(8,128)(2,1)} %collective-permute-done.9.refs_2_.refs_9_), channel_id=1, source_target_pairs={{0,1},{1,0},{2,3},{3,2},{4,5},{5,4},{6,7},{7,6},{8,9},{9,8},{10,11... | collective-permute-start | bytes 2433032 | tf_op jit(solution)/shard_map/ppermute | solution.py:86
  37.2 0.0 collective-permute-start.13
  37.2 0.5 collective-permute-start.12
  37.7 0.0 collective-permute-done.10.refs_9_.refs_12_
  37.7 1.2 %collective-permute-start.15 = (bf16[528,768]{1,0:T(8,128)(2,1)}, bf16[528,768]{1,0:T(8,128)(2,1)}, u32[]{:S(2)}, u32[]{:S(2)}) collective-permute-start(bf16[528,768]{1,0:T(8,128)(2,1)} %collective-permute-done.9.refs_2_.refs_9_), channel_id=1, source_target_pairs={{0,48},{1,17},{2,50},{3,19},{4,52},{5,21},{6,54},{7,23},{8,56},{9,... | collective-permute-start | bytes 2433032 | tf_op jit(solution)/shard_map/ppermute | solution.py:82
  38.9 0.0 collective-permute-done.11.refs_10_.refs_13_.refs_8_
  38.9 0.0 collective-permute-start.17
  39.0 0.6 collective-permute-done.14.refs_13_.refs_16_.refs_9_
  39.5 1.7 %collective-permute-start.18 = (bf16[528,768]{1,0:T(8,128)(2,1)}, bf16[528,768]{1,0:T(8,128)(2,1)}, u32[]{:S(2)}, u32[]{:S(2)}) collective-permute-start(bf16[528,768]{1,0:T(8,128)(2,1)} %collective-permute-done.5.refs_0_.refs_7_), channel_id=1, source_target_pairs={{0,66},{1,13},{2,0},{3,15},{4,70},{5,1},{6,4},{7,3},{8,74},{9,5},{... | collective-permute-start | bytes 2433032 | tf_op jit(solution)/shard_map/ppermute | solution.py:82
  41.3 0.0 collective-permute-done.13.refs_12_.refs_15_
  41.3 0.6 collective-permute-done.12.refs_11_.refs_14_
  41.8 11.5 %meet_23.1.refs_12_ = f32[14,512]{1,0:T(8,128)} custom-call(bf16[528,768]{1,0:T(8,128)(2,1)} %collective-permute-done.5.refs_0_.refs_7_, bf16[528,768]{1,0:T(8,128)(2,1)} %collective-permute-done.6.refs_1_.refs_8_, bf16[528,768]{1,0:T(8,128)(2,1)} %collective-permute-done.9.refs_2_.refs_9_, bf16[528,768]{1,0:T(8,128)(2,1)} %get-tuple-element.19.refs_0_.refs_3_, ...), custom_call_target="tpu_custom_call" | custom-call | flops 9261023232 | bytes 11354112 | tf_op jit(solution)/shard_map/meet_23/pallas_call | solution.py:289
  53.3 0.0 collective-permute-done.15.refs_0_
  53.3 0.5 collective-permute-start.19
  53.8 1.6 %collective-permute-start.7 = (bf16[528,768]{1,0:T(8,128)(2,1)}, bf16[528,768]{1,0:T(8,128)(2,1)}, u32[]{:S(2)}, u32[]{:S(2)}) collective-permute-start(bf16[528,768]{1,0:T(8,128)(2,1)} %collective-permute-done.6.refs_1_.refs_8_), channel_id=1, source_target_pairs={{0,4},{1,3},{2,6},{3,65},{4,8},{5,7},{6,10},{7,69},{8,12},{9,11},{... | collective-permute-start | bytes 2433032 | tf_op jit(solution)/shard_map/ppermute | solution.py:82
  55.4 1.1 %collective-permute-start.8 = (bf16[528,768]{1,0:T(8,128)(2,1)}, bf16[528,768]{1,0:T(8,128)(2,1)}, u32[]{:S(2)}, u32[]{:S(2)}) collective-permute-start(bf16[528,768]{1,0:T(8,128)(2,1)} %collective-permute-done.6.refs_1_.refs_8_), channel_id=1, source_target_pairs={{0,12},{1,67},{2,14},{3,1},{4,0},{5,71},{6,2},{7,5},{8,4},{9,75},{... | collective-permute-start | bytes 2433032 | tf_op jit(solution)/shard_map/ppermute | solution.py:82
  56.5 0.0 collective-permute-done.17.refs_1_.refs_4_
  56.5 1.2 %collective-permute-start.16 = (bf16[528,768]{1,0:T(8,128)(2,1)}, bf16[528,768]{1,0:T(8,128)(2,1)}, u32[]{:S(2)}, u32[]{:S(2)}) collective-permute-start(bf16[528,768]{1,0:T(8,128)(2,1)} %collective-permute-done.15.refs_0_), channel_id=1, source_target_pairs={{0,48},{1,17},{2,50},{3,19},{4,52},{5,21},{6,54},{7,23},{8,56},{9,... | collective-permute-start | bytes 2433032 | tf_op jit(solution)/shard_map/ppermute | solution.py:82
  57.7 0.0 collective-permute-done.18.refs_2_.refs_5_
  57.7 0.0 collective-permute-done.19.refs_17_.refs_10_
  57.7 13.7 %meet_28.1.refs_13_ = f32[18,512]{1,0:T(8,128)} custom-call(bf16[528,768]{1,0:T(8,128)(2,1)} %collective-permute-done.15.refs_0_, bf16[528,768]{1,0:T(8,128)(2,1)} %collective-permute-done.17.refs_1_.refs_4_, bf16[528,768]{1,0:T(8,128)(2,1)} %collective-permute-done.18.refs_2_.refs_5_, bf16[528,768]{1,0:T(8,128)(2,1)} %get-tuple-element.19.refs_0_.refs_3_, ...), custom_call_target="tpu_custom_call" | custom-call | flops 11274289152 | bytes 14598144 | tf_op jit(solution)/shard_map/meet_28/pallas_call | solution.py:289
  71.4 0.0 collective-permute-done.7.refs_0_
  71.4 0.0 collective-permute-done.8.refs_1_
  71.4 0.0 collective-permute-done.16.refs_2_
  71.4 9.0 %meet_12.3 = f32[128,1,512]{2,1,0:T(1,128)} custom-call(bf16[528,768]{1,0:T(8,128)(2,1)} %collective-permute-done.7.refs_0_, bf16[528,768]{1,0:T(8,128)(2,1)} %collective-permute-done.8.refs_1_, bf16[528,768]{1,0:T(8,128)(2,1)} %collective-permute-done.16.refs_2_, bf16[528,768]{1,0:T(8,128)(2,1)} %collective-permute-done.1.refs_2_.refs_5_.refs_3_, ...), custom_call_target="tpu_custom_call" | custom-call | flops 4831838208 | bytes 8921088 | tf_op jit(solution)/shard_map/meet_12/pallas_call | solution.py:289
  80.4 17.8 %all_to_all.5.arrived_ref = f32[128,1,512]{2,1,0:T(1,128)} all-to-all(f32[128,1,512]{2,1,0:T(1,128)} %meet_12.3), channel_id=1, replica_groups=mesh['group'=8,'row'=16] {'group','row'}, dimensions={0} | all-to-all | bytes 524288 | tf_op jit(solution)/shard_map/all_to_all | solution.py:362
  98.2 1.9 %finish.1 = f32[1,512]{1,0:T(1,128)} custom-call(f32[128,1,512]{2,1,0:T(1,128)} %all_to_all.5.arrived_ref, s32[1,512]{1,0:T(1,128)} %get-tuple-element.32.target_ref), custom_call_target="tpu_custom_call" | custom-call | tf_op jit(solution)/shard_map/finish/pallas_call | solution.py:325
Async XLA Ops:
  2.8 13.8 %collective-permute-start = (bf16[528,768]{1,0:T(8,128)(2,1)}, bf16[528,768]{1,0:T(8,128)(2,1)}, u32[]{:S(2)}, u32[]{:S(2)}) collective-permute-start(bf16[528,768]{1,0:T(8,128)(2,1)} %get-tuple-element.19.refs_0_.refs_3_), channel_id=1, source_target_pairs={{0,4},{1,3},{2,6},{3,65},{4,8},{5,7},{6,10},{7,69},{8,12},{9,11},{... | collective-permute-start | bytes 2433032 | tf_op jit(solution)/shard_map/ppermute | solution.py:82
  5.0 14.0 %collective-permute-start.1 = (bf16[528,768]{1,0:T(8,128)(2,1)}, bf16[528,768]{1,0:T(8,128)(2,1)}, u32[]{:S(2)}, u32[]{:S(2)}) collective-permute-start(bf16[528,768]{1,0:T(8,128)(2,1)} %get-tuple-element.19.refs_0_.refs_3_), channel_id=1, source_target_pairs={{0,48},{1,17},{2,50},{3,19},{4,52},{5,21},{6,54},{7,23},{8,56},{9,... | collective-permute-start | bytes 2433032 | tf_op jit(solution)/shard_map/ppermute | solution.py:82
  6.2 17.0 %collective-permute-start.2 = (bf16[528,768]{1,0:T(8,128)(2,1)}, bf16[528,768]{1,0:T(8,128)(2,1)}, u32[]{:S(2)}, u32[]{:S(2)}) collective-permute-start(bf16[528,768]{1,0:T(8,128)(2,1)} %get-tuple-element.19.refs_0_.refs_3_), channel_id=1, source_target_pairs={{0,12},{1,67},{2,14},{3,1},{4,0},{5,71},{6,2},{7,5},{8,4},{9,75},{... | collective-permute-start | bytes 2433032 | tf_op jit(solution)/shard_map/ppermute | solution.py:82
  7.6 15.5 %collective-permute-start.3 = (bf16[528,768]{1,0:T(8,128)(2,1)}, bf16[528,768]{1,0:T(8,128)(2,1)}, u32[]{:S(2)}, u32[]{:S(2)}) collective-permute-start(bf16[528,768]{1,0:T(8,128)(2,1)} %get-tuple-element.19.refs_0_.refs_3_), channel_id=1, source_target_pairs={{0,1},{1,0},{2,3},{3,2},{4,5},{5,4},{6,7},{7,6},{8,9},{9,8},{10,11... | collective-permute-start | bytes 2433032 | tf_op jit(solution)/shard_map/ppermute | solution.py:86
  16.6 6.9 %collective-permute-start.4 = (bf16[528,768]{1,0:T(8,128)(2,1)}, bf16[528,768]{1,0:T(8,128)(2,1)}, u32[]{:S(2)}, u32[]{:S(2)}) collective-permute-start(bf16[528,768]{1,0:T(8,128)(2,1)} %collective-permute-done.refs_1_.refs_4_), channel_id=1, source_target_pairs={{0,1},{1,0},{2,3},{3,2},{4,5},{5,4},{6,7},{7,6},{8,9},{9,8},{10,11... | collective-permute-start | bytes 2433032 | tf_op jit(solution)/shard_map/ppermute | solution.py:86
  18.9 12.7 %collective-permute-start.5 = (bf16[528,768]{1,0:T(8,128)(2,1)}, bf16[528,768]{1,0:T(8,128)(2,1)}, u32[]{:S(2)}, u32[]{:S(2)}) collective-permute-start(bf16[528,768]{1,0:T(8,128)(2,1)} %collective-permute-done.1.refs_2_.refs_5_.refs_3_), channel_id=1, source_target_pairs={{0,66},{1,13},{2,0},{3,15},{4,70},{5,1},{6,4},{7,3},{8,74},{9,5},{... | collective-permute-start | bytes 2433032 | tf_op jit(solution)/shard_map/ppermute | solution.py:82
  21.6 11.7 %collective-permute-start.6 = (bf16[528,768]{1,0:T(8,128)(2,1)}, bf16[528,768]{1,0:T(8,128)(2,1)}, u32[]{:S(2)}, u32[]{:S(2)}) collective-permute-start(bf16[528,768]{1,0:T(8,128)(2,1)} %collective-permute-done.refs_1_.refs_4_), channel_id=1, source_target_pairs={{0,16},{1,49},{2,18},{3,51},{4,20},{5,53},{6,22},{7,55},{8,24},{9,... | collective-permute-start | bytes 2433032 | tf_op jit(solution)/shard_map/ppermute | solution.py:82
  23.1 12.9 %collective-permute-start.9 = (bf16[528,768]{1,0:T(8,128)(2,1)}, bf16[528,768]{1,0:T(8,128)(2,1)}, u32[]{:S(2)}, u32[]{:S(2)}) collective-permute-start(bf16[528,768]{1,0:T(8,128)(2,1)} %collective-permute-done.2.refs_3_.refs_6_), channel_id=1, source_target_pairs={{0,2},{1,5},{2,64},{3,7},{4,6},{5,9},{6,68},{7,11},{8,10},{9,13},{... | collective-permute-start | bytes 2433032 | tf_op jit(solution)/shard_map/ppermute | solution.py:82
  23.1 14.6 %collective-permute-start.10 = (bf16[528,768]{1,0:T(8,128)(2,1)}, bf16[528,768]{1,0:T(8,128)(2,1)}, u32[]{:S(2)}, u32[]{:S(2)}) collective-permute-start(bf16[528,768]{1,0:T(8,128)(2,1)} %collective-permute-done.1.refs_2_.refs_5_.refs_3_), channel_id=1, source_target_pairs={{0,1},{1,0},{2,3},{3,2},{4,5},{5,4},{6,7},{7,6},{8,9},{9,8},{10,11... | collective-permute-start | bytes 2433032 | tf_op jit(solution)/shard_map/ppermute | solution.py:86
  23.5 15.4 %collective-permute-start.11 = (bf16[528,768]{1,0:T(8,128)(2,1)}, bf16[528,768]{1,0:T(8,128)(2,1)}, u32[]{:S(2)}, u32[]{:S(2)}) collective-permute-start(bf16[528,768]{1,0:T(8,128)(2,1)} %collective-permute-done.2.refs_3_.refs_6_), channel_id=1, source_target_pairs={{0,1},{1,0},{2,3},{3,2},{4,5},{5,4},{6,7},{7,6},{8,9},{9,8},{10,11... | collective-permute-start | bytes 2433032 | tf_op jit(solution)/shard_map/ppermute | solution.py:86
  36.1 3.4 %collective-permute-start.14 = (bf16[528,768]{1,0:T(8,128)(2,1)}, bf16[528,768]{1,0:T(8,128)(2,1)}, u32[]{:S(2)}, u32[]{:S(2)}) collective-permute-start(bf16[528,768]{1,0:T(8,128)(2,1)} %collective-permute-done.9.refs_2_.refs_9_), channel_id=1, source_target_pairs={{0,1},{1,0},{2,3},{3,2},{4,5},{5,4},{6,7},{7,6},{8,9},{9,8},{10,11... | collective-permute-start | bytes 2433032 | tf_op jit(solution)/shard_map/ppermute | solution.py:86
  37.2 4.0 %collective-permute-start.13 = (bf16[528,768]{1,0:T(8,128)(2,1)}, bf16[528,768]{1,0:T(8,128)(2,1)}, u32[]{:S(2)}, u32[]{:S(2)}) collective-permute-start(bf16[528,768]{1,0:T(8,128)(2,1)} %collective-permute-done.6.refs_1_.refs_8_), channel_id=1, source_target_pairs={{0,1},{1,0},{2,3},{3,2},{4,5},{5,4},{6,7},{7,6},{8,9},{9,8},{10,11... | collective-permute-start | bytes 2433032 | tf_op jit(solution)/shard_map/ppermute | solution.py:86
  37.2 4.6 %collective-permute-start.12 = (bf16[528,768]{1,0:T(8,128)(2,1)}, bf16[528,768]{1,0:T(8,128)(2,1)}, u32[]{:S(2)}, u32[]{:S(2)}) collective-permute-start(bf16[528,768]{1,0:T(8,128)(2,1)} %collective-permute-done.5.refs_0_.refs_7_), channel_id=1, source_target_pairs={{0,1},{1,0},{2,3},{3,2},{4,5},{5,4},{6,7},{7,6},{8,9},{9,8},{10,11... | collective-permute-start | bytes 2433032 | tf_op jit(solution)/shard_map/ppermute | solution.py:86
  37.7 15.6 %collective-permute-start.15 = (bf16[528,768]{1,0:T(8,128)(2,1)}, bf16[528,768]{1,0:T(8,128)(2,1)}, u32[]{:S(2)}, u32[]{:S(2)}) collective-permute-start(bf16[528,768]{1,0:T(8,128)(2,1)} %collective-permute-done.9.refs_2_.refs_9_), channel_id=1, source_target_pairs={{0,48},{1,17},{2,50},{3,19},{4,52},{5,21},{6,54},{7,23},{8,56},{9,... | collective-permute-start | bytes 2433032 | tf_op jit(solution)/shard_map/ppermute | solution.py:82
  38.9 17.5 %collective-permute-start.17 = (bf16[528,768]{1,0:T(8,128)(2,1)}, bf16[528,768]{1,0:T(8,128)(2,1)}, u32[]{:S(2)}, u32[]{:S(2)}) collective-permute-start(bf16[528,768]{1,0:T(8,128)(2,1)} %collective-permute-done.5.refs_0_.refs_7_), channel_id=1, source_target_pairs={{0,4},{1,3},{2,6},{3,65},{4,8},{5,7},{6,10},{7,69},{8,12},{9,11},{... | collective-permute-start | bytes 2433032 | tf_op jit(solution)/shard_map/ppermute | solution.py:82
  39.5 18.2 %collective-permute-start.18 = (bf16[528,768]{1,0:T(8,128)(2,1)}, bf16[528,768]{1,0:T(8,128)(2,1)}, u32[]{:S(2)}, u32[]{:S(2)}) collective-permute-start(bf16[528,768]{1,0:T(8,128)(2,1)} %collective-permute-done.5.refs_0_.refs_7_), channel_id=1, source_target_pairs={{0,66},{1,13},{2,0},{3,15},{4,70},{5,1},{6,4},{7,3},{8,74},{9,5},{... | collective-permute-start | bytes 2433032 | tf_op jit(solution)/shard_map/ppermute | solution.py:82
  53.3 4.3 %collective-permute-start.19 = (bf16[528,768]{1,0:T(8,128)(2,1)}, bf16[528,768]{1,0:T(8,128)(2,1)}, u32[]{:S(2)}, u32[]{:S(2)}) collective-permute-start(bf16[528,768]{1,0:T(8,128)(2,1)} %collective-permute-done.15.refs_0_), channel_id=1, source_target_pairs={{0,1},{1,0},{2,3},{3,2},{4,5},{5,4},{6,7},{7,6},{8,9},{9,8},{10,11... | collective-permute-start | bytes 2433032 | tf_op jit(solution)/shard_map/ppermute | solution.py:86
  53.8 17.6 %collective-permute-start.7 = (bf16[528,768]{1,0:T(8,128)(2,1)}, bf16[528,768]{1,0:T(8,128)(2,1)}, u32[]{:S(2)}, u32[]{:S(2)}) collective-permute-start(bf16[528,768]{1,0:T(8,128)(2,1)} %collective-permute-done.6.refs_1_.refs_8_), channel_id=1, source_target_pairs={{0,4},{1,3},{2,6},{3,65},{4,8},{5,7},{6,10},{7,69},{8,12},{9,11},{... | collective-permute-start | bytes 2433032 | tf_op jit(solution)/shard_map/ppermute | solution.py:82
  55.4 16.0 %collective-permute-start.8 = (bf16[528,768]{1,0:T(8,128)(2,1)}, bf16[528,768]{1,0:T(8,128)(2,1)}, u32[]{:S(2)}, u32[]{:S(2)}) collective-permute-start(bf16[528,768]{1,0:T(8,128)(2,1)} %collective-permute-done.6.refs_1_.refs_8_), channel_id=1, source_target_pairs={{0,12},{1,67},{2,14},{3,1},{4,0},{5,71},{6,2},{7,5},{8,4},{9,75},{... | collective-permute-start | bytes 2433032 | tf_op jit(solution)/shard_map/ppermute | solution.py:82
  56.5 14.9 %collective-permute-start.16 = (bf16[528,768]{1,0:T(8,128)(2,1)}, bf16[528,768]{1,0:T(8,128)(2,1)}, u32[]{:S(2)}, u32[]{:S(2)}) collective-permute-start(bf16[528,768]{1,0:T(8,128)(2,1)} %collective-permute-done.15.refs_0_), channel_id=1, source_target_pairs={{0,48},{1,17},{2,50},{3,19},{4,52},{5,21},{6,54},{7,23},{8,56},{9,... | collective-permute-start | bytes 2433032 | tf_op jit(solution)/shard_map/ppermute | solution.py:82
